TPU v7x, 32 devices: a whole 2x2x4 slice. The times are simulated.
32 devices in a mesh: row: 8 (over z, x), col: 4 (over y, core).
Axes of the slice: x: 2, y: 2, z: 4, core: 2. Of those that a mesh axis runs over, the one named last changes fastest.
Arguments:
- a_blocks: float32 [1024, 6, 4096], P(('row', 'col')), as said below
- columns: int32 [1024, 6], P(('row', 'col')), may hold values from 0 to 1023, as said below
- tentative: float32 [1024, 4096], P(('row', 'col')), may hold values from -0.75 to 0.75
- aggregate: int32 [1024], P(('row', 'col')), may hold values from 0 to 3, as said below
- owner: int32 [128], P(('row', 'col')), may hold values from 0 to 127, as said below
Outputs:
- coarse_op: float32 [128, 20, 4096], P(('row', 'col'))
Inputs may be any that keep to these rules, and one draw needn't show every extreme that they name: Column 0 of block row n is n. Other columns of block row n lie among the block rows of n's device (32 a device, devices in the order of row+col); for the first 8 rows of a device they may also lie among the last 8 rows of the device before it, and for the last 8 rows among the first 8 rows of the device after it, and each such rim row of a device with that neighbour has one. Columns may repeat; repeated blocks add. `aggregate`: every device uses every number from 0 to 3. `owner`: A permutation of the coarse rows. The coarse rows of a device (a // 4) go to positions owned (position // 4) by devices of the same index along row, at most one to each device, so each device owns 4. The diagonal entries of the blocks a_blocks[n, 0] lie between 1.5 and 8.5.
All inputs are finite; a program needn't handle non-finite values.
Results may differ from a plain program's by a relative error of at most 0.0003.
Values sent between devices are 32-bit elements; how exact they have to be, the bound alone decides.
No kernel may reach another device: no remote copies, remote signals or barrier semaphores. Data moves between devices by JAX's collectives and lax.ppermute only.
A program may use at most 256 MiB of HBM per device.

v0:
```python
import jax
import jax.numpy as jnp
from jax import lax
from jax.sharding import PartitionSpec as P

B = 64
BC = 64
K = 6
G = 4
R = 32
H = 8


highest = lax.Precision.HIGHEST
relaxation = 2.0 / 3.0


def padded(block, sides, width):
    for axis, dim in sides:
        count = lax.axis_size(axis)
        forward = [(i, i + 1) for i in range(count - 1)]
        backward = [(target, source) for source, target in forward]
        low = lax.ppermute(
            lax.slice_in_dim(block, block.shape[dim] - width, None, axis=dim), axis, forward
        )
        high = lax.ppermute(lax.slice_in_dim(block, 0, width, axis=dim), axis, backward)
        block = jnp.concatenate([low, block, high], axis=dim)
    return block


def from_behind(block, axis, distance):
    devices = range(lax.axis_size(axis))
    route = [(i - distance, i) for i in devices if i - distance in devices]
    return lax.ppermute(block, axis, route)


def prolong_rows(a_rows, col_rows, own_basis, ext_basis, ext_agg, device):
    row_count = col_rows.shape[0]
    local_index = col_rows - device * R + H
    dev_offset = (local_index >= H).astype(jnp.int32) + (local_index >= R + H).astype(jnp.int32)
    labels = (dev_offset * G + jnp.take(ext_agg, local_index)).astype(jnp.int32)
    a_mats = a_rows.reshape(row_count, K, B, B)
    basis_rows = jnp.take(ext_basis, local_index, axis=0).reshape(row_count, K, B, BC)
    applied = jnp.einsum("ikqp,ikpv->ikqv", a_mats, basis_rows, precision=highest)
    diagonal = jnp.diagonal(a_mats[:, 0], axis1=1, axis2=2)
    first_column = (jnp.arange(K) == 0).astype(applied.dtype)
    smooth = (
        first_column[None, :, None, None] * own_basis.reshape(row_count, 1, B, BC)
        - relaxation * applied / diagonal[:, None, :, None]
    )
    return (smooth.reshape(row_count, K, B * BC), labels)


def dense_rows(ext_smooth, ext_labels):
    onehot = (ext_labels[..., None] == jnp.arange(3 * G, dtype=jnp.int32)).astype(ext_smooth.dtype)
    return jnp.einsum("rmc,rmx->rcx", onehot, ext_smooth, precision=highest)


def apply_rows(a_group, index_group, ext_dense):
    count = index_group.shape[0]
    gathered = jnp.take(ext_dense, index_group, axis=0).reshape(count, K, 3 * G, B, BC)
    a_mats = a_group.reshape(count, K, B, B)
    total = jnp.einsum("sqp,scpw->scqw", a_mats[:, 0], gathered[:, 0], precision=highest)
    for stored in range(1, K):
        total = total + jnp.einsum(
            "sqp,scpw->scqw", a_mats[:, stored], gathered[:, stored], precision=highest
        )
    return total


def coarse_part(smooth, labels, applied_rows):
    count = labels.shape[0]
    onehot = (labels[..., None] == jnp.arange(3 * G, dtype=jnp.int32)).astype(smooth.dtype)
    dense = jnp.einsum("ikl,ikqv->ilqv", onehot, smooth.reshape(count, K, B, BC), precision=highest)
    return jnp.einsum("ilqv,icqw->lcvw", dense, applied_rows, precision=highest)


def local(a_blocks, columns, tentative, aggregate, owner):
    device = lax.axis_index(("row", "col"))
    ext_basis, ext_agg = (
        padded(tentative, ((("row", "col"), 0),), H),
        padded(aggregate, ((("row", "col"), 0),), H),
    )
    smooth, labels = prolong_rows(a_blocks, columns, tentative, ext_basis, ext_agg, device)
    ext_smooth, ext_labels = (
        padded(smooth, ((("row", "col"), 0),), H),
        padded(labels, ((("row", "col"), 0),), H),
    )
    position = jnp.arange(R + 2 * H, dtype=jnp.int32)
    label_shift = jnp.where(position < H, -G, jnp.where(position >= R + H, G, 0)).astype(jnp.int32)
    ext_labels = (ext_labels + label_shift[:, None]).astype(jnp.int32)
    ext_dense = dense_rows(ext_smooth, ext_labels)
    local_index = columns - device * R + H
    group_count = R // 8

    def apply_group(pieces):
        return apply_rows(pieces[0], pieces[1], ext_dense)

    applied_rows = lax.map(
        apply_group,
        (a_blocks.reshape(group_count, 8, K, B * B), local_index.reshape(group_count, 8, K)),
    )
    applied_rows = applied_rows.reshape(R, 3 * G, B, BC)
    partial_value = coarse_part(smooth, labels, applied_rows)
    from_lower = from_behind(partial_value[2 * G :], ("row", "col"), 1)
    from_upper = from_behind(partial_value[:G], ("row", "col"), -1)
    rows_full = jnp.pad(partial_value[G : 2 * G], ((0, 0), (G, G), (0, 0), (0, 0)))
    rows_full = rows_full + jnp.pad(from_lower, ((0, 0), (0, 2 * G), (0, 0), (0, 0)))
    rows_full = rows_full + jnp.pad(from_upper, ((0, 0), (2 * G, 0), (0, 0), (0, 0)))
    coarse_rows = rows_full.reshape(G, 5 * G, BC * BC)
    all_rows, all_owners = (
        lax.all_gather(coarse_rows, "col", axis=0, tiled=True),
        lax.all_gather(owner, "col", axis=0, tiled=True),
    )
    wanted = (all_owners[None, :] == device * G + jnp.arange(G, dtype=jnp.int32)[:, None]).astype(
        jnp.float32
    )
    result = jnp.einsum("ga,acx->gcx", wanted, all_rows, precision=highest)
    return result


def solution(mesh):
    placed = (
        P(("row", "col"), None, None),
        P(("row", "col"), None),
        P(("row", "col"), None),
        P(("row", "col")),
        P(("row", "col")),
    )
    return jax.shard_map(
        local, mesh=mesh, in_specs=placed, out_specs=P(("row", "col"), None, None), check_vma=False
    )
```

profile of v0, /device:TPU:0, one launch (start us, length us, event | category | flops | bytes accessed | tf_op | source)
XLA Modules:
  0.0 710.5 jit_solution(15369154962517906465)
XLA Ops:
  26.9 10.5 %copy.52 = f32[32,6,64,64]{3,2,1,0:T(8,128)} copy(f32[32,6,64,64]{0,3,2,1:T(8,128)} %bitcast.153) | data formatting | bytes 6291456 | tf_op jit(solution)/shard_map/reshape | solution.py:42
  69.8 13.5 %bitcast_subtract_fusion = f32[32,6,64,64]{2,3,1,0:T(8,128)S(1)} fusion(f32[32,64]{1,0:T(8,128)S(1)} %copy.53, f32[32,64,64]{1,2,0:T(8,128)S(1)} %copy.49, f32[6]{0:T(128)S(1)} %compare_convert_fusion, f32[32,6,64,64]{3,2,1,0:T(8,128)} %copy.52, f32[32,6,64,64]{2,3,1,0:T(8,128)} %copy.50, pred[32,6]{1,0:T(8,128)(4,1)S(1)} %get-tuple-element.56), kind=kOutput, calls=%fused_computation.40 | convolution fusion | flops 607911936 | bytes 9969880 | tf_op jit(solution)/shard_map/ikqp,ikpv->ikqv/dot_general | solution.py:44
  120.4 14.8 %fusion.30 = f32[32,12,64,64]{3,1,2,0:T(8,128)} fusion(f32[32,6,64,64]{3,1,2,0:T(8,128)} %copy.61, s32[32,6]{1,0:T(8,128)S(1)} %get-tuple-element.55), kind=kOutput, calls=%fused_computation.54 | convolution fusion | flops 113248512 | bytes 9437952 | tf_op jit(solution)/shard_map/ikl,ikqv->ilqv/dot_general | solution.py:74
  137.3 9.8 %fusion.10 = f32[48,12,4096]{2,1,0:T(8,128)} fusion(f32[8,6,4096]{2,1,0:T(8,128)S(1)} %copy.59, f32[32,6,4096]{2,1,0:T(8,128)S(1)} %copy-done.3, f32[8,6,4096]{2,1,0:T(8,128)S(1)} %copy.57, s32[48,6]{1,0:T(8,128)S(1)} %copy.48), kind=kOutput, calls=%fused_computation.34 | convolution fusion | flops 172232064 | bytes 14156928 | tf_op jit(solution)/shard_map/rmc,rmx->rcx/dot_general | solution.py:56
  147.1 400.3 %while.10 = (s32[]{:T(128)}, f32[4,8,12,64,64]{3,4,2,1,0:T(8,128)}, s32[4,8,6]{2,1,0:T(8,128)S(1)}, f32[48,12,4096]{2,1,0:T(8,128)}, f32[4,8,6,4096]{3,1,0,2:T(8,128)}, /*index=5*/s32[]{:T(128)}) while((s32[]{:T(128)}, f32[4,8,12,64,64]{3,4,2,1,0:T(8,128)}, s32[4,8,6]{2,1,0:T(8,128)S(1)}, f32[48,12,4096]{2,1,0:T(8,128)}, ...), condition=%wide.region_1.2_spmd, body=%wide.region_0.1_spmd.sunk | while | flops 1816266240 | bytes 166730816 | solution.py:99
  161.4 12.3 %gather_fusion = f32[48,12,4096]{2,1,0:T(8,128)} fusion(f32[48,12,4096]{2,1,0:T(8,128)} %get-tuple-element.120, s32[1024]{0:T(1024)S(1)} %pad_clamp_fusion.3), kind=kCustom, calls=%fused_computation.clone.1 | custom fusion | bytes 18874560 | tf_op jit(solution)/shard_map/while/body/eval_jaxpr/jit(_take)/gather | solution.py:61
  173.6 16.9 %reshape.196 = f32[8,6,12,64,64]{4,3,2,1,0:T(8,128)} reshape(f32[48,12,4096]{2,1,0:T(8,128)} %gather_fusion) | data formatting | bytes 18874368 | tf_op jit(solution)/shard_map/while/body/eval_jaxpr/jit(_take)/gather | solution.py:61
  190.5 18.7 %copy.103 = f32[8,6,12,64,64]{3,4,2,0,1:T(8,128)} copy(f32[8,6,12,64,64]{4,3,2,1,0:T(8,128)} %reshape.196) | data formatting | bytes 18874368 | tf_op jit(solution)/shard_map/while/body/eval_jaxpr/jit(_take)/gather | solution.py:61
  209.3 13.8 %broadcast_select_fusion.2 = f32[8,6,12,64,64]{3,4,2,0,1:T(8,128)} fusion(f32[8,6,12,64,64]{3,4,2,0,1:T(8,128)} %copy.103, pred[8,6]{0,1:T(8,128)(4,1)S(1)} %copy.104), kind=kLoop, calls=%fused_computation.4.clone.1 | loop fusion | flops 2359296 | bytes 18874416 | tf_op jit(solution)/shard_map/while/body/eval_jaxpr/jit(_take)/select_n | solution.py:61
  257.9 12.3 %gather_fusion = f32[48,12,4096]{2,1,0:T(8,128)} fusion(f32[48,12,4096]{2,1,0:T(8,128)} %get-tuple-element.120, s32[1024]{0:T(1024)S(1)} %pad_clamp_fusion.3), kind=kCustom, calls=%fused_computation.clone.1 | custom fusion | bytes 18874560 | tf_op jit(solution)/shard_map/while/body/eval_jaxpr/jit(_take)/gather | solution.py:61
  270.1 16.9 %reshape.196 = f32[8,6,12,64,64]{4,3,2,1,0:T(8,128)} reshape(f32[48,12,4096]{2,1,0:T(8,128)} %gather_fusion) | data formatting | bytes 18874368 | tf_op jit(solution)/shard_map/while/body/eval_jaxpr/jit(_take)/gather | solution.py:61
  287.0 18.7 %copy.103 = f32[8,6,12,64,64]{3,4,2,0,1:T(8,128)} copy(f32[8,6,12,64,64]{4,3,2,1,0:T(8,128)} %reshape.196) | data formatting | bytes 18874368 | tf_op jit(solution)/shard_map/while/body/eval_jaxpr/jit(_take)/gather | solution.py:61
  305.8 13.8 %broadcast_select_fusion.2 = f32[8,6,12,64,64]{3,4,2,0,1:T(8,128)} fusion(f32[8,6,12,64,64]{3,4,2,0,1:T(8,128)} %copy.103, pred[8,6]{0,1:T(8,128)(4,1)S(1)} %copy.104), kind=kLoop, calls=%fused_computation.4.clone.1 | loop fusion | flops 2359296 | bytes 18874416 | tf_op jit(solution)/shard_map/while/body/eval_jaxpr/jit(_take)/select_n | solution.py:61
  354.4 12.3 %gather_fusion = f32[48,12,4096]{2,1,0:T(8,128)} fusion(f32[48,12,4096]{2,1,0:T(8,128)} %get-tuple-element.120, s32[1024]{0:T(1024)S(1)} %pad_clamp_fusion.3), kind=kCustom, calls=%fused_computation.clone.1 | custom fusion | bytes 18874560 | tf_op jit(solution)/shard_map/while/body/eval_jaxpr/jit(_take)/gather | solution.py:61
  366.7 16.9 %reshape.196 = f32[8,6,12,64,64]{4,3,2,1,0:T(8,128)} reshape(f32[48,12,4096]{2,1,0:T(8,128)} %gather_fusion) | data formatting | bytes 18874368 | tf_op jit(solution)/shard_map/while/body/eval_jaxpr/jit(_take)/gather | solution.py:61
  383.6 18.7 %copy.103 = f32[8,6,12,64,64]{3,4,2,0,1:T(8,128)} copy(f32[8,6,12,64,64]{4,3,2,1,0:T(8,128)} %reshape.196) | data formatting | bytes 18874368 | tf_op jit(solution)/shard_map/while/body/eval_jaxpr/jit(_take)/gather | solution.py:61
  402.4 13.8 %broadcast_select_fusion.2 = f32[8,6,12,64,64]{3,4,2,0,1:T(8,128)} fusion(f32[8,6,12,64,64]{3,4,2,0,1:T(8,128)} %copy.103, pred[8,6]{0,1:T(8,128)(4,1)S(1)} %copy.104), kind=kLoop, calls=%fused_computation.4.clone.1 | loop fusion | flops 2359296 | bytes 18874416 | tf_op jit(solution)/shard_map/while/body/eval_jaxpr/jit(_take)/select_n | solution.py:61
  451.0 12.2 %gather_fusion = f32[48,12,4096]{2,1,0:T(8,128)} fusion(f32[48,12,4096]{2,1,0:T(8,128)} %get-tuple-element.120, s32[1024]{0:T(1024)S(1)} %pad_clamp_fusion.3), kind=kCustom, calls=%fused_computation.clone.1 | custom fusion | bytes 18874560 | tf_op jit(solution)/shard_map/while/body/eval_jaxpr/jit(_take)/gather | solution.py:61
  463.2 16.9 %reshape.196 = f32[8,6,12,64,64]{4,3,2,1,0:T(8,128)} reshape(f32[48,12,4096]{2,1,0:T(8,128)} %gather_fusion) | data formatting | bytes 18874368 | tf_op jit(solution)/shard_map/while/body/eval_jaxpr/jit(_take)/gather | solution.py:61
  480.1 18.7 %copy.103 = f32[8,6,12,64,64]{3,4,2,0,1:T(8,128)} copy(f32[8,6,12,64,64]{4,3,2,1,0:T(8,128)} %reshape.196) | data formatting | bytes 18874368 | tf_op jit(solution)/shard_map/while/body/eval_jaxpr/jit(_take)/gather | solution.py:61
  498.9 13.8 %broadcast_select_fusion.2 = f32[8,6,12,64,64]{3,4,2,0,1:T(8,128)} fusion(f32[8,6,12,64,64]{3,4,2,0,1:T(8,128)} %copy.103, pred[8,6]{0,1:T(8,128)(4,1)S(1)} %copy.104), kind=kLoop, calls=%fused_computation.4.clone.1 | loop fusion | flops 2359296 | bytes 18874416 | tf_op jit(solution)/shard_map/while/body/eval_jaxpr/jit(_take)/select_n | solution.py:61
  547.4 50.4 %fusion.22 = f32[12,12,64,64]{2,3,0,1:T(8,128)S(1)} fusion(f32[32,12,64,64]{3,1,2,0:T(8,128)} %fusion.30, f32[32,12,64,64,1]{2,3,1,0,4:T(8,128)} %bitcast.157), kind=kOutput, calls=%fused_computation.48 | convolution fusion | flops 14495514624 | bytes 14942208 | tf_op jit(solution)/shard_map/ilqv,icqw->lcvw/dot_general | solution.py:75
  616.6 35.2 %all-reduce.3 = s32[16]{0:T(128)S(1)} all-reduce(s32[16]{0:T(128)S(1)} %dynamic-update-slice), channel_id=1, replica_groups=mesh['row'=8,'col'=4] {'col'}, use_global_device_ids=true, to_apply=%add.3 | all-reduce | flops 16 | bytes 128
  651.8 43.1 %all-gather.2.cloned.1.call-done = f32[16,20,4096]{2,1,0:T(8,128)} async-done(((f32[4,20,4096]{2,1,0:T(8,128)}), f32[16,20,4096]{2,1,0:T(8,128)}) %all-gather.2.cloned.1.call-update) | async-done | bytes 5242896 | tf_op jit(solution)/shard_map/all_gather | solution.py:112
  (161 shorter events, 257.3 us)
Async XLA Ops:
  6.5 688.3 %all-gather.2.cloned.1.call-start = ((), (), s32[]{:S(2)}) async-start(), calls=%async_computation | async-start | bytes 7864320 | tf_op jit(solution)/shard_map/all_gather | solution.py:112
  7.3 35.8 %collective-permute-start = (s32[8]{0:T(128)S(1)}, s32[8]{0:T(128)S(1)}, u32[]{:S(2)}, u32[]{:S(2)}) collective-permute-start(s32[8]{0:T(128)S(1)} %get-tuple-element.68), channel_id=1, source_target_pairs={{0,1},{1,2},{2,3},{3,4},{4,5},{5,6},{6,7},{7,8},{8,9},{9,10},{10,1... | collective-permute-start | bytes 104 | tf_op jit(solution)/shard_map/ppermute | solution.py:23
  9.7 33.5 %collective-permute-start.1 = (s32[8]{0:T(128)S(1)}, s32[8]{0:T(128)S(1)}, u32[]{:S(2)}, u32[]{:S(2)}) collective-permute-start(s32[8]{0:T(128)S(1)} %get-tuple-element.69), channel_id=1, source_target_pairs={{1,0},{2,1},{3,2},{4,3},{5,4},{6,5},{7,6},{8,7},{9,8},{10,9},{11,1... | collective-permute-start | bytes 104 | tf_op jit(solution)/shard_map/ppermute | solution.py:26
  12.0 41.8 %collective-permute-start.4 = (f32[8,4096]{1,0:T(8,128)S(1)}, f32[8,4096]{1,0:T(8,128)S(1)}, u32[]{:S(2)}, u32[]{:S(2)}) collective-permute-start(f32[8,4096]{1,0:T(8,128)S(1)} %get-tuple-element.62), channel_id=1, source_target_pairs={{0,1},{1,2},{2,3},{3,4},{4,5},{5,6},{6,7},{7,8},{8,9},{9,10},{10,1... | collective-permute-start | bytes 393224 | tf_op jit(solution)/shard_map/ppermute | solution.py:23
  17.2 36.6 %collective-permute-start.5 = (f32[8,4096]{1,0:T(8,128)S(1)}, f32[8,4096]{1,0:T(8,128)S(1)}, u32[]{:S(2)}, u32[]{:S(2)}) collective-permute-start(f32[8,4096]{1,0:T(8,128)S(1)} %get-tuple-element.63), channel_id=1, source_target_pairs={{1,0},{2,1},{3,2},{4,3},{5,4},{6,5},{7,6},{8,7},{9,8},{10,9},{11,1... | collective-permute-start | bytes 393224 | tf_op jit(solution)/shard_map/ppermute | solution.py:26
  26.9 13.7 %copy-start.4 = (f32[32,4096]{1,0:T(8,128)S(1)}, f32[32,4096]{1,0:T(8,128)}, u32[]{:S(2)}) copy-start(f32[32,4096]{1,0:T(8,128)} %param.9) | copy-start | bytes 1572868
  37.4 5.8 copy-start.5
  45.0 5.7 collective-permute-start.2
  49.2 4.3 collective-permute-start.3
  105.6 29.5 %collective-permute-start.6 = (f32[8,6,4096]{2,0,1:T(8,128)}, f32[8,6,4096]{2,0,1:T(8,128)}, u32[]{:S(2)}, u32[]{:S(2)}) collective-permute-start(f32[8,6,4096]{2,0,1:T(8,128)} %slice.86), channel_id=1, source_target_pairs={{0,1},{1,2},{2,3},{3,4},{4,5},{5,6},{6,7},{7,8},{8,9},{9,10},{10,1... | collective-permute-start | bytes 2359304 | tf_op jit(solution)/shard_map/ppermute | solution.py:23
  112.0 24.8 %collective-permute-start.7 = (f32[8,6,4096]{2,0,1:T(8,128)S(1)}, f32[8,6,4096]{2,0,1:T(8,128)S(1)}, u32[]{:S(2)}, u32[]{:S(2)}) collective-permute-start(f32[8,6,4096]{2,0,1:T(8,128)S(1)} %slice.88), channel_id=1, source_target_pairs={{1,0},{2,1},{3,2},{4,3},{5,4},{6,5},{7,6},{8,7},{9,8},{10,9},{11,1... | collective-permute-start | bytes 2359304 | tf_op jit(solution)/shard_map/ppermute | solution.py:26
  120.4 16.9 %copy-start.3 = (f32[32,6,4096]{2,1,0:T(8,128)S(1)}, f32[32,6,4096]{2,1,0:T(8,128)}, u32[]{:S(2)}) copy-start(f32[32,6,4096]{2,1,0:T(8,128)} %reshape.186) | copy-start | bytes 9437188
  224.9 11.4 %copy-start.1 = (f32[8,6,64,64]{3,2,0,1:T(8,128)}, f32[8,6,64,64]{3,2,0,1:T(8,128)S(1)}, u32[]{:S(2)}) copy-start(f32[8,6,64,64]{3,2,0,1:T(8,128)S(1)} %reshape.197) | copy-start | bytes 2359300 | tf_op jit(solution)/shard_map/while
  224.9 16.4 %copy-start = (f32[8,6,12,64,64]{3,4,2,0,1:T(8,128)S(1)}, f32[8,6,12,64,64]{3,4,2,0,1:T(8,128)}, u32[]{:S(2)}) copy-start(f32[8,6,12,64,64]{3,4,2,0,1:T(8,128)} %broadcast_select_fusion.2) | copy-start | bytes 28311556 | tf_op jit(solution)/shard_map/while
  321.5 11.4 %copy-start.1 = (f32[8,6,64,64]{3,2,0,1:T(8,128)}, f32[8,6,64,64]{3,2,0,1:T(8,128)S(1)}, u32[]{:S(2)}) copy-start(f32[8,6,64,64]{3,2,0,1:T(8,128)S(1)} %reshape.197) | copy-start | bytes 2359300 | tf_op jit(solution)/shard_map/while
  321.5 16.4 %copy-start = (f32[8,6,12,64,64]{3,4,2,0,1:T(8,128)S(1)}, f32[8,6,12,64,64]{3,4,2,0,1:T(8,128)}, u32[]{:S(2)}) copy-start(f32[8,6,12,64,64]{3,4,2,0,1:T(8,128)} %broadcast_select_fusion.2) | copy-start | bytes 28311556 | tf_op jit(solution)/shard_map/while
  418.0 11.4 %copy-start.1 = (f32[8,6,64,64]{3,2,0,1:T(8,128)}, f32[8,6,64,64]{3,2,0,1:T(8,128)S(1)}, u32[]{:S(2)}) copy-start(f32[8,6,64,64]{3,2,0,1:T(8,128)S(1)} %reshape.197) | copy-start | bytes 2359300 | tf_op jit(solution)/shard_map/while
  418.0 16.4 %copy-start = (f32[8,6,12,64,64]{3,4,2,0,1:T(8,128)S(1)}, f32[8,6,12,64,64]{3,4,2,0,1:T(8,128)}, u32[]{:S(2)}) copy-start(f32[8,6,12,64,64]{3,4,2,0,1:T(8,128)} %broadcast_select_fusion.2) | copy-start | bytes 28311556 | tf_op jit(solution)/shard_map/while
  514.5 11.4 %copy-start.1 = (f32[8,6,64,64]{3,2,0,1:T(8,128)}, f32[8,6,64,64]{3,2,0,1:T(8,128)S(1)}, u32[]{:S(2)}) copy-start(f32[8,6,64,64]{3,2,0,1:T(8,128)S(1)} %reshape.197) | copy-start | bytes 2359300 | tf_op jit(solution)/shard_map/while
  514.6 16.4 %copy-start = (f32[8,6,12,64,64]{3,4,2,0,1:T(8,128)S(1)}, f32[8,6,12,64,64]{3,4,2,0,1:T(8,128)}, u32[]{:S(2)}) copy-start(f32[8,6,12,64,64]{3,4,2,0,1:T(8,128)} %broadcast_select_fusion.2) | copy-start | bytes 28311556 | tf_op jit(solution)/shard_map/while
  598.5 6.1 collective-permute-start.8
  601.7 7.6 %collective-permute-start.9 = (f32[4,12,64,64]{2,3,0,1:T(8,128)S(1)}, f32[4,12,64,64]{2,3,0,1:T(8,128)S(1)}, u32[]{:S(2)}, u32[]{:S(2)}) collective-permute-start(f32[4,12,64,64]{2,3,0,1:T(8,128)S(1)} %get-tuple-element.60), channel_id=1, source_target_pairs={{1,0},{2,1},{3,2},{4,3},{5,4},{6,5},{7,6},{8,7},{9,8},{10,9},{11,1... | collective-permute-start | bytes 2359304 | tf_op jit(solution)/shard_map/ppermute | solution.py:34
  609.8 5.3 copy-start.8
  609.8 6.5 copy-start.7
  (2 other events, 6.3 us)
Sparse Core Ops, SparseCore 0:
  615.2 79.5 all-gather.1
where the time goes:
time: 723 us; the launch traced here: 710 us
  local copies, waits for them, and re-layouts  284 us (39%)
  matrix products  227 us (31%)
  other arithmetic  56.1 us (8%)
  waiting for transfers between devices  52.2 us (7%)
  blocking collectives  35.2 us (5%)
  starting transfers between devices  26.8 us (4%)
  between operations  14.8 us (2%)
  loops' own time  14.5 us (2%)
    gather x12, local copies, waits for them, and re-layouts, apply_rows(): jnp.take(ext_dense, index_group, axis=0).reshape(count, K, 3 * G, B, BC)  191 us
    dot_general x20, matrix products, apply_rows(): jnp.einsum('sqp,scpw->scqw', a_mats[:, stored], gathered[:, stored], prec...  103 us
    select_n x8, other arithmetic, apply_rows(): jnp.take(ext_dense, index_group, axis=0).reshape(count, K, 3 * G, B, BC)  55.2 us
    dot_general x1, matrix products, coarse_part(): return jnp.einsum('ilqv,icqw->lcvw', dense, applied_rows, precision=highest)  50.4 us
    all_gather x1, waiting for transfers between devices, local(): lax.all_gather(coarse_rows, 'col', axis=0, tiled=True)  43.1 us
    unnamed x1, blocking collectives  35.2 us
    dot_general x4, matrix products, apply_rows(): jnp.einsum('sqp,scpw->scqw', a_mats[:, 0], gathered[:, 0], precision=high...  27.3 us
    ppermute x4, starting transfers between devices, padded(): lax.ppermute(lax.slice_in_dim(block, block.shape[dim] - width, None, axis...  17.2 us
  transfers between devices with their start and end apart: 11, of which 4 were waited for; matrix products, arithmetic and copies ran while one was open for 7% of the time, Pallas kernels for 0%

commit v1 on v0

v1 whole, which is shorter than its diff:
```python
import jax
import jax.numpy as jnp
from jax import lax
from jax.experimental import pallas as pl
from jax.experimental.pallas import tpu as pltpu
from jax.sharding import PartitionSpec as P

B = 64
K = 6
G = 4
R = 32
H = 8
T = 32
E = R + H
SIDE = 2 * H
AXES = ("row", "col")
RELAX = 2.0 / 3.0
F32 = jnp.float32
BF16 = jnp.bfloat16
I32 = jnp.int32


def split(x):
    hi = x.astype(BF16)
    return hi, (x - hi.astype(F32)).astype(BF16)


def lanes_of(shape):
    return lax.broadcasted_iota(I32, shape, 1)


def take_lanes(x, index):
    return jnp.take_along_axis(x, index, axis=1)


def twice(x):
    return jnp.concatenate([x, x], axis=0)


def raw_block(ref, base, row):
    return ref[pl.ds(base + row, T, stride=H), :]


def galerkin_kernel(
    ints, a_own, t_own, a_low, t_low, t_high, *refs, ncol
):
    n_out = 3 * ncol
    outs, (tf, tb, lhs, pf, w, pt_hi, pt_lo, ap, ap_hi, ap_lo, part) = refs[:n_out], refs[n_out:]
    ups, owns, downs = outs[:ncol], outs[ncol : 2 * ncol], outs[2 * ncol :]
    device = ints[9, 4]
    col = lax.rem(device, ncol)

    lane = lanes_of((T, 128))
    half = lax.rem(lane, 64)
    plain = (half, half + 64)
    sorted_half = jnp.where(half < 32, 2 * half, 2 * half - 63)
    sorted_lanes = (sorted_half, sorted_half + 64)

    def doubled(x, index):
        return jnp.concatenate([take_lanes(x, index[0]), take_lanes(x, index[1])], axis=0)

    def load_t(ref, base, row, slot):
        x = doubled(raw_block(ref, base, row), plain)
        hi, lo = split(x)
        tf[slot] = x
        tb[slot] = jnp.concatenate([hi, lo], axis=0)

    def t_rows(i, carry):
        base = (i // H) * (T * H)
        row = lax.rem(i, H)
        load_t(t_low, base, row, i)
        load_t(t_own, base, row, R + i)
        return carry

    lax.fori_loop(0, R, t_rows, 0, unroll=2)

    def t_next(i, carry):
        load_t(t_high, 0, i, 2 * R + i)
        return carry

    lax.fori_loop(0, H, t_next, 0, unroll=2)

    row_of = lax.broadcasted_iota(I32, (64, 128), 0)
    lane_of = lanes_of((64, 128))
    diagonal_mask = row_of == lane_of
    upper_half = lane_of // 64

    def position(column):
        return jnp.clip(column - (device - 1) * R, 0, 2 * R + H - 1)

    def aggregate_of(j):
        block = j // R
        return ints[8 * block, j - R * block]

    def prolong(e, a_ref, base_of, row, columns):
        for pair in range(4):
            pf[e, pair] = jnp.zeros((64, 128), F32)
        scale = None
        for k in range(K):
            x = doubled(raw_block(a_ref, base_of(k), row), sorted_lanes)
            hi, lo = split(x)
            left = jnp.concatenate([hi, lo], axis=1)
            lhs[e * K + k] = left
            j = position(columns(k))
            right = tb[j]
            product = jnp.dot(left, twice(right), preferred_element_type=F32)
            if k == 0:
                diagonal = jnp.sum(jnp.where(diagonal_mask, x, 0.0), axis=1, keepdims=True)
                scale = -RELAX / jnp.where(diagonal == 0.0, 1.0, diagonal)
            value = product * scale
            if k == 0:
                value = value + tf[j]
            slot = aggregate_of(j) + jnp.where(j // R == 1, 0, G)
            pf[e, slot // 2] += jnp.where(upper_half == lax.rem(slot, 2), value, 0.0)

    def prolong_low(i, carry):
        prolong(i, a_low, lambda k: k * (T * H), i, lambda k: ints[2 + k, R - H + i])
        return carry

    def prolong_own(i, carry):
        g = i // H
        prolong(
            H + i,
            a_own,
            lambda k: (k * (R // H) + g) * (T * H),
            lax.rem(i, H),
            lambda k: ints[10 + k, i],
        )
        return carry

    lax.fori_loop(0, H, prolong_low, 0, unroll=2)
    lax.fori_loop(0, R, prolong_own, 0, unroll=2)

    w[E] = jnp.zeros((128, 512), BF16)

    def arrange(i, carry):
        for half_index in range(2):
            e = 2 * i + half_index
            for pair in range(4):
                hi, lo = split(pf[e, pair])
                w[e, 0:64, pair * 128 : pair * 128 + 128] = hi
                w[e, 64:128, pair * 128 : pair * 128 + 128] = lo
        where = pl.ds(pl.multiple_of(i * 128, 128), 128)
        for pair in range(4):
            both = jnp.concatenate([pf[2 * i, pair], pf[2 * i + 1, pair]], axis=0)
            hi, lo = split(both.T)
            pt_hi[pair * 128 : pair * 128 + 128, where] = hi
            pt_lo[pair * 128 : pair * 128 + 128, where] = lo
        return carry

    lax.fori_loop(0, E // 2, arrange, 0)

    def apply(e, columns, lowest):
        ap[0] = jnp.zeros((64, 256), F32)
        ap[2] = jnp.zeros((64, 256), F32)
        own = jnp.zeros((64, 256), F32)
        for k in range(K):
            j = position(columns(k))
            valid = (j >= lowest) & (j < 2 * R)
            source = jnp.where(valid, j - (R - H), E)
            product = jnp.dot(lhs[e * K + k], twice(w[source]), preferred_element_type=F32)
            own = own + product[:, :256]
            place = jnp.where(source < SIDE, 0, 2)
            ap[place] += product[:, 256:]
        where = pl.ds(pl.multiple_of(e * 64, 64), 64)
        for third, value in enumerate((ap[0], own, ap[2])):
            hi, lo = split(value)
            ap_hi[where, third * 256 : third * 256 + 256] = hi
            ap_lo[where, third * 256 : third * 256 + 256] = lo

    def apply_low(i, carry):
        apply(i, lambda k: ints[2 + k, R - H + i], R)
        return carry

    def apply_own(i, carry):
        apply(H + i, lambda k: ints[10 + k, i], R - H)
        return carry

    lax.fori_loop(0, H, apply_low, 0, unroll=2)
    lax.fori_loop(0, R, apply_own, 0, unroll=2)

    def coarse(rows, inner):
        return (
            jnp.dot(pt_hi[rows, inner], ap_hi[inner, :], preferred_element_type=F32)
            + jnp.dot(pt_hi[rows, inner], ap_lo[inner, :], preferred_element_type=F32)
            + jnp.dot(pt_lo[rows, inner], ap_hi[inner, :], preferred_element_type=F32)
        )

    products = (
        coarse(slice(256, 512), slice(0, SIDE * 64)),
        coarse(slice(0, 256), slice(0, E * 64)),
        coarse(slice(256, 512), slice((E - H) * 64, E * 64)),
    )
    for which in range(3):
        for pair in range(6):
            part[which, pair] = products[which][:, pair * 128 : pair * 128 + 128]

    low_lanes = lane < 64

    def give(out, which, s, home, ints_row):
        chosen = jnp.int32(0)
        place = jnp.int32(-1)
        for g in range(G):
            spot = ints[ints_row, g]
            distance = lax.rem(lax.rem(spot // G, ncol) - home + ncol, ncol)
            hit = distance == s
            chosen = jnp.where(hit, g, chosen)
            place = jnp.where(hit, lax.rem(spot, G), place)
        for pair in range(6):
            even = part[which, pair, pl.ds(chosen * 64, T, stride=2), :]
            odd = part[which, pair, pl.ds(chosen * 64 + 1, T, stride=2), :]
            first = jnp.where(low_lanes, even, pltpu.roll(odd, 64, 1))
            second = jnp.where(low_lanes, pltpu.roll(even, 64, 1), odd)
            out[2 * pair * T : (2 * pair + 1) * T, :] = first
            out[(2 * pair + 1) * T : (2 * pair + 2) * T, :] = second
        out[3 * G * T : 3 * G * T + 8, :] = jnp.full((8, 128), place.astype(F32))

    for s in range(ncol):
        give(downs[s], 0, s, lax.rem(col + ncol - 1, ncol), 1)
        give(owns[s], 1, s, col, 9)
        give(ups[s], 2, s, lax.rem(col + 1, ncol), 17)


def combine_kernel(*refs, ncol):
    ups, owns, downs, out = refs[:ncol], refs[ncol : 2 * ncol], refs[2 * ncol : 3 * ncol], refs[-1]
    span = G * T
    for j in range(G):
        for c in range(5):
            value = jnp.zeros((span, 128), F32)
            for s in range(ncol):
                term = None
                for source, shift in ((ups[s], 0), (owns[s], 1), (downs[s], 2)):
                    if 0 <= c - shift < 3:
                        piece = source[(c - shift) * span : (c - shift + 1) * span, :]
                        term = piece if term is None else term + piece
                mark = owns[s][3 * span : 3 * span + 1, :] == float(j)
                value = jnp.where(mark, term, value)
            out[pl.ds(c * span * G + j, span, stride=G), :] = value


def local(a_blocks, columns, tentative, aggregate, owner, *, nrow, ncol):
    count = nrow * ncol
    device = lax.axis_index(AXES).astype(I32)
    up = [(d, d + 1) for d in range(count - 1)]
    down = [(d + 1, d) for d in range(count - 1)]

    a_rows = (
        a_blocks.transpose(1, 0, 2)
        .reshape(K, R // H, H, T, 128)
        .transpose(0, 1, 3, 2, 4)
    )
    t_rows = tentative.reshape(R // H, H, T, 128).transpose(0, 2, 1, 3)
    own_ints = jnp.concatenate(
        [
            jnp.pad(aggregate.reshape(1, R), ((0, 0), (0, 128 - R))),
            jnp.pad(
                jnp.concatenate([owner, device.reshape(1)]).reshape(1, G + 1),
                ((0, 0), (0, 128 - G - 1)),
            ),
            jnp.pad(columns.T, ((0, 0), (0, 128 - R))),
        ],
        axis=0,
    )
    meta = own_ints.astype(F32)
    last = t_rows[R // H - 1].reshape(T * H, 128)
    first = t_rows[0].reshape(T * H, 128)
    small_up = lax.ppermute(jnp.concatenate([last, meta], axis=0), AXES, up)
    small_down = lax.ppermute(jnp.concatenate([first, meta], axis=0), AXES, down)
    big = lax.ppermute(
        jnp.concatenate(
            [
                a_rows[:, R // H - 1].reshape(K * T * H, 128),
                t_rows[: R // H - 1].reshape((R // H - 1) * T * H, 128),
            ],
            axis=0,
        ),
        AXES,
        up,
    )
    ints = jnp.concatenate(
        [small_up[T * H :].astype(I32), own_ints, small_down[T * H :].astype(I32)], axis=0
    )
    t_low = jnp.concatenate([big[K * T * H :], small_up[: T * H]], axis=0)

    payload = jax.ShapeDtypeStruct((3 * G * T + 8, 128), F32)
    vmem = pl.BlockSpec(memory_space=pltpu.VMEM)
    smem = pl.BlockSpec(memory_space=pltpu.SMEM)
    parts = pl.pallas_call(
        lambda *refs: galerkin_kernel(*refs, ncol=ncol),
        out_shape=[payload] * (3 * ncol),
        in_specs=[smem] + [vmem] * 5,
        out_specs=[vmem] * (3 * ncol),
        scratch_shapes=[
            pltpu.VMEM((2 * R + H, 64, 128), F32),
            pltpu.VMEM((2 * R + H, 128, 128), BF16),
            pltpu.VMEM((E * K, 64, 256), BF16),
            pltpu.VMEM((E, 4, 64, 128), F32),
            pltpu.VMEM((E + 1, 128, 512), BF16),
            pltpu.VMEM((512, E * 64), BF16),
            pltpu.VMEM((512, E * 64), BF16),
            pltpu.VMEM((3, 64, 256), F32),
            pltpu.VMEM((E * 64, 768), BF16),
            pltpu.VMEM((E * 64, 768), BF16),
            pltpu.VMEM((3, 6, 256, 128), F32),
        ],
        compiler_params=pltpu.CompilerParams(vmem_limit_bytes=58 * 1024 * 1024),
    )(
        ints,
        a_rows.reshape(K * R * T, 128),
        t_rows.reshape(R * T, 128),
        big[: K * T * H],
        t_low,
        small_down[: T * H],
    )
    ups, owns, downs = parts[:ncol], parts[ncol : 2 * ncol], parts[2 * ncol :]

    def routed(block, offset, s):
        route = []
        for d in range(count):
            home = d + offset
            if 0 <= home < count:
                route.append((d, home // ncol * ncol + (home + s) % ncol))
        if all(source == target for source, target in route):
            return block
        return lax.ppermute(block, AXES, route)

    ups = [routed(ups[s], 1, s) for s in range(ncol)]
    owns = [routed(owns[s], 0, s) for s in range(ncol)]
    downs = [routed(downs[s], -1, s) for s in range(ncol)]
    result = pl.pallas_call(
        lambda *refs: combine_kernel(*refs, ncol=ncol),
        out_shape=jax.ShapeDtypeStruct((5 * G * T * G, 128), F32),
        in_specs=[vmem] * (3 * ncol),
        out_specs=vmem,
        compiler_params=pltpu.CompilerParams(vmem_limit_bytes=32 * 1024 * 1024),
    )(*ups, *owns, *downs)
    return result.reshape(5 * G, T, G, 128).transpose(2, 0, 1, 3).reshape(G, 5 * G, T * 128)


def solution(mesh):
    placed = (
        P(AXES, None, None),
        P(AXES, None),
        P(AXES, None),
        P(AXES),
        P(AXES),
    )
    nrow, ncol = mesh.shape["row"], mesh.shape["col"]
    return jax.shard_map(
        lambda *args: local(*args, nrow=nrow, ncol=ncol),
        mesh=mesh,
        in_specs=placed,
        out_specs=P(AXES, None, None),
        check_vma=False,
    )
```

time: 723 us -> 102 us (0.14); the launches traced: 710 us -> 102 us
  local copies, waits for them, and re-layouts: 284 us -> 7.58 us
  matrix products: 227 us -> 0 us
  other arithmetic: 56.1 us -> 1.04 us
  Pallas kernels: 0 us -> 39.1 us
  waiting for transfers between devices: 52.2 us -> 13.8 us
  blocking collectives: 35.2 us -> 0 us
  between operations: 14.8 us -> 0.26 us
  loops' own time: 14.5 us -> 0 us
  starting transfers between devices: 26.8 us -> 40.2 us
    dot_general x29 -> x0, matrix products: 227 us -> none  [the longest x20 103 us: apply_rows(): jnp.einsum('sqp,scpw->scqw', a_mats[:, stored], gathered[:, stored], prec...]
    gather x19 -> x0, local copies, waits for them, and re-layouts: 211 us -> none  [the longest x12 191 us: apply_rows(): jnp.take(ext_dense, index_group, axis=0).reshape(count, K, 3 * G, B, BC)]
    select_n x9 -> x0, other arithmetic: 55.2 us -> none  [the longest x8 55.2 us: apply_rows(): jnp.take(ext_dense, index_group, axis=0).reshape(count, K, 3 * G, B, BC)]
    all_gather x1 -> x0, waiting for transfers between devices: 43.1 us -> none  [local(): lax.all_gather(coarse_rows, 'col', axis=0, tiled=True)]
    pallas_call x0 -> x2, Pallas kernels: none -> 39.1 us  [the longest x1 37.2 us: local(): pl.pallas_call(lambda *refs: galerkin_kernel(*refs, ncol=ncol), out_shape...]
    unnamed x1 -> x0, blocking collectives: 35.2 us -> none
    reshape x9 -> x0, local copies, waits for them, and re-layouts: 31.8 us -> none  [the longest x2 13.6 us: prolong_rows(): return (smooth.reshape(row_count, K, B * BC), labels)]
    another operation x1 -> x0, loops' own time: 14.5 us -> none  [local(): lax.map(apply_group, (a_blocks.reshape(group_count, 8, K, B * B), local_i...]
  transfers between devices with their start and end apart: 11 -> 14, of which waited for: 4 -> 6; matrix products, arithmetic and copies ran while one was open for 7% -> 3% of each run, Pallas kernels for 0% -> 0%
where the time goes in v1:
time: 102 us
  starting transfers between devices  40.2 us (39%)
  Pallas kernels  39.1 us (38%)
  waiting for transfers between devices  13.8 us (14%)
  local copies, waits for them, and re-layouts  7.58 us (7%)
  other arithmetic  1.04 us (1%)
    pallas_call x1, Pallas kernels, local(): pl.pallas_call(lambda *refs: galerkin_kernel(*refs, ncol=ncol), out_shape...  37.2 us
    ppermute x11, starting transfers between devices, routed(): return lax.ppermute(block, AXES, route)  31.2 us
    ppermute x11, waiting for transfers between devices, routed(): return lax.ppermute(block, AXES, route)  12.9 us
    ppermute x1, starting transfers between devices, local(): small_up = lax.ppermute(jnp.concatenate([last, meta], axis=0), AXES, up)  5.1 us
    ppermute x1, starting transfers between devices, local(): lax.ppermute(jnp.concatenate([a_rows[:, R // H - 1].reshape(K * T * H, 12...  2.56 us
    transpose x1, local copies, waits for them, and re-layouts, local(): a_rows = a_blocks.transpose(1, 0, 2).reshape(K, R // H, H, T, 128).transp...  2.1 us
  transfers between devices with their start and end apart: 14, of which 6 were waited for; matrix products, arithmetic and copies ran while one was open for 3% of the time, Pallas kernels for 0%

profile of v1, /device:TPU:0, one launch (start us, length us, event | category | flops | bytes accessed | tf_op | source)
XLA Modules:
  0.0 101.9 jit_solution(13802339031955404853)
XLA Ops:
  0.0 1.0 %slice.45 = f32[3,32,8,128]{3,2,1,0:T(8,128)S(1)} slice(f32[4,32,8,128]{3,2,1,0:T(8,128)} %bitcast.34), slice={[0:3], [0:32], [0:8], [0:128]} | slice | bytes 786432 | tf_op jit(solution)/shard_map/slice | solution.py:273
  1.0 2.1 %copy_bitcast_fusion = f32[6,4,32,8,128]{4,3,2,0,1:T(8,128)S(1)} fusion(f32[32,6,4096]{2,0,1:T(8,128)} %param.5), kind=kLoop, calls=%fused_computation | loop fusion | bytes 6291456 | tf_op jit(solution)/shard_map/transpose | solution.py:250
  3.3 2.6 %collective-permute-start.2 = (f32[2304,128]{1,0:T(8,128)S(1)}, f32[2304,128]{1,0:T(8,128)S(1)}, u32[]{:S(2)}, u32[]{:S(2)}) collective-permute-start(f32[2304,128]{1,0:T(8,128)S(1)} %pad_maximum_fusion), channel_id=1, source_target_pairs={{0,1},{1,2},{2,3},{3,4},{4,5},{5,6},{6,7},{7,8},{8,9},{9,10},{10,1... | collective-permute-start | bytes 3538952 | tf_op jit(solution)/shard_map/ppermute | solution.py:269
  6.1 1.3 %collective-permute-start.1 = (f32[264,128]{1,0:T(8,128)S(1)}, f32[264,128]{1,0:T(8,128)S(1)}, u32[]{:S(2)}, u32[]{:S(2)}) collective-permute-start(f32[264,128]{1,0:T(8,128)S(1)} %get-tuple-element.31), channel_id=1, source_target_pairs={{1,0},{2,1},{3,2},{4,3},{5,4},{6,5},{7,6},{8,7},{9,8},{10,9},{11,1... | collective-permute-start | bytes 405512 | tf_op jit(solution)/shard_map/ppermute | solution.py:268
  7.4 5.1 %collective-permute-start = (f32[264,128]{1,0:T(8,128)S(1)}, f32[264,128]{1,0:T(8,128)S(1)}, u32[]{:S(2)}, u32[]{:S(2)}) collective-permute-start(f32[264,128]{1,0:T(8,128)S(1)} %get-tuple-element.32), channel_id=1, source_target_pairs={{0,1},{1,2},{2,3},{3,4},{4,5},{5,6},{6,7},{7,8},{8,9},{9,10},{10,1... | collective-permute-start | bytes 405512 | tf_op jit(solution)/shard_map/ppermute | solution.py:267
  12.5 0.9 collective-permute-done
  13.5 1.8 %concatenate.26.refs_0_ = s32[24,128]{1,0:T(8,128)} concatenate(s32[8,128]{1,0:T(8,128)S(1)} %slice_convert_fusion.1, s32[1,128]{1,0:T(1,128)S(1)} %pad.12, s32[1,128]{1,0:T(1,128)S(1)} %pad.13, s32[6,128]{1,0:T(8,128)S(1)} %pad.14, s32[8,128]{1,0:T(8,128)S(1)} %slice_convert_fusion), dimensions={0} | concatenate | bytes 24576 | tf_op jit(solution)/shard_map/concatenate | solution.py:280
  16.8 0.9 slice.46.refs_3_
  17.8 37.2 %shard_map.55 = (f32[392,128]{1,0:T(8,128)}, f32[392,128]{1,0:T(8,128)}, f32[392,128]{1,0:T(8,128)}, f32[392,128]{1,0:T(8,128)}, f32[392,128]{1,0:T(8,128)}, /*i...) custom-call(s32[24,128]{1,0:T(8,128)} %concatenate.26.refs_0_, ...), custom_call_target="tpu_custom_call" | custom-call | tf_op jit(solution)/shard_map/pallas_call | solution.py:288
  55.0 12.9 %collective-permute-start.3 = (f32[392,128]{1,0:T(8,128)}, f32[392,128]{1,0:T(8,128)S(1)}, u32[]{:S(2)}, u32[]{:S(2)}) collective-permute-start(f32[392,128]{1,0:T(8,128)} %get-tuple-element.17), channel_id=1, source_target_pairs={{0,1},{1,2},{2,3},{3,4},{4,5},{5,6},{6,7},{7,8},{8,9},{9,10},{10,1... | collective-permute-start | bytes 602120 | tf_op jit(solution)/shard_map/ppermute | solution.py:325
  67.9 4.3 %collective-permute-start.4 = (f32[392,128]{1,0:T(8,128)}, f32[392,128]{1,0:T(8,128)S(1)}, u32[]{:S(2)}, u32[]{:S(2)}) collective-permute-start(f32[392,128]{1,0:T(8,128)} %get-tuple-element.18), channel_id=1, source_target_pairs={{0,2},{1,3},{2,0},{3,5},{4,6},{5,7},{6,4},{7,9},{8,10},{9,11},{10,... | collective-permute-start | bytes 602120 | tf_op jit(solution)/shard_map/ppermute | solution.py:325
  72.2 4.3 %collective-permute-start.5 = (f32[392,128]{1,0:T(8,128)}, f32[392,128]{1,0:T(8,128)S(1)}, u32[]{:S(2)}, u32[]{:S(2)}) collective-permute-start(f32[392,128]{1,0:T(8,128)} %get-tuple-element.19), channel_id=1, source_target_pairs={{0,3},{1,0},{2,1},{3,6},{4,7},{5,4},{6,5},{7,10},{8,11},{9,8},{10,... | collective-permute-start | bytes 602120 | tf_op jit(solution)/shard_map/ppermute | solution.py:325
  76.5 1.6 %collective-permute-start.6 = (f32[392,128]{1,0:T(8,128)}, f32[392,128]{1,0:T(8,128)S(1)}, u32[]{:S(2)}, u32[]{:S(2)}) collective-permute-start(f32[392,128]{1,0:T(8,128)} %get-tuple-element.20), channel_id=1, source_target_pairs={{0,0},{1,1},{2,2},{3,7},{4,4},{5,5},{6,6},{7,11},{8,8},{9,9},{10,1... | collective-permute-start | bytes 602120 | tf_op jit(solution)/shard_map/ppermute | solution.py:325
  78.1 3.0 %collective-permute-start.8 = (f32[392,128]{1,0:T(8,128)}, f32[392,128]{1,0:T(8,128)S(1)}, u32[]{:S(2)}, u32[]{:S(2)}) collective-permute-start(f32[392,128]{1,0:T(8,128)} %get-tuple-element.23), channel_id=1, source_target_pairs={{0,2},{1,3},{2,0},{3,1},{4,6},{5,7},{6,4},{7,5},{8,10},{9,11},{10,... | collective-permute-start | bytes 602120 | tf_op jit(solution)/shard_map/ppermute | solution.py:325
  81.1 1.3 %collective-permute-start.10 = (f32[392,128]{1,0:T(8,128)}, f32[392,128]{1,0:T(8,128)S(1)}, u32[]{:S(2)}, u32[]{:S(2)}) collective-permute-start(f32[392,128]{1,0:T(8,128)} %get-tuple-element.25), channel_id=1, source_target_pairs={{1,0},{2,1},{3,2},{4,3},{5,4},{6,5},{7,6},{8,7},{9,8},{10,9},{11,1... | collective-permute-start | bytes 602120 | tf_op jit(solution)/shard_map/ppermute | solution.py:325
  82.4 1.3 %collective-permute-start.11 = (f32[392,128]{1,0:T(8,128)}, f32[392,128]{1,0:T(8,128)S(1)}, u32[]{:S(2)}, u32[]{:S(2)}) collective-permute-start(f32[392,128]{1,0:T(8,128)} %get-tuple-element.26), channel_id=1, source_target_pairs={{1,1},{2,2},{3,3},{4,0},{5,5},{6,6},{7,7},{8,4},{9,9},{10,10},{11,... | collective-permute-start | bytes 602120 | tf_op jit(solution)/shard_map/ppermute | solution.py:325
  83.7 2.1 %collective-permute-done.7.refs_5_ = f32[392,128]{1,0:T(8,128)S(1)} collective-permute-done((f32[392,128]{1,0:T(8,128)}, f32[392,128]{1,0:T(8,128)S(1)}, u32[]{:S(2)}, u32[]{:S(2)}) %collective-permute-start.7) | collective-permute-done | bytes 200736 | tf_op jit(solution)/shard_map/ppermute | solution.py:325
  85.8 1.3 %collective-permute-start.12 = (f32[392,128]{1,0:T(8,128)}, f32[392,128]{1,0:T(8,128)S(1)}, u32[]{:S(2)}, u32[]{:S(2)}) collective-permute-start(f32[392,128]{1,0:T(8,128)} %get-tuple-element.27), channel_id=1, source_target_pairs={{1,2},{2,3},{3,0},{4,1},{5,6},{6,7},{7,4},{8,5},{9,10},{10,11},{11... | collective-permute-start | bytes 602120 | tf_op jit(solution)/shard_map/ppermute | solution.py:325
  87.1 1.3 %collective-permute-start.13 = (f32[392,128]{1,0:T(8,128)}, f32[392,128]{1,0:T(8,128)S(1)}, u32[]{:S(2)}, u32[]{:S(2)}) collective-permute-start(f32[392,128]{1,0:T(8,128)} %get-tuple-element.28), channel_id=1, source_target_pairs={{1,3},{2,0},{3,1},{4,2},{5,7},{6,4},{7,5},{8,6},{9,11},{10,8},{11,... | collective-permute-start | bytes 602120 | tf_op jit(solution)/shard_map/ppermute | solution.py:325
  88.4 3.5 %collective-permute-done.9.refs_7_ = f32[392,128]{1,0:T(8,128)S(1)} collective-permute-done((f32[392,128]{1,0:T(8,128)}, f32[392,128]{1,0:T(8,128)S(1)}, u32[]{:S(2)}, u32[]{:S(2)}) %collective-permute-start.9) | collective-permute-done | bytes 200736 | tf_op jit(solution)/shard_map/ppermute | solution.py:325
  92.6 2.6 %collective-permute-done.12.refs_10_ = f32[392,128]{1,0:T(8,128)S(1)} collective-permute-done((f32[392,128]{1,0:T(8,128)}, f32[392,128]{1,0:T(8,128)S(1)}, u32[]{:S(2)}, u32[]{:S(2)}) %collective-permute-start.12) | collective-permute-done | bytes 200736 | tf_op jit(solution)/shard_map/ppermute | solution.py:325
  95.2 3.9 %collective-permute-done.13.refs_11_ = f32[392,128]{1,0:T(8,128)S(1)} collective-permute-done((f32[392,128]{1,0:T(8,128)}, f32[392,128]{1,0:T(8,128)S(1)}, u32[]{:S(2)}, u32[]{:S(2)}) %collective-permute-start.13) | collective-permute-done | bytes 200736 | tf_op jit(solution)/shard_map/ppermute | solution.py:325
  99.1 0.9 copy-done
  100.1 1.9 %shard_map.56 = f32[2560,128]{1,0:T(8,128)} custom-call(f32[392,128]{1,0:T(8,128)S(1)} %collective-permute-done.3.refs_0_, f32[392,128]{1,0:T(8,128)S(1)} %collective-permute-done.4.refs_1_, f32[392,128]{1,0:T(8,128)S(1)} %collective-permute-done.5.refs_2_, f32[392,128]{1,0:T(8,128)S(1)} %collective-permute-done.6.refs_3_, f32[392,128]{1,0:T(8,128)S(1)} %copy-done, ...), custom_call_target="tpu_custom_call" | custom-call | tf_op jit(solution)/shard_map/pallas_call | solution.py:330
  (35 shorter events, 2.6 us)
Async XLA Ops:
  3.1 2.8 %copy-start.3 = (s32[4]{0:T(128)S(1)}, s32[4]{0:T(128)}, u32[]{:S(2)}) copy-start(s32[4]{0:T(128)} %param.9) | copy-start | bytes 52
  3.1 2.9 %copy-start.4 = (s32[32]{0:T(128)S(1)}, s32[32]{0:T(128)}, u32[]{:S(2)}) copy-start(s32[32]{0:T(128)} %param.8) | copy-start | bytes 388
  3.2 2.9 %copy-start.2 = (s32[32,6]{0,1:T(8,128)S(1)}, s32[32,6]{0,1:T(8,128)}, u32[]{:S(2)}) copy-start(s32[32,6]{0,1:T(8,128)} %param.6) | copy-start | bytes 2308
  3.2 2.9 %copy-start.1 = (f32[32,4096]{1,0:T(8,128)S(1)}, f32[32,4096]{1,0:T(8,128)}, u32[]{:S(2)}) copy-start(f32[32,4096]{1,0:T(8,128)} %param.7) | copy-start | bytes 1572868
  3.3 12.6 %collective-permute-start.2 = (f32[2304,128]{1,0:T(8,128)S(1)}, f32[2304,128]{1,0:T(8,128)S(1)}, u32[]{:S(2)}, u32[]{:S(2)}) collective-permute-start(f32[2304,128]{1,0:T(8,128)S(1)} %pad_maximum_fusion), channel_id=1, source_target_pairs={{0,1},{1,2},{2,3},{3,4},{4,5},{5,6},{6,7},{7,8},{8,9},{9,10},{10,1... | collective-permute-start | bytes 3538952 | tf_op jit(solution)/shard_map/ppermute | solution.py:269
  6.1 6.4 %collective-permute-start.1 = (f32[264,128]{1,0:T(8,128)S(1)}, f32[264,128]{1,0:T(8,128)S(1)}, u32[]{:S(2)}, u32[]{:S(2)}) collective-permute-start(f32[264,128]{1,0:T(8,128)S(1)} %get-tuple-element.31), channel_id=1, source_target_pairs={{1,0},{2,1},{3,2},{4,3},{5,4},{6,5},{7,6},{8,7},{9,8},{10,9},{11,1... | collective-permute-start | bytes 405512 | tf_op jit(solution)/shard_map/ppermute | solution.py:268
  7.4 6.1 %collective-permute-start = (f32[264,128]{1,0:T(8,128)S(1)}, f32[264,128]{1,0:T(8,128)S(1)}, u32[]{:S(2)}, u32[]{:S(2)}) collective-permute-start(f32[264,128]{1,0:T(8,128)S(1)} %get-tuple-element.32), channel_id=1, source_target_pairs={{0,1},{1,2},{2,3},{3,4},{4,5},{5,6},{6,7},{7,8},{8,9},{9,10},{10,1... | collective-permute-start | bytes 405512 | tf_op jit(solution)/shard_map/ppermute | solution.py:267
  55.0 23.1 %collective-permute-start.3 = (f32[392,128]{1,0:T(8,128)}, f32[392,128]{1,0:T(8,128)S(1)}, u32[]{:S(2)}, u32[]{:S(2)}) collective-permute-start(f32[392,128]{1,0:T(8,128)} %get-tuple-element.17), channel_id=1, source_target_pairs={{0,1},{1,2},{2,3},{3,4},{4,5},{5,6},{6,7},{7,8},{8,9},{9,10},{10,1... | collective-permute-start | bytes 602120 | tf_op jit(solution)/shard_map/ppermute | solution.py:325
  67.9 13.2 %collective-permute-start.4 = (f32[392,128]{1,0:T(8,128)}, f32[392,128]{1,0:T(8,128)S(1)}, u32[]{:S(2)}, u32[]{:S(2)}) collective-permute-start(f32[392,128]{1,0:T(8,128)} %get-tuple-element.18), channel_id=1, source_target_pairs={{0,2},{1,3},{2,0},{3,5},{4,6},{5,7},{6,4},{7,9},{8,10},{9,11},{10,... | collective-permute-start | bytes 602120 | tf_op jit(solution)/shard_map/ppermute | solution.py:325
  72.2 8.9 %collective-permute-start.5 = (f32[392,128]{1,0:T(8,128)}, f32[392,128]{1,0:T(8,128)S(1)}, u32[]{:S(2)}, u32[]{:S(2)}) collective-permute-start(f32[392,128]{1,0:T(8,128)} %get-tuple-element.19), channel_id=1, source_target_pairs={{0,3},{1,0},{2,1},{3,6},{4,7},{5,4},{6,5},{7,10},{8,11},{9,8},{10,... | collective-permute-start | bytes 602120 | tf_op jit(solution)/shard_map/ppermute | solution.py:325
  76.5 5.9 %collective-permute-start.6 = (f32[392,128]{1,0:T(8,128)}, f32[392,128]{1,0:T(8,128)S(1)}, u32[]{:S(2)}, u32[]{:S(2)}) collective-permute-start(f32[392,128]{1,0:T(8,128)} %get-tuple-element.20), channel_id=1, source_target_pairs={{0,0},{1,1},{2,2},{3,7},{4,4},{5,5},{6,6},{7,11},{8,8},{9,9},{10,1... | collective-permute-start | bytes 602120 | tf_op jit(solution)/shard_map/ppermute | solution.py:325
  78.0 7.7 %collective-permute-start.7 = (f32[392,128]{1,0:T(8,128)}, f32[392,128]{1,0:T(8,128)S(1)}, u32[]{:S(2)}, u32[]{:S(2)}) collective-permute-start(f32[392,128]{1,0:T(8,128)} %get-tuple-element.22), channel_id=1, source_target_pairs={{0,1},{1,2},{2,3},{3,0},{4,5},{5,6},{6,7},{7,4},{8,9},{9,10},{10,1... | collective-permute-start | bytes 602120 | tf_op jit(solution)/shard_map/ppermute | solution.py:325
  78.1 9.0 %collective-permute-start.8 = (f32[392,128]{1,0:T(8,128)}, f32[392,128]{1,0:T(8,128)S(1)}, u32[]{:S(2)}, u32[]{:S(2)}) collective-permute-start(f32[392,128]{1,0:T(8,128)} %get-tuple-element.23), channel_id=1, source_target_pairs={{0,2},{1,3},{2,0},{3,1},{4,6},{5,7},{6,4},{7,5},{8,10},{9,11},{10,... | collective-permute-start | bytes 602120 | tf_op jit(solution)/shard_map/ppermute | solution.py:325
  81.1 10.8 %collective-permute-start.9 = (f32[392,128]{1,0:T(8,128)}, f32[392,128]{1,0:T(8,128)S(1)}, u32[]{:S(2)}, u32[]{:S(2)}) collective-permute-start(f32[392,128]{1,0:T(8,128)} %get-tuple-element.24), channel_id=1, source_target_pairs={{0,3},{1,0},{2,1},{3,2},{4,7},{5,4},{6,5},{7,6},{8,11},{9,8},{10,9... | collective-permute-start | bytes 602120 | tf_op jit(solution)/shard_map/ppermute | solution.py:325
  81.1 10.8 %collective-permute-start.10 = (f32[392,128]{1,0:T(8,128)}, f32[392,128]{1,0:T(8,128)S(1)}, u32[]{:S(2)}, u32[]{:S(2)}) collective-permute-start(f32[392,128]{1,0:T(8,128)} %get-tuple-element.25), channel_id=1, source_target_pairs={{1,0},{2,1},{3,2},{4,3},{5,4},{6,5},{7,6},{8,7},{9,8},{10,9},{11,1... | collective-permute-start | bytes 602120 | tf_op jit(solution)/shard_map/ppermute | solution.py:325
  82.4 10.2 %collective-permute-start.11 = (f32[392,128]{1,0:T(8,128)}, f32[392,128]{1,0:T(8,128)S(1)}, u32[]{:S(2)}, u32[]{:S(2)}) collective-permute-start(f32[392,128]{1,0:T(8,128)} %get-tuple-element.26), channel_id=1, source_target_pairs={{1,1},{2,2},{3,3},{4,0},{5,5},{6,6},{7,7},{8,4},{9,9},{10,10},{11,... | collective-permute-start | bytes 602120 | tf_op jit(solution)/shard_map/ppermute | solution.py:325
  85.8 9.4 %collective-permute-start.12 = (f32[392,128]{1,0:T(8,128)}, f32[392,128]{1,0:T(8,128)S(1)}, u32[]{:S(2)}, u32[]{:S(2)}) collective-permute-start(f32[392,128]{1,0:T(8,128)} %get-tuple-element.27), channel_id=1, source_target_pairs={{1,2},{2,3},{3,0},{4,1},{5,6},{6,7},{7,4},{8,5},{9,10},{10,11},{11... | collective-permute-start | bytes 602120 | tf_op jit(solution)/shard_map/ppermute | solution.py:325
  87.1 12.1 %collective-permute-start.13 = (f32[392,128]{1,0:T(8,128)}, f32[392,128]{1,0:T(8,128)S(1)}, u32[]{:S(2)}, u32[]{:S(2)}) collective-permute-start(f32[392,128]{1,0:T(8,128)} %get-tuple-element.28), channel_id=1, source_target_pairs={{1,3},{2,0},{3,1},{4,2},{5,7},{6,4},{7,5},{8,6},{9,11},{10,8},{11,... | collective-permute-start | bytes 602120 | tf_op jit(solution)/shard_map/ppermute | solution.py:325
  99.1 0.9 copy-start

commit v2 on v0

v2 whole, which is shorter than its diff:
```python
import jax
import jax.numpy as jnp
from jax import lax
from jax.experimental import pallas as pl
from jax.experimental.pallas import tpu as pltpu
from jax.sharding import PartitionSpec as P

B = 64
K = 6
G = 4
R = 32
H = 8
T = 32
TH = T * H
QUAD = 4
UNROLL = 4
AXES = ("row", "col")
RELAX = 2.0 / 3.0
F32 = jnp.float32
BF16 = jnp.bfloat16
I32 = jnp.int32
MB = 1024 * 1024


def most_batches(rows, columns, ranges):
    return (rows * K + (QUAD - 1) * columns) // QUAD + ranges * (UNROLL - 1) + 1


def split(x):
    hi = x.astype(BF16)
    return hi, (x - hi.astype(F32)).astype(BF16)


def lanes_of(shape):
    return lax.broadcasted_iota(I32, shape, 1)


def raw_block(ref, base, row):
    return ref[pl.ds(base + row, T, stride=H), :]


def doubled(x):
    low = lanes_of((T, 128)) < 64
    other = pltpu.roll(x, 64, 1)
    return jnp.where(low, x, other), jnp.where(low, other, x)


def stacked(x):
    return jnp.concatenate(doubled(x), axis=0)


def right_of(table):
    return jnp.concatenate([table[:64], table[:64], table[64:], table[64:]], axis=0)


def wide(left):
    return jnp.concatenate([left, left], axis=1)


def load_tentative(ref, base, row, tn, tb, slot):
    even, odd = doubled(raw_block(ref, base, row))
    spot = slot & 7
    tn[spot, pl.ds(0, T, stride=2), :] = even
    tn[spot, pl.ds(1, T, stride=2), :] = odd
    hi, lo = split(tn[spot])
    tb[slot] = jnp.concatenate([hi, lo], axis=0)


def prolong(e, a_ref, base_of, row, start, pf, tb, entries, keep):
    row_of = lax.broadcasted_iota(I32, (64, 128), 0)
    row_of = jnp.where(row_of < T, 2 * row_of, 2 * row_of - 63)
    lane_of = lanes_of((64, 128))
    scale = None
    for k in range(K):
        x = stacked(raw_block(a_ref, base_of(k), row))
        rounded = x.astype(BF16).astype(F32)
        left = jnp.where(lane_of < 64, rounded, x - rounded).astype(BF16)
        keep(k, left)
        j, slot = entries(k)
        product = jnp.dot(wide(left), right_of(tb[j]), preferred_element_type=F32)
        if k == 0:
            diagonal = jnp.sum(jnp.where(row_of == lane_of, x, 0.0), axis=1, keepdims=True)
            scale = -RELAX / jnp.where(diagonal == 0.0, 1.0, diagonal)
            for pair in range(4):
                pf[e, pair] = jnp.zeros((64, 128), F32)
            value = product * scale + start
        else:
            value = product * scale
        pf[e, slot >> 1] += jnp.where(lane_of // 64 == (slot & 1), value, 0.0)


def as_right(value, nat, spot, w, e, pair):
    nat[spot, pl.ds(0, T, stride=2), :] = value[:T]
    nat[spot, pl.ds(1, T, stride=2), :] = value[T:]
    hi, lo = split(nat[spot])
    w[e, 0:64, pair * 128 : pair * 128 + 128] = hi
    w[e, 64:128, pair * 128 : pair * 128 + 128] = lo


def as_left(first, second, pt_hi, pt_lo, pair, where):
    hi, lo = split(jnp.concatenate([first, second], axis=0).T)
    pt_hi[pair * 128 : pair * 128 + 128, where] = hi
    pt_lo[pair * 128 : pair * 128 + 128, where] = lo


def place_range(counts, starts, order, batch_source, first, last, begin, dummy):
    def one(source, at):
        starts[source] = at
        after = at + ((counts[source] + QUAD - 1) >> 2)
        for q in range(QUAD):
            order[jnp.maximum(after * QUAD - QUAD, 0) + q] = dummy
        return after

    after = lax.fori_loop(first, last, one, begin)
    for q in range(QUAD * (UNROLL - 1)):
        order[after * QUAD + q] = dummy
    for q in range(UNROLL - 1):
        batch_source[after + q] = first
    return (after + UNROLL - 1) // UNROLL * UNROLL


def fill_order(starts, order, batch_source, rank, pair):
    source = rank >> 9
    spot = starts[source] * QUAD + (rank & 511)
    order[spot] = pair
    batch_source[spot >> 2] = source


def apply_range(order, batch_source, begin, end, lhs, w, w_from, ap, row_from, own, side):
    width = 256 if side is None else 512

    def step(i, carry):
        for u in range(UNROLL):
            b = i * UNROLL + u
            pairs = [order[b * QUAD + q] for q in range(QUAD)]
            left = wide(jnp.concatenate([lhs[pair] for pair in pairs], axis=0))
            right = right_of(w[batch_source[b] - w_from, :, :width])
            product = jnp.dot(left, right, preferred_element_type=F32)
            for q, pair in enumerate(pairs):
                e = row_from(pair >> 3)
                ap[e, own] += product[q * 64 : q * 64 + 64, :256]
                if side is not None:
                    ap[e, side] += product[q * 64 : q * 64 + 64, 256:]
        return carry

    lax.fori_loop(begin // UNROLL, end // UNROLL, step, 0)


def product3(left, right):
    (left_hi, left_lo), (right_hi, right_lo) = left, right
    return (
        jnp.dot(left_hi, right_hi, preferred_element_type=F32)
        + jnp.dot(left_hi, right_lo, preferred_element_type=F32)
        + jnp.dot(left_lo, right_hi, preferred_element_type=F32)
    )


def give(out, part, s, col, ncol, ints, mark):
    chosen = jnp.int32(0)
    place = jnp.int32(-1)
    for g in range(G):
        spot = ints[1, g].astype(I32)
        hit = lax.rem(lax.rem(spot >> 2, ncol) - col + ncol, ncol) == s
        chosen = jnp.where(hit, g, chosen)
        place = jnp.where(hit, spot & 3, place)
    low = lanes_of((T, 128)) < 64
    for pair in range(6):
        even = part[pair, pl.ds(chosen * 64, T, stride=2), :]
        odd = part[pair, pl.ds(chosen * 64 + 1, T, stride=2), :]
        first = jnp.where(low, even, pltpu.roll(odd, 64, 1))
        second = jnp.where(low, pltpu.roll(even, 64, 1), odd)
        out[2 * pair * T : (2 * pair + 1) * T, :] = first
        out[(2 * pair + 1) * T : (2 * pair + 2) * T, :] = second
    if mark:
        out[3 * G * T : 3 * G * T + 8, :] = jnp.full((8, 128), place.astype(F32))


def early_kernel(mine, a_own, t_own, small_up, small_down, *refs, ncol):
    ups, refs = refs[:ncol], refs[ncol:]
    part_out, ap_out, lhs_out, w_out, pt_hi_out, pt_lo_out = refs[:6]
    a_rows, tn, tb, lhs, pf, nat, w, pt_hi_u, pt_lo_u, pt_hi, pt_lo, ap, ap_hi, ap_lo = refs[6:20]
    part_own, part_up = refs[20:22]
    low_ints, high_ints, slots, counts, starts, ranks, order, batch_source, sems = refs[22:]
    copies = [
        pltpu.make_async_copy(a_own, a_rows, sems.at[2]),
        pltpu.make_async_copy(small_up.at[pl.ds(TH, 8)], low_ints, sems.at[0]),
        pltpu.make_async_copy(small_down.at[pl.ds(TH, 8)], high_ints, sems.at[1]),
    ]
    for copy in copies:
        copy.start()

    def t_rows(i, carry):
        load_tentative(t_own, (i // H) * TH, lax.rem(i, H), tn, tb, H + i)
        return carry

    def t_ends(i, carry):
        load_tentative(small_up, 0, i, tn, tb, i)
        load_tentative(small_down, 0, i, tn, tb, R + H + i)
        return carry

    lax.fori_loop(0, R, t_rows, 0, unroll=4)
    lax.fori_loop(0, H, t_ends, 0, unroll=2)
    for copy in copies:
        copy.wait()
    device = mine[1, G].astype(I32)
    col = lax.rem(device, ncol)
    origin = device * R - H
    for i in range(H):
        slots[i] = low_ints[0, R - H + i].astype(I32) + G
        slots[H + R + i] = high_ints[0, i].astype(I32) + G
    for i in range(R):
        slots[H + i] = mine[0, i].astype(I32)
    for i in range(R + 1):
        counts[i] = 0

    lhs[R * 8] = jnp.zeros((64, 128), BF16)

    def prolong_rows(i, carry):
        group = i // H
        row = lax.rem(i, H)

        def entries(k):
            j = mine[2 + k, i].astype(I32) - origin
            source = jnp.where((j >= H) & (j < R + H), j - H, R)
            seen = counts[source]
            counts[source] = seen + 1
            ranks[i * 8 + k] = source * 512 + seen
            return j, slots[j]

        def keep(k, left):
            lhs[i * 8 + k] = left

        start = stacked(raw_block(t_own, group * TH, row))
        prolong(
            i, a_rows, lambda k: (k * (R // H) + group) * TH, row, start, pf, tb, entries, keep
        )
        return carry

    lax.fori_loop(0, R, prolong_rows, 0, unroll=4)

    place = lambda first, last, begin: place_range(
        counts, starts, order, batch_source, first, last, begin, R * 8
    )
    first_end = place(0, H, jnp.int32(0))
    second_end = place(H, R - H, first_end)
    third_end = place(R - H, R, second_end)
    starts[R] = MOST_EARLY

    for third in range(3):
        ap[R, third] = jnp.zeros((64, 256), F32)

    def arrange(i, carry, pairs, w_ref, pt_refs, first):
        for e in (2 * i, 2 * i + 1):
            for pair in range(pairs):
                as_right(pf[e, pair], nat, (e & 1) * 4 + pair, w_ref, e, pair)
            for third in range(3):
                ap[e, third] = jnp.zeros((64, 256), F32)
            for k in range(K):
                fill_order(starts, order, batch_source, ranks[e * 8 + k], e * 8 + k)
        where = pl.ds(pl.multiple_of((i - first // 2) * 128, 128), 128)
        for pair in range(pairs):
            as_left(pf[2 * i, pair], pf[2 * i + 1, pair], *pt_refs, pair, where)
        return carry

    inner = (pt_hi, pt_lo)
    lax.fori_loop(0, H // 2, lambda i, c: arrange(i, c, 4, w, (pt_hi_u, pt_lo_u), 0), 0)
    lax.fori_loop(H // 2, (R - H) // 2, lambda i, c: arrange(i, c, 2, w, inner, H), 0)
    lax.fori_loop((R - H) // 2, R // 2, lambda i, c: arrange(i, c, 4, w, inner, H), 0)

    saved = [
        pltpu.make_async_copy(lhs.at[pl.ds(0, H * 8)], lhs_out, sems.at[3]),
        pltpu.make_async_copy(w.at[pl.ds(0, H)], w_out, sems.at[4]),
        pltpu.make_async_copy(pt_hi_u, pt_hi_out, sems.at[5]),
        pltpu.make_async_copy(pt_lo_u, pt_lo_out, sems.at[6]),
    ]
    for copy in saved:
        copy.start()
    same = lambda e: e
    apply_range(order, batch_source, 0, first_end, lhs, w, 0, ap, same, 1, 0)
    apply_range(order, batch_source, first_end, second_end, lhs, w, 0, ap, same, 1, None)
    apply_range(order, batch_source, second_end, third_end, lhs, w, 0, ap, same, 1, 2)

    saved.append(pltpu.make_async_copy(ap.at[pl.ds(0, H)], ap_out, sems.at[7]))
    saved[-1].start()

    def split_ap(e, carry):
        where = pl.ds(pl.multiple_of((e - H) * 64, 64), 64)
        for third in range(3):
            hi, lo = split(ap[e, third])
            ap_hi[where, third * 256 : third * 256 + 256] = hi
            ap_lo[where, third * 256 : third * 256 + 256] = lo
        return carry

    lax.fori_loop(H, R, split_ap, 0, unroll=2)

    last = slice((R - 2 * H) * 64, (R - H) * 64)
    up = product3(
        (pt_hi[256:512, last], pt_lo[256:512, last]), (ap_hi[last, :], ap_lo[last, :])
    )
    for pair in range(6):
        part_up[pair] = up[:, pair * 128 : pair * 128 + 128]
    for s in range(ncol):
        give(ups[s], part_up, s, col, ncol, high_ints, False)
    own = product3((pt_hi[0:256, :], pt_lo[0:256, :]), (ap_hi[...], ap_lo[...]))
    for pair in range(6):
        part_own[pair] = own[:, pair * 128 : pair * 128 + 128]
    saved.append(pltpu.make_async_copy(part_own, part_out, sems.at[8]))
    saved[-1].start()
    for copy in saved:
        copy.wait()


def late_kernel(mine, small_up, t_first, big, *refs, ncol):
    part_in, ap_in, lhs_in, w_in, pt_hi_in, pt_lo_in = refs[:6]
    owns, downs, refs = refs[6 : 6 + ncol], refs[6 + ncol : 6 + 2 * ncol], refs[6 + 2 * ncol :]
    tn, tb, lhs, pf, nat, w, pt_hi, pt_lo, ap, ap_hi, ap_lo, part_down, part_full = refs[:13]
    t_low, a_low, part_own, ap_u, lhs_u, w_u, pt_hi_u, pt_lo_u = refs[13:21]
    low_ints, slots, counts, starts, ranks, order, batch_source, sems = refs[21:]
    copies = [
        pltpu.make_async_copy(big.at[pl.ds(K * TH, (R - H) * T)], t_low, sems.at[0]),
        pltpu.make_async_copy(small_up.at[pl.ds(TH, 8)], low_ints, sems.at[1]),
        pltpu.make_async_copy(big.at[pl.ds(0, K * TH)], a_low, sems.at[2]),
        pltpu.make_async_copy(lhs_in, lhs_u.at[pl.ds(0, H * 8)], sems.at[3]),
        pltpu.make_async_copy(w_in, w_u, sems.at[4]),
        pltpu.make_async_copy(ap_in, ap_u, sems.at[5]),
        pltpu.make_async_copy(pt_hi_in, pt_hi_u, sems.at[6]),
        pltpu.make_async_copy(pt_lo_in, pt_lo_u, sems.at[7]),
        pltpu.make_async_copy(part_in, part_own, sems.at[8]),
    ]
    for copy in copies:
        copy.start()

    def t_rows(i, carry):
        load_tentative(t_low, (i // H) * TH, lax.rem(i, H), tn, tb, i)
        return carry

    def t_ends(i, carry):
        load_tentative(small_up, 0, i, tn, tb, R - H + i)
        load_tentative(t_first, 0, i, tn, tb, R + i)
        return carry

    lax.fori_loop(0, H, t_ends, 0, unroll=2)
    copies[0].wait()
    lax.fori_loop(0, R - H, t_rows, 0, unroll=4)
    copies[1].wait()
    copies[2].wait()
    device = mine[1, G].astype(I32)
    col = lax.rem(device, ncol)
    origin = (device - 1) * R
    for i in range(R):
        slots[i] = low_ints[0, i].astype(I32) + G
    for i in range(H):
        slots[R + i] = mine[0, i].astype(I32)
    for i in range(2 * H + 1):
        counts[i] = 0

    def rank(valid, j, at):
        source = jnp.where(valid, j - (R - H), 2 * H)
        seen = counts[source]
        counts[source] = seen + 1
        ranks[at] = source * 512 + seen

    def prolong_rows(i, carry):
        def entries(k):
            j = low_ints[2 + k, R - H + i].astype(I32) - origin
            rank(j >= R, j, i * 8 + k)
            return j, slots[j]

        def keep(k, left):
            lhs[i * 8 + k] = left

        for k in range(K):
            j = mine[2 + k, i].astype(I32) - origin
            rank(j < R, j, (H + i) * 8 + k)
        start = stacked(raw_block(small_up, 0, i))
        prolong(i, a_low, lambda k: k * TH, i, start, pf, tb, entries, keep)
        return carry

    lax.fori_loop(0, H, prolong_rows, 0, unroll=4)

    place = lambda first, last, begin: place_range(
        counts, starts, order, batch_source, first, last, begin, H * 8
    )
    first_end = place(0, H, jnp.int32(0))
    second_end = place(H, 2 * H, first_end)
    starts[2 * H] = MOST_LATE
    lhs[H * 8] = jnp.zeros((64, 128), BF16)
    for copy in copies[3:]:
        copy.wait()
    lhs_u[H * 8] = jnp.zeros((64, 128), BF16)
    for side in range(2):
        ap[2 * H, side] = jnp.zeros((64, 256), F32)

    def arrange(i, carry):
        for e in (2 * i, 2 * i + 1):
            for pair in range(4):
                as_right(pf[e, pair], nat, (e & 1) * 4 + pair, w, e, pair)
            for side in range(2):
                ap[e, side] = jnp.zeros((64, 256), F32)
                ap[H + e, side] = ap_u[e, side]
            for k in range(K):
                fill_order(starts, order, batch_source, ranks[e * 8 + k], e * 8 + k)
                fill_order(starts, order, batch_source, ranks[(H + e) * 8 + k], e * 8 + k)
        where = pl.ds(pl.multiple_of(i * 128, 128), 128)
        for pair in range(4):
            as_left(pf[2 * i, pair], pf[2 * i + 1, pair], pt_hi, pt_lo, pair, where)
        return carry

    lax.fori_loop(0, H // 2, arrange, 0)

    apply_range(
        order, batch_source, 0, first_end, lhs_u, w, 0, ap, lambda e: e + H, 1, 0
    )
    apply_range(
        order,
        batch_source,
        first_end,
        second_end,
        lhs,
        w_u,
        H,
        ap,
        lambda e: jnp.where(e == H, 2 * H, e),
        1,
        0,
    )

    def split_ap(e, carry):
        where = pl.ds(pl.multiple_of(e * 64, 64), 64)
        for side in range(2):
            hi, lo = split(ap[e, side])
            ap_hi[where, side * 256 : side * 256 + 256] = hi
            ap_lo[where, side * 256 : side * 256 + 256] = lo
        return carry

    lax.fori_loop(0, 2 * H, split_ap, 0, unroll=2)

    def split_third(e, carry):
        where = pl.ds(pl.multiple_of((H + e) * 64, 64), 64)
        hi, lo = split(ap_u[e, 2])
        ap_hi[where, 512:768] = hi
        ap_lo[where, 512:768] = lo
        return carry

    lax.fori_loop(0, H, split_third, 0, unroll=2)

    lows, highs = slice(0, H * 64), slice(H * 64, 2 * H * 64)

    def coarse(rows):
        high = product3((pt_hi_u[rows, :], pt_lo_u[rows, :]), (ap_hi[highs, :], ap_lo[highs, :]))
        low = product3((pt_hi[rows, :], pt_lo[rows, :]), (ap_hi[lows, :512], ap_lo[lows, :512]))
        return [
            high[:, pair * 128 : pair * 128 + 128]
            + (low[:, pair * 128 : pair * 128 + 128] if pair < 4 else 0.0)
            for pair in range(6)
        ]

    for pair, value in enumerate(coarse(slice(256, 512))):
        part_down[pair] = value
    for s in range(ncol):
        give(downs[s], part_down, s, col, ncol, low_ints, False)
    for pair, value in enumerate(coarse(slice(0, 256))):
        part_full[pair] = value + part_own[pair]
    for s in range(ncol):
        give(owns[s], part_full, s, col, ncol, mine, True)


MOST_EARLY = most_batches(R, R, 3)
MOST_LATE = most_batches(2 * H, 2 * H, 2)


def combine_kernel(mine, *refs, ncol):
    ups, owns, downs = refs[:ncol], refs[ncol : 2 * ncol], refs[2 * ncol : 3 * ncol]
    cross_up, cross_down, out, total = refs[3 * ncol :]
    col = lax.rem(mine[1, G].astype(I32), ncol)
    span = G * T
    for s in range(ncol):
        home = lax.rem(col - s + ncol, ncol)
        total[s, 0 : 4 * span] = jnp.zeros((4 * span, 128), F32)
        total[s, 4 * span : 5 * span] = jnp.zeros((span, 128), F32)
        total[s, span : 4 * span] = owns[s][0 : 3 * span]

        @pl.when(home > 0)
        def _():
            total[s, 0 : 3 * span] += ups[(s + 1) % ncol][...]

        @pl.when(home == 0)
        def _():
            total[s, 0 : 3 * span] += cross_up[...]

        @pl.when(home < ncol - 1)
        def _():
            total[s, 2 * span : 5 * span] += downs[(s - 1) % ncol][...]

        @pl.when(home == ncol - 1)
        def _():
            total[s, 2 * span : 5 * span] += cross_down[...]

    for j in range(G):
        for c in range(5):
            value = jnp.zeros((span, 128), F32)
            for s in range(ncol):
                mark = owns[s][3 * span : 3 * span + 1, :] == float(j)
                value = jnp.where(mark, total[s, c * span : (c + 1) * span], value)
            out[pl.ds(c * span * G + j, span, stride=G), :] = value


def local(a_blocks, columns, tentative, aggregate, owner, *, nrow, ncol):
    count = nrow * ncol
    device = lax.axis_index(AXES).astype(I32)
    col = lax.axis_index("col")
    up = [(d, d + 1) for d in range(count - 1)]
    down = [(d + 1, d) for d in range(count - 1)]

    def lying(blocks):
        shape = blocks.shape
        inner = blocks.reshape(*shape[:-2], shape[-2] // H, H, T, 128)
        return inner.swapaxes(-3, -2).reshape(-1, 128)

    a_own = lying(a_blocks.transpose(1, 0, 2))
    a_last = lying(a_blocks[R - H :].transpose(1, 0, 2))
    t_own = lying(tentative)
    last, first = t_own[(R - H) * T :], t_own[:TH]
    meta = jnp.concatenate(
        [
            jnp.pad(aggregate.reshape(1, R), ((0, 0), (0, 128 - R))),
            jnp.pad(
                jnp.concatenate([owner, device.reshape(1)]).reshape(1, G + 1),
                ((0, 0), (0, 128 - G - 1)),
            ),
            jnp.pad(columns.T, ((0, 0), (0, 128 - R))),
        ],
        axis=0,
    ).astype(F32)
    small_up = lax.ppermute(jnp.concatenate([last, meta], axis=0), AXES, up)
    small_down = lax.ppermute(jnp.concatenate([first, meta], axis=0), AXES, down)
    big = jnp.concatenate([a_last, t_own[: (R - H) * T]], axis=0)
    big, small_up, small_down = lax.optimization_barrier((big, small_up, small_down))
    big = lax.ppermute(big, AXES, up)

    span = 3 * G * T
    plain = jax.ShapeDtypeStruct((span, 128), F32)
    marked = jax.ShapeDtypeStruct((span + 8, 128), F32)
    vmem = pl.BlockSpec(memory_space=pltpu.VMEM)
    smem = pl.BlockSpec(memory_space=pltpu.SMEM)
    hbm = pl.BlockSpec(memory_space=pltpu.HBM)
    state_shapes = [
        pltpu.HBM((6, 256, 128), F32),
        pltpu.HBM((H, 3, 64, 256), F32),
        pltpu.HBM((H * 8, 64, 128), BF16),
        pltpu.HBM((H, 128, 512), BF16),
        pltpu.HBM((512, H * 64), BF16),
        pltpu.HBM((512, H * 64), BF16),
    ]
    outs = pl.pallas_call(
        lambda *refs: early_kernel(*refs, ncol=ncol),
        out_shape=[plain] * ncol + state_shapes,
        in_specs=[smem, hbm] + [vmem] * 3,
        out_specs=[vmem] * ncol + [hbm] * len(state_shapes),
        scratch_shapes=[
            pltpu.VMEM((K * R * T, 128), F32),
            pltpu.VMEM((8, 64, 128), F32),
            pltpu.VMEM((R + 2 * H, 128, 128), BF16),
            pltpu.VMEM((R * 8 + 1, 64, 128), BF16),
            pltpu.VMEM((R, 4, 64, 128), F32),
            pltpu.VMEM((8, 64, 128), F32),
            pltpu.VMEM((R, 128, 512), BF16),
            pltpu.VMEM((512, H * 64), BF16),
            pltpu.VMEM((512, H * 64), BF16),
            pltpu.VMEM((512, (R - H) * 64), BF16),
            pltpu.VMEM((512, (R - H) * 64), BF16),
            pltpu.VMEM((R + 1, 3, 64, 256), F32),
            pltpu.VMEM(((R - H) * 64, 768), BF16),
            pltpu.VMEM(((R - H) * 64, 768), BF16),
            pltpu.VMEM((6, 256, 128), F32),
            pltpu.VMEM((6, 256, 128), F32),
            pltpu.SMEM((8, 128), F32),
            pltpu.SMEM((8, 128), F32),
            pltpu.SMEM((R + 2 * H,), I32),
            pltpu.SMEM((R + 1,), I32),
            pltpu.SMEM((R + 1,), I32),
            pltpu.SMEM((R * 8,), I32),
            pltpu.SMEM((MOST_EARLY * QUAD + R * K,), I32),
            pltpu.SMEM((MOST_EARLY + R * K // QUAD,), I32),
            pltpu.SemaphoreType.DMA((9,)),
        ],
        compiler_params=pltpu.CompilerParams(vmem_limit_bytes=44 * MB),
    )(meta, a_own, t_own, small_up, small_down)
    ups, state = outs[:ncol], [pltpu.with_memory_space_constraint(x, pltpu.HBM) for x in outs[ncol:]]

    def rotated(blocks):
        moved = [blocks[0]]
        for s in range(1, ncol):
            route = [(c, (c + s) % ncol) for c in range(ncol)]
            moved.append(lax.ppermute(blocks[s], "col", route))
        return moved

    def chosen(blocks, index):
        value = blocks[0]
        for s in range(1, ncol):
            value = jnp.where(index == s, blocks[s], value)
        return value

    ups = rotated(ups)
    outs = pl.pallas_call(
        lambda *refs: late_kernel(*refs, ncol=ncol),
        out_shape=[marked] * ncol + [plain] * ncol,
        in_specs=[smem, vmem, vmem, hbm] + [hbm] * len(state_shapes),
        out_specs=[vmem] * (2 * ncol),
        scratch_shapes=[
            pltpu.VMEM((8, 64, 128), F32),
            pltpu.VMEM((R + H, 128, 128), BF16),
            pltpu.VMEM((H * 8 + 1, 64, 128), BF16),
            pltpu.VMEM((H, 4, 64, 128), F32),
            pltpu.VMEM((8, 64, 128), F32),
            pltpu.VMEM((H, 128, 512), BF16),
            pltpu.VMEM((512, H * 64), BF16),
            pltpu.VMEM((512, H * 64), BF16),
            pltpu.VMEM((2 * H + 1, 2, 64, 256), F32),
            pltpu.VMEM((2 * H * 64, 768), BF16),
            pltpu.VMEM((2 * H * 64, 768), BF16),
            pltpu.VMEM((6, 256, 128), F32),
            pltpu.VMEM((6, 256, 128), F32),
            pltpu.VMEM(((R - H) * T, 128), F32),
            pltpu.VMEM((K * TH, 128), F32),
            pltpu.VMEM((6, 256, 128), F32),
            pltpu.VMEM((H, 3, 64, 256), F32),
            pltpu.VMEM((H * 8 + 1, 64, 128), BF16),
            pltpu.VMEM((H, 128, 512), BF16),
            pltpu.VMEM((512, H * 64), BF16),
            pltpu.VMEM((512, H * 64), BF16),
            pltpu.SMEM((8, 128), F32),
            pltpu.SMEM((R + H,), I32),
            pltpu.SMEM((2 * H + 1,), I32),
            pltpu.SMEM((2 * H + 1,), I32),
            pltpu.SMEM((2 * H * 8,), I32),
            pltpu.SMEM((MOST_LATE * QUAD + 2 * H * K,), I32),
            pltpu.SMEM((MOST_LATE + 2 * H * K // QUAD,), I32),
            pltpu.SemaphoreType.DMA((9,)),
        ],
        compiler_params=pltpu.CompilerParams(vmem_limit_bytes=26 * MB),
    )(meta, small_up, first, big, *state)
    owns, downs = outs[:ncol], outs[ncol:]
    downs = rotated(downs)
    owns = rotated(owns)
    cross_up = lax.ppermute(
        chosen(ups, lax.rem(col + 1, ncol)), "row", [(r, r + 1) for r in range(nrow - 1)]
    )
    cross_down = lax.ppermute(
        chosen(downs, col), "row", [(r + 1, r) for r in range(nrow - 1)]
    )
    result = pl.pallas_call(
        lambda *refs: combine_kernel(*refs, ncol=ncol),
        out_shape=jax.ShapeDtypeStruct((5 * G * T * G, 128), F32),
        in_specs=[smem] + [vmem] * (3 * ncol + 2),
        out_specs=vmem,
        scratch_shapes=[pltpu.VMEM((ncol, 5 * G * T, 128), F32)],
        compiler_params=pltpu.CompilerParams(vmem_limit_bytes=16 * MB),
    )(meta, *ups, *owns, *downs, cross_up, cross_down)
    return result.reshape(5 * G, T, G, 128).transpose(2, 0, 1, 3).reshape(G, 5 * G, T * 128)


def solution(mesh):
    placed = (
        P(AXES, None, None),
        P(AXES, None),
        P(AXES, None),
        P(AXES),
        P(AXES),
    )
    nrow, ncol = mesh.shape["row"], mesh.shape["col"]
    return jax.shard_map(
        lambda *args: local(*args, nrow=nrow, ncol=ncol),
        mesh=mesh,
        in_specs=placed,
        out_specs=P(AXES, None, None),
        check_vma=False,
    )
```

time: 723 us -> 72.7 us (0.10); the launches traced: 710 us -> 71.5 us
  local copies, waits for them, and re-layouts: 284 us -> 1.09 us
  matrix products: 227 us -> 0 us
  other arithmetic: 56.1 us -> 2.63 us
  waiting for transfers between devices: 52.2 us -> 12 us
  blocking collectives: 35.2 us -> 0 us
  Pallas kernels: 0 us -> 30.2 us
  between operations: 14.8 us -> 0.18 us
  loops' own time: 14.5 us -> 0 us
    dot_general x29 -> x0, matrix products: 227 us -> none  [the longest x20 103 us: apply_rows(): jnp.einsum('sqp,scpw->scqw', a_mats[:, stored], gathered[:, stored], prec...]
    gather x19 -> x0, local copies, waits for them, and re-layouts: 211 us -> none  [the longest x12 191 us: apply_rows(): jnp.take(ext_dense, index_group, axis=0).reshape(count, K, 3 * G, B, BC)]
    select_n x9 -> x2, other arithmetic: 55.2 us -> 0.09 us  [chosen(): value = jnp.where(index == s, blocks[s], value)]
    all_gather x1 -> x0, waiting for transfers between devices: 43.1 us -> none  [local(): lax.all_gather(coarse_rows, 'col', axis=0, tiled=True)]
    unnamed x1 -> x0, blocking collectives: 35.2 us -> none
    reshape x9 -> x0, local copies, waits for them, and re-layouts: 31.8 us -> none  [the longest x2 13.6 us: prolong_rows(): return (smooth.reshape(row_count, K, B * BC), labels)]
    pallas_call x0 -> x3, Pallas kernels: none -> 30.2 us  [the longest x1 19.2 us: local(): pl.pallas_call(lambda *refs: early_kernel(*refs, ncol=ncol), out_shape=[p...]
    another operation x1 -> x0, loops' own time: 14.5 us -> none  [local(): lax.map(apply_group, (a_blocks.reshape(group_count, 8, K, B * B), local_i...]
  transfers between devices with their start and end apart: 11 -> 14, of which waited for: 4 -> 5; matrix products, arithmetic and copies ran while one was open for 7% -> 2% of each run, Pallas kernels for 0% -> 39%
where the time goes in v2:
time: 72.7 us; the launch traced here: 71.5 us
  Pallas kernels  30.2 us (42%)
  starting transfers between devices  25.3 us (35%)
  waiting for transfers between devices  12 us (17%)
  other arithmetic  2.63 us (4%)
  local copies, waits for them, and re-layouts  1.09 us (1%)
    pallas_call x1, Pallas kernels, local(): pl.pallas_call(lambda *refs: early_kernel(*refs, ncol=ncol), out_shape=[p...  19.2 us
    ppermute x9, starting transfers between devices, rotated(): moved.append(lax.ppermute(blocks[s], 'col', route))  9.79 us
    pallas_call x1, Pallas kernels, local(): pl.pallas_call(lambda *refs: late_kernel(*refs, ncol=ncol), out_shape=[ma...  8.79 us
    ppermute x9, waiting for transfers between devices, rotated(): moved.append(lax.ppermute(blocks[s], 'col', route))  5.95 us
    ppermute x1, starting transfers between devices, local(): big = lax.ppermute(big, AXES, up)  5.55 us
    ppermute x1, starting transfers between devices, local(): lax.ppermute(chosen(ups, lax.rem(col + 1, ncol)), 'row', [(r, r + 1) for...  4.9 us
    ppermute x1, waiting for transfers between devices, local(): lax.ppermute(chosen(downs, col), 'row', [(r + 1, r) for r in range(nrow -...  3.17 us
    ppermute x1, waiting for transfers between devices, local(): lax.ppermute(jnp.concatenate([first, meta], axis=0), AXES, down)  2.91 us
  transfers between devices with their start and end apart: 14, of which 5 were waited for; matrix products, arithmetic and copies ran while one was open for 2% of the time, Pallas kernels for 39%

profile of v2, /device:TPU:0, one launch (start us, length us, event | category | flops | bytes accessed | tf_op | source)
XLA Modules:
  0.0 71.5 jit_solution(9874411282518911973)
XLA Ops:
  0.0 1.0 %slice_bitcast_fusion = (f32[256,128]{1,0:T(8,128)S(1)}, f32[256,128]{1,0:T(8,128)S(1)}) fusion(f32[4,32,8,128]{3,2,1,0:T(8,128)} %bitcast.36), kind=kLoop, calls=%fused_computation.5 | loop fusion | bytes 524288 | tf_op jit(solution)/shard_map/slice | solution.py:523
  1.1 0.7 %add_bitcast_fusion = s32[1,5]{1,0:T(1,128)S(1)} fusion(s32[1]{0:T(128)} %bitcast.1, s32[4]{0:T(128)} %param.9), kind=kLoop, calls=%fused_computation.10 | loop fusion | flops 5 | bytes 40 | tf_op jit(solution)/shard_map/reshape | solution.py:528
  1.8 0.7 fusion.refs_0_
  2.5 2.4 %collective-permute-start = (f32[264,128]{1,0:T(8,128)S(1)}, f32[264,128]{1,0:T(8,128)S(1)}, u32[]{:S(2)}, u32[]{:S(2)}) collective-permute-start(f32[264,128]{1,0:T(8,128)S(1)} %get-tuple-element.50), channel_id=1, source_target_pairs={{0,1},{1,2},{2,3},{3,4},{4,5},{5,6},{6,7},{7,8},{8,9},{9,10},{10,1... | collective-permute-start | bytes 405512 | tf_op jit(solution)/shard_map/ppermute | solution.py:535
  4.9 1.4 %collective-permute-start.1 = (f32[264,128]{1,0:T(8,128)S(1)}, f32[264,128]{1,0:T(8,128)S(1)}, u32[]{:S(2)}, u32[]{:S(2)}) collective-permute-start(f32[264,128]{1,0:T(8,128)S(1)} %get-tuple-element.49), channel_id=1, source_target_pairs={{1,0},{2,1},{3,2},{4,3},{5,4},{6,5},{7,6},{8,7},{9,8},{10,9},{11,1... | collective-permute-start | bytes 405512 | tf_op jit(solution)/shard_map/ppermute | solution.py:536
  6.4 1.1 %pad_maximum_fusion = f32[2304,128]{1,0:T(8,128)} fusion(f32[768,128]{1,0:T(8,128)S(1)} %bitcast.39, f32[1536,128]{1,0:T(8,128)S(1)} %bitcast.35), kind=kLoop, calls=%fused_computation | loop fusion | flops 294912 | bytes 2359296 | tf_op jit(solution)/shard_map/concatenate | solution.py:537
  7.5 2.9 %collective-permute-done.1.refs_4_ = f32[264,128]{1,0:T(8,128)S(1)} collective-permute-done((f32[264,128]{1,0:T(8,128)S(1)}, f32[264,128]{1,0:T(8,128)S(1)}, u32[]{:S(2)}, u32[]{:S(2)}) %collective-permute-start.1) | collective-permute-done | bytes 135200 | tf_op jit(solution)/shard_map/ppermute | solution.py:536
  10.4 5.5 %collective-permute-start.5 = (f32[2304,128]{1,0:T(8,128)}, f32[2304,128]{1,0:T(8,128)S(1)}, u32[]{:S(2)}, u32[]{:S(2)}) collective-permute-start(f32[2304,128]{1,0:T(8,128)} %pad_maximum_fusion), channel_id=1, source_target_pairs={{0,1},{1,2},{2,3},{3,4},{4,5},{5,6},{6,7},{7,8},{8,9},{9,10},{10,1... | collective-permute-start | bytes 3538952 | tf_op jit(solution)/shard_map/ppermute | solution.py:539
  16.0 19.2 %shard_map.55 = (f32[384,128]{1,0:T(8,128)S(1)}, f32[384,128]{1,0:T(8,128)S(1)}, f32[384,128]{1,0:T(8,128)S(1)}, f32[384,128]{1,0:T(8,128)S(1)}, f32[6,256,128]{...) custom-call(f32[8,128]{1,0:T(8,128)S(1)} %fusion.refs_0_, ...), custom_call_target="tpu_custom_call" | custom-call | tf_op jit(solution)/shard_map/pallas_call | solution.py:555
  35.3 1.9 %collective-permute-start.3 = (f32[384,128]{1,0:T(8,128)S(1)}, f32[384,128]{1,0:T(8,128)S(1)}, u32[]{:S(2)}, u32[]{:S(2)}) collective-permute-start(f32[384,128]{1,0:T(8,128)S(1)} %get-tuple-element.30), channel_id=1, source_target_pairs={{0,2},{1,3},{2,0},{3,1},{4,6},{5,7},{6,4},{7,5},{8,10},{9,11},{10,... | collective-permute-start | bytes 589832 | tf_op jit(solution)/shard_map/ppermute | solution.py:595
  37.1 1.4 %collective-permute-start.4 = (f32[384,128]{1,0:T(8,128)S(1)}, f32[384,128]{1,0:T(8,128)S(1)}, u32[]{:S(2)}, u32[]{:S(2)}) collective-permute-start(f32[384,128]{1,0:T(8,128)S(1)} %get-tuple-element.31), channel_id=1, source_target_pairs={{0,3},{1,0},{2,1},{3,2},{4,7},{5,4},{6,5},{7,6},{8,11},{9,8},{10,9... | collective-permute-start | bytes 589832 | tf_op jit(solution)/shard_map/ppermute | solution.py:595
  38.5 8.8 %shard_map.56 = (f32[392,128]{1,0:T(8,128)S(1)}, f32[392,128]{1,0:T(8,128)S(1)}, f32[392,128]{1,0:T(8,128)S(1)}, f32[392,128]{1,0:T(8,128)S(1)}, f32[384,128]{1,...) custom-call(f32[8,128]{1,0:T(8,128)S(1)} %fusion.refs_0_, ...), custom_call_target="tpu_custom_call" | custom-call | tf_op jit(solution)/shard_map/pallas_call | solution.py:605
  47.3 0.1 collective-permute-start.9
  47.4 1.2 %collective-permute-start.10 = (f32[384,128]{1,0:T(8,128)S(1)}, f32[384,128]{1,0:T(8,128)S(1)}, u32[]{:S(2)}, u32[]{:S(2)}) collective-permute-start(f32[384,128]{1,0:T(8,128)S(1)} %get-tuple-element.45), channel_id=1, source_target_pairs={{0,2},{1,3},{2,0},{3,1},{4,6},{5,7},{6,4},{7,5},{8,10},{9,11},{10,... | collective-permute-start | bytes 589832 | tf_op jit(solution)/shard_map/ppermute | solution.py:595
  48.6 1.4 %collective-permute-start.11 = (f32[384,128]{1,0:T(8,128)S(1)}, f32[384,128]{1,0:T(8,128)S(1)}, u32[]{:S(2)}, u32[]{:S(2)}) collective-permute-start(f32[384,128]{1,0:T(8,128)S(1)} %get-tuple-element.46), channel_id=1, source_target_pairs={{0,3},{1,0},{2,1},{3,2},{4,7},{5,4},{6,5},{7,6},{8,11},{9,8},{10,9... | collective-permute-start | bytes 589832 | tf_op jit(solution)/shard_map/ppermute | solution.py:595
  50.1 4.9 %collective-permute-start.12 = (f32[384,128]{1,0:T(8,128)S(1)}, f32[384,128]{1,0:T(8,128)S(1)}, u32[]{:S(2)}, u32[]{:S(2)}) collective-permute-start(f32[384,128]{1,0:T(8,128)S(1)} %select_select_fusion.1), channel_id=1, source_target_pairs={{0,4},{4,8},{8,12},{12,16},{16,20},{20,24},{24,28},{1,5},{5,9},{9,... | collective-permute-start | bytes 589832 | tf_op jit(solution)/shard_map/ppermute | solution.py:646
  55.1 1.3 %collective-permute-start.7 = (f32[392,128]{1,0:T(8,128)S(1)}, f32[392,128]{1,0:T(8,128)S(1)}, u32[]{:S(2)}, u32[]{:S(2)}) collective-permute-start(f32[392,128]{1,0:T(8,128)S(1)} %get-tuple-element.41), channel_id=1, source_target_pairs={{0,2},{1,3},{2,0},{3,1},{4,6},{5,7},{6,4},{7,5},{8,10},{9,11},{10,... | collective-permute-start | bytes 602120 | tf_op jit(solution)/shard_map/ppermute | solution.py:595
  56.4 2.4 %collective-permute-start.8 = (f32[392,128]{1,0:T(8,128)S(1)}, f32[392,128]{1,0:T(8,128)S(1)}, u32[]{:S(2)}, u32[]{:S(2)}) collective-permute-start(f32[392,128]{1,0:T(8,128)S(1)} %get-tuple-element.42), channel_id=1, source_target_pairs={{0,3},{1,0},{2,1},{3,2},{4,7},{5,4},{6,5},{7,6},{8,11},{9,8},{10,9... | collective-permute-start | bytes 602120 | tf_op jit(solution)/shard_map/ppermute | solution.py:595
  58.9 1.3 %collective-permute-start.13 = (f32[384,128]{1,0:T(8,128)S(1)}, f32[384,128]{1,0:T(8,128)S(1)}, u32[]{:S(2)}, u32[]{:S(2)}) collective-permute-start(f32[384,128]{1,0:T(8,128)S(1)} %select_select_fusion), channel_id=1, source_target_pairs={{4,0},{8,4},{12,8},{16,12},{20,16},{24,20},{28,24},{5,1},{9,5},{13... | collective-permute-start | bytes 589832 | tf_op jit(solution)/shard_map/ppermute | solution.py:649
  60.2 2.3 %collective-permute-done.6.refs_6_ = f32[392,128]{1,0:T(8,128)S(1)} collective-permute-done((f32[392,128]{1,0:T(8,128)S(1)}, f32[392,128]{1,0:T(8,128)S(1)}, u32[]{:S(2)}, u32[]{:S(2)}) %collective-permute-start.6) | collective-permute-done | bytes 200736 | tf_op jit(solution)/shard_map/ppermute | solution.py:595
  62.5 1.2 %collective-permute-done.7.refs_7_ = f32[392,128]{1,0:T(8,128)S(1)} collective-permute-done((f32[392,128]{1,0:T(8,128)S(1)}, f32[392,128]{1,0:T(8,128)S(1)}, u32[]{:S(2)}, u32[]{:S(2)}) %collective-permute-start.7) | collective-permute-done | bytes 200736 | tf_op jit(solution)/shard_map/ppermute | solution.py:595
  63.7 2.4 %collective-permute-done.8.refs_8_ = f32[392,128]{1,0:T(8,128)S(1)} collective-permute-done((f32[392,128]{1,0:T(8,128)S(1)}, f32[392,128]{1,0:T(8,128)S(1)}, u32[]{:S(2)}, u32[]{:S(2)}) %collective-permute-start.8) | collective-permute-done | bytes 200736 | tf_op jit(solution)/shard_map/ppermute | solution.py:595
  66.1 3.2 %collective-permute-done.13.refs_14_ = f32[384,128]{1,0:T(8,128)S(1)} collective-permute-done((f32[384,128]{1,0:T(8,128)S(1)}, f32[384,128]{1,0:T(8,128)S(1)}, u32[]{:S(2)}, u32[]{:S(2)}) %collective-permute-start.13) | collective-permute-done | bytes 196640 | tf_op jit(solution)/shard_map/ppermute | solution.py:649
  69.3 2.2 %shard_map.57 = f32[2560,128]{1,0:T(8,128)} custom-call(f32[8,128]{1,0:T(8,128)S(1)} %fusion.refs_0_, f32[384,128]{1,0:T(8,128)S(1)} %get-tuple-element.28.refs_1_, f32[384,128]{1,0:T(8,128)S(1)} %collective-permute-done.2.refs_2_, f32[384,128]{1,0:T(8,128)S(1)} %collective-permute-done.3.refs_3_, f32[384,128]{1,0:T(8,128)S(1)} %collective-permute-done.4.refs_4_, ...), custom_call_target="tpu_custom_call" | custom-call | tf_op jit(solution)/shard_map/pallas_call | solution.py:652
  (21 shorter events, 0.3 us)
Async XLA Ops:
  0.0 6.3 %copy-start.1 = (f32[32,4096]{1,0:T(8,128)S(1)}, f32[32,4096]{1,0:T(8,128)}, u32[]{:S(2)}) copy-start(f32[32,4096]{1,0:T(8,128)} %param.7) | copy-start | bytes 1572868
  2.5 5.0 %collective-permute-start = (f32[264,128]{1,0:T(8,128)S(1)}, f32[264,128]{1,0:T(8,128)S(1)}, u32[]{:S(2)}, u32[]{:S(2)}) collective-permute-start(f32[264,128]{1,0:T(8,128)S(1)} %get-tuple-element.50), channel_id=1, source_target_pairs={{0,1},{1,2},{2,3},{3,4},{4,5},{5,6},{6,7},{7,8},{8,9},{9,10},{10,1... | collective-permute-start | bytes 405512 | tf_op jit(solution)/shard_map/ppermute | solution.py:535
  4.9 1.5 %slice-start = ((f32[32,6,4096]{2,0,1:T(8,128)}), f32[8,6,4096]{2,0,1:T(8,128)S(1)}, s32[]{:S(2)}) async-start(f32[32,6,4096]{2,0,1:T(8,128)} %param.5), calls=%async_computation | async-start | bytes 1572864 | tf_op jit(solution)/shard_map/slice | solution.py:521
  4.9 5.5 %collective-permute-start.1 = (f32[264,128]{1,0:T(8,128)S(1)}, f32[264,128]{1,0:T(8,128)S(1)}, u32[]{:S(2)}, u32[]{:S(2)}) collective-permute-start(f32[264,128]{1,0:T(8,128)S(1)} %get-tuple-element.49), channel_id=1, source_target_pairs={{1,0},{2,1},{3,2},{4,3},{5,4},{6,5},{7,6},{8,7},{9,8},{10,9},{11,1... | collective-permute-start | bytes 405512 | tf_op jit(solution)/shard_map/ppermute | solution.py:536
  6.4 9.6 %copy-start = (f32[32,6,4096]{2,0,1:T(8,128)S(1)}, f32[32,6,4096]{2,0,1:T(8,128)}, u32[]{:S(2)}) copy-start(f32[32,6,4096]{2,0,1:T(8,128)} %param.5) | copy-start | bytes 9437188
  10.4 28.1 %collective-permute-start.5 = (f32[2304,128]{1,0:T(8,128)}, f32[2304,128]{1,0:T(8,128)S(1)}, u32[]{:S(2)}, u32[]{:S(2)}) collective-permute-start(f32[2304,128]{1,0:T(8,128)} %pad_maximum_fusion), channel_id=1, source_target_pairs={{0,1},{1,2},{2,3},{3,4},{4,5},{5,6},{6,7},{7,8},{8,9},{9,10},{10,1... | collective-permute-start | bytes 3538952 | tf_op jit(solution)/shard_map/ppermute | solution.py:539
  35.2 13.4 %collective-permute-start.2 = (f32[384,128]{1,0:T(8,128)S(1)}, f32[384,128]{1,0:T(8,128)S(1)}, u32[]{:S(2)}, u32[]{:S(2)}) collective-permute-start(f32[384,128]{1,0:T(8,128)S(1)} %get-tuple-element.29), channel_id=1, source_target_pairs={{0,1},{1,2},{2,3},{3,0},{4,5},{5,6},{6,7},{7,4},{8,9},{9,10},{10,1... | collective-permute-start | bytes 589832 | tf_op jit(solution)/shard_map/ppermute | solution.py:595
  35.3 14.8 %collective-permute-start.3 = (f32[384,128]{1,0:T(8,128)S(1)}, f32[384,128]{1,0:T(8,128)S(1)}, u32[]{:S(2)}, u32[]{:S(2)}) collective-permute-start(f32[384,128]{1,0:T(8,128)S(1)} %get-tuple-element.30), channel_id=1, source_target_pairs={{0,2},{1,3},{2,0},{3,1},{4,6},{5,7},{6,4},{7,5},{8,10},{9,11},{10,... | collective-permute-start | bytes 589832 | tf_op jit(solution)/shard_map/ppermute | solution.py:595
  37.1 12.9 %collective-permute-start.4 = (f32[384,128]{1,0:T(8,128)S(1)}, f32[384,128]{1,0:T(8,128)S(1)}, u32[]{:S(2)}, u32[]{:S(2)}) collective-permute-start(f32[384,128]{1,0:T(8,128)S(1)} %get-tuple-element.31), channel_id=1, source_target_pairs={{0,3},{1,0},{2,1},{3,2},{4,7},{5,4},{6,5},{7,6},{8,11},{9,8},{10,9... | collective-permute-start | bytes 589832 | tf_op jit(solution)/shard_map/ppermute | solution.py:595
  47.3 7.7 %collective-permute-start.9 = (f32[384,128]{1,0:T(8,128)S(1)}, f32[384,128]{1,0:T(8,128)S(1)}, u32[]{:S(2)}, u32[]{:S(2)}) collective-permute-start(f32[384,128]{1,0:T(8,128)S(1)} %get-tuple-element.44), channel_id=1, source_target_pairs={{0,1},{1,2},{2,3},{3,0},{4,5},{5,6},{6,7},{7,4},{8,9},{9,10},{10,1... | collective-permute-start | bytes 589832 | tf_op jit(solution)/shard_map/ppermute | solution.py:595
  47.4 9.0 %collective-permute-start.10 = (f32[384,128]{1,0:T(8,128)S(1)}, f32[384,128]{1,0:T(8,128)S(1)}, u32[]{:S(2)}, u32[]{:S(2)}) collective-permute-start(f32[384,128]{1,0:T(8,128)S(1)} %get-tuple-element.45), channel_id=1, source_target_pairs={{0,2},{1,3},{2,0},{3,1},{4,6},{5,7},{6,4},{7,5},{8,10},{9,11},{10,... | collective-permute-start | bytes 589832 | tf_op jit(solution)/shard_map/ppermute | solution.py:595
  48.6 10.1 %collective-permute-start.11 = (f32[384,128]{1,0:T(8,128)S(1)}, f32[384,128]{1,0:T(8,128)S(1)}, u32[]{:S(2)}, u32[]{:S(2)}) collective-permute-start(f32[384,128]{1,0:T(8,128)S(1)} %get-tuple-element.46), channel_id=1, source_target_pairs={{0,3},{1,0},{2,1},{3,2},{4,7},{5,4},{6,5},{7,6},{8,11},{9,8},{10,9... | collective-permute-start | bytes 589832 | tf_op jit(solution)/shard_map/ppermute | solution.py:595
  50.1 10.1 %collective-permute-start.12 = (f32[384,128]{1,0:T(8,128)S(1)}, f32[384,128]{1,0:T(8,128)S(1)}, u32[]{:S(2)}, u32[]{:S(2)}) collective-permute-start(f32[384,128]{1,0:T(8,128)S(1)} %select_select_fusion.1), channel_id=1, source_target_pairs={{0,4},{4,8},{8,12},{12,16},{16,20},{20,24},{24,28},{1,5},{5,9},{9,... | collective-permute-start | bytes 589832 | tf_op jit(solution)/shard_map/ppermute | solution.py:646
  55.0 7.5 %collective-permute-start.6 = (f32[392,128]{1,0:T(8,128)S(1)}, f32[392,128]{1,0:T(8,128)S(1)}, u32[]{:S(2)}, u32[]{:S(2)}) collective-permute-start(f32[392,128]{1,0:T(8,128)S(1)} %get-tuple-element.40), channel_id=1, source_target_pairs={{0,1},{1,2},{2,3},{3,0},{4,5},{5,6},{6,7},{7,4},{8,9},{9,10},{10,1... | collective-permute-start | bytes 602120 | tf_op jit(solution)/shard_map/ppermute | solution.py:595
  55.1 8.6 %collective-permute-start.7 = (f32[392,128]{1,0:T(8,128)S(1)}, f32[392,128]{1,0:T(8,128)S(1)}, u32[]{:S(2)}, u32[]{:S(2)}) collective-permute-start(f32[392,128]{1,0:T(8,128)S(1)} %get-tuple-element.41), channel_id=1, source_target_pairs={{0,2},{1,3},{2,0},{3,1},{4,6},{5,7},{6,4},{7,5},{8,10},{9,11},{10,... | collective-permute-start | bytes 602120 | tf_op jit(solution)/shard_map/ppermute | solution.py:595
  56.4 9.7 %collective-permute-start.8 = (f32[392,128]{1,0:T(8,128)S(1)}, f32[392,128]{1,0:T(8,128)S(1)}, u32[]{:S(2)}, u32[]{:S(2)}) collective-permute-start(f32[392,128]{1,0:T(8,128)S(1)} %get-tuple-element.42), channel_id=1, source_target_pairs={{0,3},{1,0},{2,1},{3,2},{4,7},{5,4},{6,5},{7,6},{8,11},{9,8},{10,9... | collective-permute-start | bytes 602120 | tf_op jit(solution)/shard_map/ppermute | solution.py:595
  58.9 10.4 %collective-permute-start.13 = (f32[384,128]{1,0:T(8,128)S(1)}, f32[384,128]{1,0:T(8,128)S(1)}, u32[]{:S(2)}, u32[]{:S(2)}) collective-permute-start(f32[384,128]{1,0:T(8,128)S(1)} %select_select_fusion), channel_id=1, source_target_pairs={{4,0},{8,4},{12,8},{16,12},{20,16},{24,20},{28,24},{5,1},{9,5},{13... | collective-permute-start | bytes 589832 | tf_op jit(solution)/shard_map/ppermute | solution.py:649

commit v3 on v2

--- a/solution.py
+++ b/solution.py
@@ -13,7 +13,8 @@
 T = 32
 TH = T * H
 QUAD = 4
-UNROLL = 4
+MANY, FEW = 8, 4
+STEP = 8
 AXES = ("row", "col")
 RELAX = 2.0 / 3.0
 F32 = jnp.float32
@@ -22,8 +23,8 @@
 MB = 1024 * 1024
 
 
-def most_batches(rows, columns, ranges):
-    return (rows * K + (QUAD - 1) * columns) // QUAD + ranges * (UNROLL - 1) + 1
+def most_batches(rows, columns, ranges, unroll):
+    return (rows * K + (QUAD - 1) * columns) // QUAD + ranges * (unroll - 1) + 1
 
 
 def split(x):
@@ -66,7 +67,7 @@
     tb[slot] = jnp.concatenate([hi, lo], axis=0)
 
 
-def prolong(e, a_ref, base_of, row, start, pf, tb, entries, keep):
+def prolong(at, a_ref, base_of, row, start, pf, tb, entries, keep):
     row_of = lax.broadcasted_iota(I32, (64, 128), 0)
     row_of = jnp.where(row_of < T, 2 * row_of, 2 * row_of - 63)
     lane_of = lanes_of((64, 128))
@@ -82,11 +83,11 @@
             diagonal = jnp.sum(jnp.where(row_of == lane_of, x, 0.0), axis=1, keepdims=True)
             scale = -RELAX / jnp.where(diagonal == 0.0, 1.0, diagonal)
             for pair in range(4):
-                pf[e, pair] = jnp.zeros((64, 128), F32)
+                pf[at, pair] = jnp.zeros((64, 128), F32)
             value = product * scale + start
         else:
             value = product * scale
-        pf[e, slot >> 1] += jnp.where(lane_of // 64 == (slot & 1), value, 0.0)
+        pf[at, slot >> 1] += jnp.where(lane_of // 64 == (slot & 1), value, 0.0)
 
 
 def as_right(value, nat, spot, w, e, pair):
@@ -103,7 +104,7 @@
     pt_lo[pair * 128 : pair * 128 + 128, where] = lo
 
 
-def place_range(counts, starts, order, batch_source, first, last, begin, dummy):
+def place_range(counts, starts, order, batch_source, first, last, begin, dummy, unroll):
     def one(source, at):
         starts[source] = at
         after = at + ((counts[source] + QUAD - 1) >> 2)
@@ -112,11 +113,11 @@
         return after
 
     after = lax.fori_loop(first, last, one, begin)
-    for q in range(QUAD * (UNROLL - 1)):
+    for q in range(QUAD * (unroll - 1)):
         order[after * QUAD + q] = dummy
-    for q in range(UNROLL - 1):
+    for q in range(unroll - 1):
         batch_source[after + q] = first
-    return (after + UNROLL - 1) // UNROLL * UNROLL
+    return (after + unroll - 1) // unroll * unroll
 
 
 def fill_order(starts, order, batch_source, rank, pair):
@@ -126,12 +127,12 @@
     batch_source[spot >> 2] = source
 
 
-def apply_range(order, batch_source, begin, end, lhs, w, w_from, ap, row_from, own, side):
+def apply_range(order, batch_source, begin, end, lhs, w, w_from, ap, row_from, own, side, unroll):
     width = 256 if side is None else 512
 
     def step(i, carry):
-        for u in range(UNROLL):
-            b = i * UNROLL + u
+        for u in range(unroll):
+            b = i * unroll + u
             pairs = [order[b * QUAD + q] for q in range(QUAD)]
             left = wide(jnp.concatenate([lhs[pair] for pair in pairs], axis=0))
             right = right_of(w[batch_source[b] - w_from, :, :width])
@@ -143,7 +144,7 @@
                     ap[e, side] += product[q * 64 : q * 64 + 64, 256:]
         return carry
 
-    lax.fori_loop(begin // UNROLL, end // UNROLL, step, 0)
+    lax.fori_loop(begin // unroll, end // unroll, step, 0)
 
 
 def product3(left, right):
@@ -178,11 +179,14 @@
 def early_kernel(mine, a_own, t_own, small_up, small_down, *refs, ncol):
     ups, refs = refs[:ncol], refs[ncol:]
     part_out, ap_out, lhs_out, w_out, pt_hi_out, pt_lo_out = refs[:6]
-    a_rows, tn, tb, lhs, pf, nat, w, pt_hi_u, pt_lo_u, pt_hi, pt_lo, ap, ap_hi, ap_lo = refs[6:20]
-    part_own, part_up = refs[20:22]
-    low_ints, high_ints, slots, counts, starts, ranks, order, batch_source, sems = refs[22:]
+    a_rows, tn, tb, lhs, w, pt_hi_u, pt_lo_u, pt_hi, pt_lo, ap, ap_hi, ap_lo = refs[6:18]
+    part_own, part_up = refs[18:20]
+    pf, nat = refs[20 : 20 + STEP], refs[20 + STEP : 20 + 2 * STEP]
+    refs = refs[20 + 2 * STEP :]
+    low_ints, high_ints, slots, counts, starts, ranks, order, batch_source, sems = refs
+    whole = pltpu.make_async_copy(a_own, a_rows, sems.at[2])
+    whole.start()
     copies = [
-        pltpu.make_async_copy(a_own, a_rows, sems.at[2]),
         pltpu.make_async_copy(small_up.at[pl.ds(TH, 8)], low_ints, sems.at[0]),
         pltpu.make_async_copy(small_down.at[pl.ds(TH, 8)], high_ints, sems.at[1]),
     ]
@@ -215,9 +219,8 @@
 
     lhs[R * 8] = jnp.zeros((64, 128), BF16)
 
-    def prolong_rows(i, carry):
-        group = i // H
-        row = lax.rem(i, H)
+    def prolong_row(i, group, u):
+        row = i - group * H
 
         def entries(k):
             j = mine[2 + k, i].astype(I32) - origin
@@ -231,15 +234,20 @@
             lhs[i * 8 + k] = left
 
         start = stacked(raw_block(t_own, group * TH, row))
-        prolong(
-            i, a_rows, lambda k: (k * (R // H) + group) * TH, row, start, pf, tb, entries, keep
-        )
-        return carry
-
-    lax.fori_loop(0, R, prolong_rows, 0, unroll=4)
+        base_of = lambda k: (k * (R // H) + group) * TH
+        prolong(i // STEP, a_rows, base_of, row, start, pf[u], tb, entries, keep)
+
+    whole.wait()
+
+    def prolong_rows(i, carry):
+        for u in range(STEP):
+            prolong_row(i * STEP + u, i // (H // STEP), u)
+        return carry
+
+    lax.fori_loop(0, R // STEP, prolong_rows, 0)
 
     place = lambda first, last, begin: place_range(
-        counts, starts, order, batch_source, first, last, begin, R * 8
+        counts, starts, order, batch_source, first, last, begin, R * 8, MANY
     )
     first_end = place(0, H, jnp.int32(0))
     second_end = place(H, R - H, first_end)
@@ -249,23 +257,26 @@
     for third in range(3):
         ap[R, third] = jnp.zeros((64, 256), F32)
 
-    def arrange(i, carry, pairs, w_ref, pt_refs, first):
-        for e in (2 * i, 2 * i + 1):
+    def arrange(i, carry, pairs, pt_refs, first):
+        for u in range(STEP):
+            e = i * STEP + u
             for pair in range(pairs):
-                as_right(pf[e, pair], nat, (e & 1) * 4 + pair, w_ref, e, pair)
+                as_right(pf[u][i, pair], nat[u], pair, w, e, pair)
             for third in range(3):
                 ap[e, third] = jnp.zeros((64, 256), F32)
             for k in range(K):
                 fill_order(starts, order, batch_source, ranks[e * 8 + k], e * 8 + k)
-        where = pl.ds(pl.multiple_of((i - first // 2) * 128, 128), 128)
-        for pair in range(pairs):
-            as_left(pf[2 * i, pair], pf[2 * i + 1, pair], *pt_refs, pair, where)
+        for u in range(0, STEP, 2):
+            where = pl.ds(pl.multiple_of((i * STEP + u - first) * 64, 128), 128)
+            for pair in range(pairs):
+                as_left(pf[u][i, pair], pf[u + 1][i, pair], *pt_refs, pair, where)
         return carry
 
     inner = (pt_hi, pt_lo)
-    lax.fori_loop(0, H // 2, lambda i, c: arrange(i, c, 4, w, (pt_hi_u, pt_lo_u), 0), 0)
-    lax.fori_loop(H // 2, (R - H) // 2, lambda i, c: arrange(i, c, 2, w, inner, H), 0)
-    lax.fori_loop((R - H) // 2, R // 2, lambda i, c: arrange(i, c, 4, w, inner, H), 0)
+    at = [0, H // STEP, (R - H) // STEP, R // STEP]
+    lax.fori_loop(at[0], at[1], lambda i, c: arrange(i, c, 4, (pt_hi_u, pt_lo_u), 0), 0)
+    lax.fori_loop(at[1], at[2], lambda i, c: arrange(i, c, 2, inner, H), 0)
+    lax.fori_loop(at[2], at[3], lambda i, c: arrange(i, c, 4, inner, H), 0)
 
     saved = [
         pltpu.make_async_copy(lhs.at[pl.ds(0, H * 8)], lhs_out, sems.at[3]),
@@ -276,9 +287,9 @@
     for copy in saved:
         copy.start()
     same = lambda e: e
-    apply_range(order, batch_source, 0, first_end, lhs, w, 0, ap, same, 1, 0)
-    apply_range(order, batch_source, first_end, second_end, lhs, w, 0, ap, same, 1, None)
-    apply_range(order, batch_source, second_end, third_end, lhs, w, 0, ap, same, 1, 2)
+    apply_range(order, batch_source, 0, first_end, lhs, w, 0, ap, same, 1, 0, MANY)
+    apply_range(order, batch_source, first_end, second_end, lhs, w, 0, ap, same, 1, None, MANY)
+    apply_range(order, batch_source, second_end, third_end, lhs, w, 0, ap, same, 1, 2, MANY)
 
     saved.append(pltpu.make_async_copy(ap.at[pl.ds(0, H)], ap_out, sems.at[7]))
     saved[-1].start()
@@ -293,19 +304,19 @@
 
     lax.fori_loop(H, R, split_ap, 0, unroll=2)
 
-    last = slice((R - 2 * H) * 64, (R - H) * 64)
-    up = product3(
-        (pt_hi[256:512, last], pt_lo[256:512, last]), (ap_hi[last, :], ap_lo[last, :])
-    )
-    for pair in range(6):
-        part_up[pair] = up[:, pair * 128 : pair * 128 + 128]
-    for s in range(ncol):
-        give(ups[s], part_up, s, col, ncol, high_ints, False)
     own = product3((pt_hi[0:256, :], pt_lo[0:256, :]), (ap_hi[...], ap_lo[...]))
     for pair in range(6):
         part_own[pair] = own[:, pair * 128 : pair * 128 + 128]
     saved.append(pltpu.make_async_copy(part_own, part_out, sems.at[8]))
     saved[-1].start()
+    last = slice((R - 2 * H) * 64, (R - H) * 64)
+    up = product3(
+        (pt_hi[256:512, last], pt_lo[256:512, last]), (ap_hi[last, :], ap_lo[last, :])
+    )
+    for pair in range(6):
+        part_up[pair] = up[:, pair * 128 : pair * 128 + 128]
+    for s in range(ncol):
+        give(ups[s], part_up, s, col, ncol, high_ints, False)
     for copy in saved:
         copy.wait()
 
@@ -313,9 +324,10 @@
 def late_kernel(mine, small_up, t_first, big, *refs, ncol):
     part_in, ap_in, lhs_in, w_in, pt_hi_in, pt_lo_in = refs[:6]
     owns, downs, refs = refs[6 : 6 + ncol], refs[6 + ncol : 6 + 2 * ncol], refs[6 + 2 * ncol :]
-    tn, tb, lhs, pf, nat, w, pt_hi, pt_lo, ap, ap_hi, ap_lo, part_down, part_full = refs[:13]
-    t_low, a_low, part_own, ap_u, lhs_u, w_u, pt_hi_u, pt_lo_u = refs[13:21]
-    low_ints, slots, counts, starts, ranks, order, batch_source, sems = refs[21:]
+    tn, tb, lhs, w, pt_hi, pt_lo, ap, ap_hi, ap_lo, part_down, part_full = refs[:11]
+    t_low, a_low, part_own, ap_u, lhs_u, w_u, pt_hi_u, pt_lo_u = refs[11:19]
+    pf, nat = refs[19 : 19 + STEP], refs[19 + STEP : 19 + 2 * STEP]
+    low_ints, slots, counts, starts, ranks, order, batch_source, sems = refs[19 + 2 * STEP :]
     copies = [
         pltpu.make_async_copy(big.at[pl.ds(K * TH, (R - H) * T)], t_low, sems.at[0]),
         pltpu.make_async_copy(small_up.at[pl.ds(TH, 8)], low_ints, sems.at[1]),
@@ -360,7 +372,7 @@
         counts[source] = seen + 1
         ranks[at] = source * 512 + seen
 
-    def prolong_rows(i, carry):
+    def prolong_row(i, u):
         def entries(k):
             j = low_ints[2 + k, R - H + i].astype(I32) - origin
             rank(j >= R, j, i * 8 + k)
@@ -373,13 +385,17 @@
             j = mine[2 + k, i].astype(I32) - origin
             rank(j < R, j, (H + i) * 8 + k)
         start = stacked(raw_block(small_up, 0, i))
-        prolong(i, a_low, lambda k: k * TH, i, start, pf, tb, entries, keep)
-        return carry
-
-    lax.fori_loop(0, H, prolong_rows, 0, unroll=4)
+        prolong(i // STEP, a_low, lambda k: k * TH, i, start, pf[u], tb, entries, keep)
+
+    def prolong_rows(i, carry):
+        for u in range(STEP):
+            prolong_row(i * STEP + u, u)
+        return carry
+
+    lax.fori_loop(0, H // STEP, prolong_rows, 0)
 
     place = lambda first, last, begin: place_range(
-        counts, starts, order, batch_source, first, last, begin, H * 8
+        counts, starts, order, batch_source, first, last, begin, H * 8, FEW
     )
     first_end = place(0, H, jnp.int32(0))
     second_end = place(H, 2 * H, first_end)
@@ -392,24 +408,26 @@
         ap[2 * H, side] = jnp.zeros((64, 256), F32)
 
     def arrange(i, carry):
-        for e in (2 * i, 2 * i + 1):
+        for u in range(STEP):
+            e = i * STEP + u
             for pair in range(4):
-                as_right(pf[e, pair], nat, (e & 1) * 4 + pair, w, e, pair)
+                as_right(pf[u][i, pair], nat[u], pair, w, e, pair)
             for side in range(2):
                 ap[e, side] = jnp.zeros((64, 256), F32)
                 ap[H + e, side] = ap_u[e, side]
             for k in range(K):
                 fill_order(starts, order, batch_source, ranks[e * 8 + k], e * 8 + k)
                 fill_order(starts, order, batch_source, ranks[(H + e) * 8 + k], e * 8 + k)
-        where = pl.ds(pl.multiple_of(i * 128, 128), 128)
-        for pair in range(4):
-            as_left(pf[2 * i, pair], pf[2 * i + 1, pair], pt_hi, pt_lo, pair, where)
-        return carry
-
-    lax.fori_loop(0, H // 2, arrange, 0)
+        for u in range(0, STEP, 2):
+            where = pl.ds(pl.multiple_of((i * STEP + u) * 64, 128), 128)
+            for pair in range(4):
+                as_left(pf[u][i, pair], pf[u + 1][i, pair], pt_hi, pt_lo, pair, where)
+        return carry
+
+    lax.fori_loop(0, H // STEP, arrange, 0)
 
     apply_range(
-        order, batch_source, 0, first_end, lhs_u, w, 0, ap, lambda e: e + H, 1, 0
+        order, batch_source, 0, first_end, lhs_u, w, 0, ap, lambda e: e + H, 1, 0, FEW
     )
     apply_range(
         order,
@@ -423,6 +441,7 @@
         lambda e: jnp.where(e == H, 2 * H, e),
         1,
         0,
+        FEW,
     )
 
     def split_ap(e, carry):
@@ -465,8 +484,8 @@
         give(owns[s], part_full, s, col, ncol, mine, True)
 
 
-MOST_EARLY = most_batches(R, R, 3)
-MOST_LATE = most_batches(2 * H, 2 * H, 2)
+MOST_EARLY = most_batches(R, R, 3, MANY)
+MOST_LATE = most_batches(2 * H, 2 * H, 2, FEW)
 
 
 def combine_kernel(mine, *refs, ncol):
@@ -476,7 +495,7 @@
     span = G * T
     for s in range(ncol):
         home = lax.rem(col - s + ncol, ncol)
-        total[s, 0 : 4 * span] = jnp.zeros((4 * span, 128), F32)
+        total[s, 0:span] = jnp.zeros((span, 128), F32)
         total[s, 4 * span : 5 * span] = jnp.zeros((span, 128), F32)
         total[s, span : 4 * span] = owns[s][0 : 3 * span]
 
@@ -535,7 +554,6 @@
     small_up = lax.ppermute(jnp.concatenate([last, meta], axis=0), AXES, up)
     small_down = lax.ppermute(jnp.concatenate([first, meta], axis=0), AXES, down)
     big = jnp.concatenate([a_last, t_own[: (R - H) * T]], axis=0)
-    big, small_up, small_down = lax.optimization_barrier((big, small_up, small_down))
     big = lax.ppermute(big, AXES, up)
 
     span = 3 * G * T
@@ -562,8 +580,6 @@
             pltpu.VMEM((8, 64, 128), F32),
             pltpu.VMEM((R + 2 * H, 128, 128), BF16),
             pltpu.VMEM((R * 8 + 1, 64, 128), BF16),
-            pltpu.VMEM((R, 4, 64, 128), F32),
-            pltpu.VMEM((8, 64, 128), F32),
             pltpu.VMEM((R, 128, 512), BF16),
             pltpu.VMEM((512, H * 64), BF16),
             pltpu.VMEM((512, H * 64), BF16),
@@ -574,6 +590,8 @@
             pltpu.VMEM(((R - H) * 64, 768), BF16),
             pltpu.VMEM((6, 256, 128), F32),
             pltpu.VMEM((6, 256, 128), F32),
+            *[pltpu.VMEM((R // STEP, 4, 64, 128), F32)] * STEP,
+            *[pltpu.VMEM((4, 64, 128), F32)] * STEP,
             pltpu.SMEM((8, 128), F32),
             pltpu.SMEM((8, 128), F32),
             pltpu.SMEM((R + 2 * H,), I32),
@@ -585,6 +603,7 @@
             pltpu.SemaphoreType.DMA((9,)),
         ],
         compiler_params=pltpu.CompilerParams(vmem_limit_bytes=44 * MB),
+        cost_estimate=pl.CostEstimate(flops=22 * 10**9, bytes_accessed=12 * MB, transcendentals=0),
     )(meta, a_own, t_own, small_up, small_down)
     ups, state = outs[:ncol], [pltpu.with_memory_space_constraint(x, pltpu.HBM) for x in outs[ncol:]]
 
@@ -611,8 +630,6 @@
             pltpu.VMEM((8, 64, 128), F32),
             pltpu.VMEM((R + H, 128, 128), BF16),
             pltpu.VMEM((H * 8 + 1, 64, 128), BF16),
-            pltpu.VMEM((H, 4, 64, 128), F32),
-            pltpu.VMEM((8, 64, 128), F32),
             pltpu.VMEM((H, 128, 512), BF16),
             pltpu.VMEM((512, H * 64), BF16),
             pltpu.VMEM((512, H * 64), BF16),
@@ -629,6 +646,8 @@
             pltpu.VMEM((H, 128, 512), BF16),
             pltpu.VMEM((512, H * 64), BF16),
             pltpu.VMEM((512, H * 64), BF16),
+            *[pltpu.VMEM((H // STEP, 4, 64, 128), F32)] * STEP,
+            *[pltpu.VMEM((4, 64, 128), F32)] * STEP,
             pltpu.SMEM((8, 128), F32),
             pltpu.SMEM((R + H,), I32),
             pltpu.SMEM((2 * H + 1,), I32),
@@ -642,13 +661,12 @@
     )(meta, small_up, first, big, *state)
     owns, downs = outs[:ncol], outs[ncol:]
     downs = rotated(downs)
+    to_next = chosen(ups, lax.rem(col + 1, ncol))
+    to_last = chosen(downs, col)
+    to_next, downs[0] = lax.optimization_barrier((to_next, downs[0]))
+    cross_up = lax.ppermute(to_next, "row", [(r, r + 1) for r in range(nrow - 1)])
+    cross_down = lax.ppermute(to_last, "row", [(r + 1, r) for r in range(nrow - 1)])
     owns = rotated(owns)
-    cross_up = lax.ppermute(
-        chosen(ups, lax.rem(col + 1, ncol)), "row", [(r, r + 1) for r in range(nrow - 1)]
-    )
-    cross_down = lax.ppermute(
-        chosen(downs, col), "row", [(r + 1, r) for r in range(nrow - 1)]
-    )
     result = pl.pallas_call(
         lambda *refs: combine_kernel(*refs, ncol=ncol),
         out_shape=jax.ShapeDtypeStruct((5 * G * T * G, 128), F32),

time: 72.7 us -> 70.2 us (0.966); the launches traced: 71.5 us -> 69.8 us
  starting transfers between devices: 25.3 us -> 24.4 us
    ppermute x2, waiting for transfers between devices: 3.17 us -> 6.68 us  [the longest x1 3.46 us: local(): lax.ppermute(to_next, 'row', [(r, r + 1) for r in range(nrow - 1)])]
    ppermute x1, waiting for transfers between devices: 2.91 us -> 0.01 us  [local(): lax.ppermute(jnp.concatenate([first, meta], axis=0), AXES, down)]
    ppermute x9, starting transfers between devices: 9.79 us -> 8.75 us  [rotated(): moved.append(lax.ppermute(blocks[s], 'col', route))]
    ppermute x9, waiting for transfers between devices: 5.95 us -> 5.04 us  [rotated(): moved.append(lax.ppermute(blocks[s], 'col', route))]
where the time goes in v3:
time: 70.2 us; the launch traced here: 69.8 us
  Pallas kernels  29.7 us (42%)
  starting transfers between devices  24.4 us (35%)
  waiting for transfers between devices  11.7 us (17%)
  other arithmetic  2.63 us (4%)
  local copies, waits for them, and re-layouts  1.09 us (2%)
    pallas_call x1, Pallas kernels, local(): pl.pallas_call(lambda *refs: early_kernel(*refs, ncol=ncol), out_shape=[p...  18.7 us
    pallas_call x1, Pallas kernels, local(): pl.pallas_call(lambda *refs: late_kernel(*refs, ncol=ncol), out_shape=[ma...  8.81 us
    ppermute x9, starting transfers between devices, rotated(): moved.append(lax.ppermute(blocks[s], 'col', route))  8.75 us
    ppermute x1, starting transfers between devices, local(): big = lax.ppermute(big, AXES, up)  5.35 us
    ppermute x1, starting transfers between devices, local(): lax.ppermute(to_next, 'row', [(r, r + 1) for r in range(nrow - 1)])  5.23 us
    ppermute x9, waiting for transfers between devices, rotated(): moved.append(lax.ppermute(blocks[s], 'col', route))  5.04 us
    ppermute x1, waiting for transfers between devices, local(): lax.ppermute(to_next, 'row', [(r, r + 1) for r in range(nrow - 1)])  3.46 us
    ppermute x1, waiting for transfers between devices, local(): lax.ppermute(to_last, 'row', [(r + 1, r) for r in range(nrow - 1)])  3.22 us
  transfers between devices with their start and end apart: 14, of which 5 were waited for; matrix products, arithmetic and copies ran while one was open for 2% of the time, Pallas kernels for 39%

profile of v3, /device:TPU:0, one launch (start us, length us, event | category | flops | bytes accessed | tf_op | source)
XLA Modules:
  0.0 69.8 jit_solution(4834657831647704772)
XLA Ops:
  0.0 1.0 %slice_bitcast_fusion = (f32[256,128]{1,0:T(8,128)S(1)}, f32[256,128]{1,0:T(8,128)S(1)}) fusion(f32[4,32,8,128]{3,2,1,0:T(8,128)} %bitcast.34), kind=kLoop, calls=%fused_computation.5 | loop fusion | bytes 524288 | tf_op jit(solution)/shard_map/slice | solution.py:542
  1.1 0.7 %add_bitcast_fusion = s32[1,5]{1,0:T(1,128)S(1)} fusion(s32[1]{0:T(128)} %bitcast.1, s32[4]{0:T(128)} %param.9), kind=kLoop, calls=%fused_computation.10 | loop fusion | flops 5 | bytes 40 | tf_op jit(solution)/shard_map/reshape | solution.py:547
  1.8 0.7 %fusion.refs_0_ = f32[8,128]{1,0:T(8,128)S(1)} fusion(s32[6,32]{1,0:T(8,128)} %bitcast.40, s32[1,5]{1,0:T(1,128)S(1)} %add_bitcast_fusion, s32[1,32]{1,0:T(1,128)} %bitcast.41), kind=kLoop, calls=%fused_computation.8 | loop fusion | flops 3072 | bytes 5012 | tf_op jit(solution)/shard_map/convert_element_type | solution.py:553
  2.5 2.4 %collective-permute-start = (f32[264,128]{1,0:T(8,128)S(1)}, f32[264,128]{1,0:T(8,128)S(1)}, u32[]{:S(2)}, u32[]{:S(2)}) collective-permute-start(f32[264,128]{1,0:T(8,128)S(1)} %get-tuple-element.48), channel_id=1, source_target_pairs={{0,1},{1,2},{2,3},{3,4},{4,5},{5,6},{6,7},{7,8},{8,9},{9,10},{10,1... | collective-permute-start | bytes 405512 | tf_op jit(solution)/shard_map/ppermute | solution.py:554
  4.9 1.4 %collective-permute-start.1 = (f32[264,128]{1,0:T(8,128)S(1)}, f32[264,128]{1,0:T(8,128)S(1)}, u32[]{:S(2)}, u32[]{:S(2)}) collective-permute-start(f32[264,128]{1,0:T(8,128)S(1)} %get-tuple-element.47), channel_id=1, source_target_pairs={{1,0},{2,1},{3,2},{4,3},{5,4},{6,5},{7,6},{8,7},{9,8},{10,9},{11,1... | collective-permute-start | bytes 405512 | tf_op jit(solution)/shard_map/ppermute | solution.py:555
  6.4 1.1 %pad_maximum_fusion = f32[2304,128]{1,0:T(8,128)} fusion(f32[768,128]{1,0:T(8,128)S(1)} %bitcast.39, f32[1536,128]{1,0:T(8,128)S(1)} %bitcast.38), kind=kLoop, calls=%fused_computation | loop fusion | flops 294912 | bytes 2359296 | tf_op jit(solution)/shard_map/concatenate | solution.py:556
  7.5 5.4 %collective-permute-start.5 = (f32[2304,128]{1,0:T(8,128)}, f32[2304,128]{1,0:T(8,128)S(1)}, u32[]{:S(2)}, u32[]{:S(2)}) collective-permute-start(f32[2304,128]{1,0:T(8,128)} %pad_maximum_fusion), channel_id=1, source_target_pairs={{0,1},{1,2},{2,3},{3,4},{4,5},{5,6},{6,7},{7,8},{8,9},{9,10},{10,1... | collective-permute-start | bytes 3538952 | tf_op jit(solution)/shard_map/ppermute | solution.py:557
  12.9 18.7 %shard_map.55 = (f32[384,128]{1,0:T(8,128)S(1)}, f32[384,128]{1,0:T(8,128)S(1)}, f32[384,128]{1,0:T(8,128)S(1)}, f32[384,128]{1,0:T(8,128)S(1)}, f32[6,256,128]{...) custom-call(f32[8,128]{1,0:T(8,128)S(1)} %fusion.refs_0_, ...), custom_call_target="tpu_custom_call" | custom-call | flops 22000001024 | bytes 12582912 | tf_op jit(solution)/shard_map/pallas_call | solution.py:573
  31.6 1.7 %collective-permute-start.2 = (f32[384,128]{1,0:T(8,128)S(1)}, f32[384,128]{1,0:T(8,128)S(1)}, u32[]{:S(2)}, u32[]{:S(2)}) collective-permute-start(f32[384,128]{1,0:T(8,128)S(1)} %get-tuple-element.26), channel_id=1, source_target_pairs={{0,1},{1,2},{2,3},{3,0},{4,5},{5,6},{6,7},{7,4},{8,9},{9,10},{10,1... | collective-permute-start | bytes 589832 | tf_op jit(solution)/shard_map/ppermute | solution.py:614
  33.3 1.9 %collective-permute-start.3 = (f32[384,128]{1,0:T(8,128)S(1)}, f32[384,128]{1,0:T(8,128)S(1)}, u32[]{:S(2)}, u32[]{:S(2)}) collective-permute-start(f32[384,128]{1,0:T(8,128)S(1)} %get-tuple-element.27), channel_id=1, source_target_pairs={{0,2},{1,3},{2,0},{3,1},{4,6},{5,7},{6,4},{7,5},{8,10},{9,11},{10,... | collective-permute-start | bytes 589832 | tf_op jit(solution)/shard_map/ppermute | solution.py:614
  35.2 8.8 %shard_map.56 = (f32[392,128]{1,0:T(8,128)S(1)}, f32[392,128]{1,0:T(8,128)S(1)}, f32[392,128]{1,0:T(8,128)S(1)}, f32[392,128]{1,0:T(8,128)S(1)}, f32[384,128]{1,...) custom-call(f32[8,128]{1,0:T(8,128)S(1)} %fusion.refs_0_, ...), custom_call_target="tpu_custom_call" | custom-call | tf_op jit(solution)/shard_map/pallas_call | solution.py:624
  44.0 1.0 %collective-permute-start.9 = (f32[384,128]{1,0:T(8,128)S(1)}, f32[384,128]{1,0:T(8,128)S(1)}, u32[]{:S(2)}, u32[]{:S(2)}) collective-permute-start(f32[384,128]{1,0:T(8,128)S(1)} %get-tuple-element.41), channel_id=1, source_target_pairs={{0,1},{1,2},{2,3},{3,0},{4,5},{5,6},{6,7},{7,4},{8,9},{9,10},{10,1... | collective-permute-start | bytes 589832 | tf_op jit(solution)/shard_map/ppermute | solution.py:614
  45.0 1.9 %collective-permute-start.10 = (f32[384,128]{1,0:T(8,128)S(1)}, f32[384,128]{1,0:T(8,128)S(1)}, u32[]{:S(2)}, u32[]{:S(2)}) collective-permute-start(f32[384,128]{1,0:T(8,128)S(1)} %get-tuple-element.42), channel_id=1, source_target_pairs={{0,2},{1,3},{2,0},{3,1},{4,6},{5,7},{6,4},{7,5},{8,10},{9,11},{10,... | collective-permute-start | bytes 589832 | tf_op jit(solution)/shard_map/ppermute | solution.py:614
  46.9 1.4 %collective-permute-start.11 = (f32[384,128]{1,0:T(8,128)S(1)}, f32[384,128]{1,0:T(8,128)S(1)}, u32[]{:S(2)}, u32[]{:S(2)}) collective-permute-start(f32[384,128]{1,0:T(8,128)S(1)} %get-tuple-element.43), channel_id=1, source_target_pairs={{0,3},{1,0},{2,1},{3,2},{4,7},{5,4},{6,5},{7,6},{8,11},{9,8},{10,9... | collective-permute-start | bytes 589832 | tf_op jit(solution)/shard_map/ppermute | solution.py:614
  48.4 0.4 collective-permute-start.7
  48.8 0.9 %collective-permute-done.9.refs_10_ = f32[384,128]{1,0:T(8,128)S(1)} collective-permute-done((f32[384,128]{1,0:T(8,128)S(1)}, f32[384,128]{1,0:T(8,128)S(1)}, u32[]{:S(2)}, u32[]{:S(2)}) %collective-permute-start.9) | collective-permute-done | bytes 196640 | tf_op jit(solution)/shard_map/ppermute | solution.py:614
  49.7 0.5 collective-permute-start.8
  50.1 2.7 %collective-permute-done.10.refs_11_ = f32[384,128]{1,0:T(8,128)S(1)} collective-permute-done((f32[384,128]{1,0:T(8,128)S(1)}, f32[384,128]{1,0:T(8,128)S(1)}, u32[]{:S(2)}, u32[]{:S(2)}) %collective-permute-start.10) | collective-permute-done | bytes 196640 | tf_op jit(solution)/shard_map/ppermute | solution.py:614
  52.8 5.2 %collective-permute-start.12 = (f32[384,128]{1,0:T(8,128)S(1)}, f32[384,128]{1,0:T(8,128)S(1)}, u32[]{:S(2)}, u32[]{:S(2)}) collective-permute-start(f32[384,128]{1,0:T(8,128)S(1)} %select_select_fusion.1), channel_id=1, source_target_pairs={{0,4},{4,8},{8,12},{12,16},{16,20},{20,24},{24,28},{1,5},{5,9},{9,... | collective-permute-start | bytes 589832 | tf_op jit(solution)/shard_map/ppermute | solution.py:667
  58.1 1.3 %collective-permute-start.13 = (f32[384,128]{1,0:T(8,128)S(1)}, f32[384,128]{1,0:T(8,128)S(1)}, u32[]{:S(2)}, u32[]{:S(2)}) collective-permute-start(f32[384,128]{1,0:T(8,128)S(1)} %select_select_fusion), channel_id=1, source_target_pairs={{4,0},{8,4},{12,8},{16,12},{20,16},{24,20},{28,24},{5,1},{9,5},{13... | collective-permute-start | bytes 589832 | tf_op jit(solution)/shard_map/ppermute | solution.py:668
  59.4 3.5 %collective-permute-done.12.refs_13_ = f32[384,128]{1,0:T(8,128)S(1)} collective-permute-done((f32[384,128]{1,0:T(8,128)S(1)}, f32[384,128]{1,0:T(8,128)S(1)}, u32[]{:S(2)}, u32[]{:S(2)}) %collective-permute-start.12) | collective-permute-done | bytes 196640 | tf_op jit(solution)/shard_map/ppermute | solution.py:667
  62.9 1.4 %collective-permute-done.8.refs_8_ = f32[392,128]{1,0:T(8,128)S(1)} collective-permute-done((f32[392,128]{1,0:T(8,128)S(1)}, f32[392,128]{1,0:T(8,128)S(1)}, u32[]{:S(2)}, u32[]{:S(2)}) %collective-permute-start.8) | collective-permute-done | bytes 200736 | tf_op jit(solution)/shard_map/ppermute | solution.py:614
  64.3 3.2 %collective-permute-done.13.refs_14_ = f32[384,128]{1,0:T(8,128)S(1)} collective-permute-done((f32[384,128]{1,0:T(8,128)S(1)}, f32[384,128]{1,0:T(8,128)S(1)}, u32[]{:S(2)}, u32[]{:S(2)}) %collective-permute-start.13) | collective-permute-done | bytes 196640 | tf_op jit(solution)/shard_map/ppermute | solution.py:668
  67.5 2.2 %shard_map.57 = f32[2560,128]{1,0:T(8,128)} custom-call(f32[8,128]{1,0:T(8,128)S(1)} %fusion.refs_0_, f32[384,128]{1,0:T(8,128)S(1)} %get-tuple-element.25.refs_1_, f32[384,128]{1,0:T(8,128)S(1)} %collective-permute-done.2.refs_2_, f32[384,128]{1,0:T(8,128)S(1)} %collective-permute-done.3.refs_3_, f32[384,128]{1,0:T(8,128)S(1)} %collective-permute-done.4.refs_4_, ...), custom_call_target="tpu_custom_call" | custom-call | tf_op jit(solution)/shard_map/pallas_call | solution.py:670
  (21 shorter events, 0.2 us)
Async XLA Ops:
  0.0 6.3 %copy-start = (f32[32,4096]{1,0:T(8,128)S(1)}, f32[32,4096]{1,0:T(8,128)}, u32[]{:S(2)}) copy-start(f32[32,4096]{1,0:T(8,128)} %param.7) | copy-start | bytes 1572868
  2.5 10.3 %collective-permute-start = (f32[264,128]{1,0:T(8,128)S(1)}, f32[264,128]{1,0:T(8,128)S(1)}, u32[]{:S(2)}, u32[]{:S(2)}) collective-permute-start(f32[264,128]{1,0:T(8,128)S(1)} %get-tuple-element.48), channel_id=1, source_target_pairs={{0,1},{1,2},{2,3},{3,4},{4,5},{5,6},{6,7},{7,8},{8,9},{9,10},{10,1... | collective-permute-start | bytes 405512 | tf_op jit(solution)/shard_map/ppermute | solution.py:554
  4.9 1.5 %slice-start = ((f32[32,6,4096]{2,0,1:T(8,128)}), f32[8,6,4096]{2,0,1:T(8,128)S(1)}, s32[]{:S(2)}) async-start(f32[32,6,4096]{2,0,1:T(8,128)} %param.5), calls=%async_computation | async-start | bytes 1572864 | tf_op jit(solution)/shard_map/slice | solution.py:540
  4.9 8.0 %collective-permute-start.1 = (f32[264,128]{1,0:T(8,128)S(1)}, f32[264,128]{1,0:T(8,128)S(1)}, u32[]{:S(2)}, u32[]{:S(2)}) collective-permute-start(f32[264,128]{1,0:T(8,128)S(1)} %get-tuple-element.47), channel_id=1, source_target_pairs={{1,0},{2,1},{3,2},{4,3},{5,4},{6,5},{7,6},{8,7},{9,8},{10,9},{11,1... | collective-permute-start | bytes 405512 | tf_op jit(solution)/shard_map/ppermute | solution.py:555
  6.4 6.5 %copy-start.1 = (f32[32,6,4096]{2,0,1:T(8,128)S(1)}, f32[32,6,4096]{2,0,1:T(8,128)}, u32[]{:S(2)}) copy-start(f32[32,6,4096]{2,0,1:T(8,128)} %param.5) | copy-start | bytes 9437188
  7.5 27.7 %collective-permute-start.5 = (f32[2304,128]{1,0:T(8,128)}, f32[2304,128]{1,0:T(8,128)S(1)}, u32[]{:S(2)}, u32[]{:S(2)}) collective-permute-start(f32[2304,128]{1,0:T(8,128)} %pad_maximum_fusion), channel_id=1, source_target_pairs={{0,1},{1,2},{2,3},{3,4},{4,5},{5,6},{6,7},{7,8},{8,9},{9,10},{10,1... | collective-permute-start | bytes 3538952 | tf_op jit(solution)/shard_map/ppermute | solution.py:557
  31.6 15.3 %collective-permute-start.2 = (f32[384,128]{1,0:T(8,128)S(1)}, f32[384,128]{1,0:T(8,128)S(1)}, u32[]{:S(2)}, u32[]{:S(2)}) collective-permute-start(f32[384,128]{1,0:T(8,128)S(1)} %get-tuple-element.26), channel_id=1, source_target_pairs={{0,1},{1,2},{2,3},{3,0},{4,5},{5,6},{6,7},{7,4},{8,9},{9,10},{10,1... | collective-permute-start | bytes 589832 | tf_op jit(solution)/shard_map/ppermute | solution.py:614
  33.3 14.9 %collective-permute-start.3 = (f32[384,128]{1,0:T(8,128)S(1)}, f32[384,128]{1,0:T(8,128)S(1)}, u32[]{:S(2)}, u32[]{:S(2)}) collective-permute-start(f32[384,128]{1,0:T(8,128)S(1)} %get-tuple-element.27), channel_id=1, source_target_pairs={{0,2},{1,3},{2,0},{3,1},{4,6},{5,7},{6,4},{7,5},{8,10},{9,11},{10,... | collective-permute-start | bytes 589832 | tf_op jit(solution)/shard_map/ppermute | solution.py:614
  35.2 13.1 %collective-permute-start.4 = (f32[384,128]{1,0:T(8,128)S(1)}, f32[384,128]{1,0:T(8,128)S(1)}, u32[]{:S(2)}, u32[]{:S(2)}) collective-permute-start(f32[384,128]{1,0:T(8,128)S(1)} %get-tuple-element.28), channel_id=1, source_target_pairs={{0,3},{1,0},{2,1},{3,2},{4,7},{5,4},{6,5},{7,6},{8,11},{9,8},{10,9... | collective-permute-start | bytes 589832 | tf_op jit(solution)/shard_map/ppermute | solution.py:614
  44.0 5.7 %collective-permute-start.9 = (f32[384,128]{1,0:T(8,128)S(1)}, f32[384,128]{1,0:T(8,128)S(1)}, u32[]{:S(2)}, u32[]{:S(2)}) collective-permute-start(f32[384,128]{1,0:T(8,128)S(1)} %get-tuple-element.41), channel_id=1, source_target_pairs={{0,1},{1,2},{2,3},{3,0},{4,5},{5,6},{6,7},{7,4},{8,9},{9,10},{10,1... | collective-permute-start | bytes 589832 | tf_op jit(solution)/shard_map/ppermute | solution.py:614
  45.0 7.8 %collective-permute-start.10 = (f32[384,128]{1,0:T(8,128)S(1)}, f32[384,128]{1,0:T(8,128)S(1)}, u32[]{:S(2)}, u32[]{:S(2)}) collective-permute-start(f32[384,128]{1,0:T(8,128)S(1)} %get-tuple-element.42), channel_id=1, source_target_pairs={{0,2},{1,3},{2,0},{3,1},{4,6},{5,7},{6,4},{7,5},{8,10},{9,11},{10,... | collective-permute-start | bytes 589832 | tf_op jit(solution)/shard_map/ppermute | solution.py:614
  46.9 11.2 %collective-permute-start.11 = (f32[384,128]{1,0:T(8,128)S(1)}, f32[384,128]{1,0:T(8,128)S(1)}, u32[]{:S(2)}, u32[]{:S(2)}) collective-permute-start(f32[384,128]{1,0:T(8,128)S(1)} %get-tuple-element.43), channel_id=1, source_target_pairs={{0,3},{1,0},{2,1},{3,2},{4,7},{5,4},{6,5},{7,6},{8,11},{9,8},{10,9... | collective-permute-start | bytes 589832 | tf_op jit(solution)/shard_map/ppermute | solution.py:614
  48.3 14.6 %collective-permute-start.6 = (f32[392,128]{1,0:T(8,128)S(1)}, f32[392,128]{1,0:T(8,128)S(1)}, u32[]{:S(2)}, u32[]{:S(2)}) collective-permute-start(f32[392,128]{1,0:T(8,128)S(1)} %get-tuple-element.36), channel_id=1, source_target_pairs={{0,1},{1,2},{2,3},{3,0},{4,5},{5,6},{6,7},{7,4},{8,9},{9,10},{10,1... | collective-permute-start | bytes 602120 | tf_op jit(solution)/shard_map/ppermute | solution.py:614
  48.4 14.5 %collective-permute-start.7 = (f32[392,128]{1,0:T(8,128)S(1)}, f32[392,128]{1,0:T(8,128)S(1)}, u32[]{:S(2)}, u32[]{:S(2)}) collective-permute-start(f32[392,128]{1,0:T(8,128)S(1)} %get-tuple-element.37), channel_id=1, source_target_pairs={{0,2},{1,3},{2,0},{3,1},{4,6},{5,7},{6,4},{7,5},{8,10},{9,11},{10,... | collective-permute-start | bytes 602120 | tf_op jit(solution)/shard_map/ppermute | solution.py:614
  49.7 14.6 %collective-permute-start.8 = (f32[392,128]{1,0:T(8,128)S(1)}, f32[392,128]{1,0:T(8,128)S(1)}, u32[]{:S(2)}, u32[]{:S(2)}) collective-permute-start(f32[392,128]{1,0:T(8,128)S(1)} %get-tuple-element.38), channel_id=1, source_target_pairs={{0,3},{1,0},{2,1},{3,2},{4,7},{5,4},{6,5},{7,6},{8,11},{9,8},{10,9... | collective-permute-start | bytes 602120 | tf_op jit(solution)/shard_map/ppermute | solution.py:614
  52.8 10.1 %collective-permute-start.12 = (f32[384,128]{1,0:T(8,128)S(1)}, f32[384,128]{1,0:T(8,128)S(1)}, u32[]{:S(2)}, u32[]{:S(2)}) collective-permute-start(f32[384,128]{1,0:T(8,128)S(1)} %select_select_fusion.1), channel_id=1, source_target_pairs={{0,4},{4,8},{8,12},{12,16},{16,20},{20,24},{24,28},{1,5},{5,9},{9,... | collective-permute-start | bytes 589832 | tf_op jit(solution)/shard_map/ppermute | solution.py:667
  58.1 9.4 %collective-permute-start.13 = (f32[384,128]{1,0:T(8,128)S(1)}, f32[384,128]{1,0:T(8,128)S(1)}, u32[]{:S(2)}, u32[]{:S(2)}) collective-permute-start(f32[384,128]{1,0:T(8,128)S(1)} %select_select_fusion), channel_id=1, source_target_pairs={{4,0},{8,4},{12,8},{16,12},{20,16},{24,20},{28,24},{5,1},{9,5},{13... | collective-permute-start | bytes 589832 | tf_op jit(solution)/shard_map/ppermute | solution.py:668

commit v4 on v3

--- a/solution.py
+++ b/solution.py
@@ -13,7 +13,7 @@
 T = 32
 TH = T * H
 QUAD = 4
-MANY, FEW = 8, 4
+MANY, FEW = 8, 12
 STEP = 8
 AXES = ("row", "col")
 RELAX = 2.0 / 3.0
@@ -176,14 +176,56 @@
         out[3 * G * T : 3 * G * T + 8, :] = jnp.full((8, 128), place.astype(F32))
 
 
-def early_kernel(mine, a_own, t_own, small_up, small_down, *refs, ncol):
+def pack_kernel(a_own, t_own, columns, aggregate, owner, *refs, ncol):
+    meta, pay_up, pay_down, pay_big, column_ints, aggregate_ints, owner_ints, sems = refs
+    ints = [
+        pltpu.make_async_copy(columns, column_ints, sems.at[0]),
+        pltpu.make_async_copy(aggregate, aggregate_ints, sems.at[1]),
+        pltpu.make_async_copy(owner, owner_ints, sems.at[2]),
+    ]
+    small = [
+        pltpu.make_async_copy(
+            t_own.at[pl.ds((R - H) * T, TH)], pay_up.at[pl.ds(0, TH)], sems.at[3]
+        ),
+        pltpu.make_async_copy(t_own.at[pl.ds(0, TH)], pay_down.at[pl.ds(0, TH)], sems.at[4]),
+        pltpu.make_async_copy(
+            t_own.at[pl.ds(0, (R - H) * T)], pay_big.at[pl.ds(K * TH, (R - H) * T)], sems.at[5]
+        ),
+    ]
+    last = [
+        pltpu.make_async_copy(
+            a_own.at[pl.ds(((k + 1) * (R // H) - 1) * TH, TH)],
+            pay_big.at[pl.ds(k * TH, TH)],
+            sems.at[6 + k],
+        )
+        for k in range(K)
+    ]
+    for copy in ints + small + last:
+        copy.start()
+    meta[...] = jnp.zeros((8, 128), F32)
+    for copy in ints:
+        copy.wait()
+    device = lax.axis_index("row") * ncol + lax.axis_index("col")
+    meta[0:1, 0:R] = aggregate_ints[...].astype(F32)
+    meta[1:2, 0:G] = owner_ints[...].astype(F32)
+    meta[1:2, G : G + 1] = jnp.full((1, 1), device.astype(F32))
+    meta[2 : 2 + K, 0:R] = column_ints[...].astype(F32)
+    pay_up[TH : TH + 8, :] = meta[...]
+    pay_down[TH : TH + 8, :] = meta[...]
+    for copy in small + last:
+        copy.wait()
+
+
+def early_kernel(mine, a_own, t_in, small_up, small_down, *refs, ncol):
     ups, refs = refs[:ncol], refs[ncol:]
     part_out, ap_out, lhs_out, w_out, pt_hi_out, pt_lo_out = refs[:6]
     a_rows, tn, tb, lhs, w, pt_hi_u, pt_lo_u, pt_hi, pt_lo, ap, ap_hi, ap_lo = refs[6:18]
-    part_own, part_up = refs[18:20]
-    pf, nat = refs[20 : 20 + STEP], refs[20 + STEP : 20 + 2 * STEP]
-    refs = refs[20 + 2 * STEP :]
+    part_own, part_up, t_own = refs[18:21]
+    pf, nat = refs[21 : 21 + STEP], refs[21 + STEP : 21 + 2 * STEP]
+    refs = refs[21 + 2 * STEP :]
     low_ints, high_ints, slots, counts, starts, ranks, order, batch_source, sems = refs
+    tentative = pltpu.make_async_copy(t_in, t_own, sems.at[9])
+    tentative.start()
     whole = pltpu.make_async_copy(a_own, a_rows, sems.at[2])
     whole.start()
     copies = [
@@ -202,8 +244,9 @@
         load_tentative(small_down, 0, i, tn, tb, R + H + i)
         return carry
 
+    lax.fori_loop(0, H, t_ends, 0, unroll=2)
+    tentative.wait()
     lax.fori_loop(0, R, t_rows, 0, unroll=4)
-    lax.fori_loop(0, H, t_ends, 0, unroll=2)
     for copy in copies:
         copy.wait()
     device = mine[1, G].astype(I32)
@@ -526,7 +569,6 @@
 
 def local(a_blocks, columns, tentative, aggregate, owner, *, nrow, ncol):
     count = nrow * ncol
-    device = lax.axis_index(AXES).astype(I32)
     col = lax.axis_index("col")
     up = [(d, d + 1) for d in range(count - 1)]
     down = [(d + 1, d) for d in range(count - 1)]
@@ -537,31 +579,43 @@
         return inner.swapaxes(-3, -2).reshape(-1, 128)
 
     a_own = lying(a_blocks.transpose(1, 0, 2))
-    a_last = lying(a_blocks[R - H :].transpose(1, 0, 2))
     t_own = lying(tentative)
-    last, first = t_own[(R - H) * T :], t_own[:TH]
-    meta = jnp.concatenate(
-        [
-            jnp.pad(aggregate.reshape(1, R), ((0, 0), (0, 128 - R))),
-            jnp.pad(
-                jnp.concatenate([owner, device.reshape(1)]).reshape(1, G + 1),
-                ((0, 0), (0, 128 - G - 1)),
-            ),
-            jnp.pad(columns.T, ((0, 0), (0, 128 - R))),
+    a_own, t_own = [pltpu.with_memory_space_constraint(x, pltpu.HBM) for x in (a_own, t_own)]
+    vmem = pl.BlockSpec(memory_space=pltpu.VMEM)
+    smem = pl.BlockSpec(memory_space=pltpu.SMEM)
+    hbm = pl.BlockSpec(memory_space=pltpu.HBM)
+    meta, pay_up, pay_down, pay_big = pl.pallas_call(
+        lambda *refs: pack_kernel(*refs, ncol=ncol),
+        out_shape=[
+            jax.ShapeDtypeStruct((8, 128), F32),
+            jax.ShapeDtypeStruct((TH + 8, 128), F32),
+            jax.ShapeDtypeStruct((TH + 8, 128), F32),
+            jax.ShapeDtypeStruct((K * TH + (R - H) * T, 128), F32),
         ],
-        axis=0,
-    ).astype(F32)
-    small_up = lax.ppermute(jnp.concatenate([last, meta], axis=0), AXES, up)
-    small_down = lax.ppermute(jnp.concatenate([first, meta], axis=0), AXES, down)
-    big = jnp.concatenate([a_last, t_own[: (R - H) * T]], axis=0)
-    big = lax.ppermute(big, AXES, up)
+        in_specs=[hbm] * 5,
+        out_specs=[vmem] * 4,
+        scratch_shapes=[
+            pltpu.VMEM((K, R), I32),
+            pltpu.VMEM((1, R), I32),
+            pltpu.VMEM((1, G), I32),
+            pltpu.SemaphoreType.DMA((6 + K,)),
+        ],
+        compiler_params=pltpu.CompilerParams(vmem_limit_bytes=4 * MB),
+    )(
+        a_own,
+        t_own,
+        *[
+            pltpu.with_memory_space_constraint(x, pltpu.HBM)
+            for x in (columns.T, aggregate.reshape(1, R), owner.reshape(1, G))
+        ],
+    )
+    small_up = lax.ppermute(pay_up, AXES, up)
+    small_down = lax.ppermute(pay_down, AXES, down)
+    big = lax.ppermute(pay_big, AXES, up)
 
     span = 3 * G * T
     plain = jax.ShapeDtypeStruct((span, 128), F32)
     marked = jax.ShapeDtypeStruct((span + 8, 128), F32)
-    vmem = pl.BlockSpec(memory_space=pltpu.VMEM)
-    smem = pl.BlockSpec(memory_space=pltpu.SMEM)
-    hbm = pl.BlockSpec(memory_space=pltpu.HBM)
     state_shapes = [
         pltpu.HBM((6, 256, 128), F32),
         pltpu.HBM((H, 3, 64, 256), F32),
@@ -573,7 +627,7 @@
     outs = pl.pallas_call(
         lambda *refs: early_kernel(*refs, ncol=ncol),
         out_shape=[plain] * ncol + state_shapes,
-        in_specs=[smem, hbm] + [vmem] * 3,
+        in_specs=[smem, hbm, hbm] + [vmem] * 2,
         out_specs=[vmem] * ncol + [hbm] * len(state_shapes),
         scratch_shapes=[
             pltpu.VMEM((K * R * T, 128), F32),
@@ -590,6 +644,7 @@
             pltpu.VMEM(((R - H) * 64, 768), BF16),
             pltpu.VMEM((6, 256, 128), F32),
             pltpu.VMEM((6, 256, 128), F32),
+            pltpu.VMEM((R * T, 128), F32),
             *[pltpu.VMEM((R // STEP, 4, 64, 128), F32)] * STEP,
             *[pltpu.VMEM((4, 64, 128), F32)] * STEP,
             pltpu.SMEM((8, 128), F32),
@@ -600,9 +655,9 @@
             pltpu.SMEM((R * 8,), I32),
             pltpu.SMEM((MOST_EARLY * QUAD + R * K,), I32),
             pltpu.SMEM((MOST_EARLY + R * K // QUAD,), I32),
-            pltpu.SemaphoreType.DMA((9,)),
+            pltpu.SemaphoreType.DMA((10,)),
         ],
-        compiler_params=pltpu.CompilerParams(vmem_limit_bytes=44 * MB),
+        compiler_params=pltpu.CompilerParams(vmem_limit_bytes=45 * MB),
         cost_estimate=pl.CostEstimate(flops=22 * 10**9, bytes_accessed=12 * MB, transcendentals=0),
     )(meta, a_own, t_own, small_up, small_down)
     ups, state = outs[:ncol], [pltpu.with_memory_space_constraint(x, pltpu.HBM) for x in outs[ncol:]]
@@ -658,7 +713,7 @@
             pltpu.SemaphoreType.DMA((9,)),
         ],
         compiler_params=pltpu.CompilerParams(vmem_limit_bytes=26 * MB),
-    )(meta, small_up, first, big, *state)
+    )(meta, small_up, pay_down, big, *state)
     owns, downs = outs[:ncol], outs[ncol:]
     downs = rotated(downs)
     to_next = chosen(ups, lax.rem(col + 1, ncol))

time: 70.2 us -> 69.1 us (0.984)
  other arithmetic: 2.63 us -> 0.08 us
  Pallas kernels: 29.7 us -> 32.1 us
  local copies, waits for them, and re-layouts: 1.09 us -> 0 us
    pallas_call x0 -> x1, Pallas kernels: none -> 1.5 us  [local(): pl.pallas_call(lambda *refs: pack_kernel(*refs, ncol=ncol), out_shape=[ja...]
    pallas_call x1, Pallas kernels: 18.7 us -> 19.9 us  [local(): pl.pallas_call(lambda *refs: early_kernel(*refs, ncol=ncol), out_shape=[p...]
    concatenate x2 -> x0, other arithmetic: 1.11 us -> none  [the longest x1 1.09 us: local(): big = jnp.concatenate([a_last, t_own[:(R - H) * T]], axis=0)]
    ppermute x9, starting transfers between devices: 8.75 us -> 9.84 us  [rotated(): moved.append(lax.ppermute(blocks[s], 'col', route))]
    slice x4 -> x0, local copies, waits for them, and re-layouts: 1.08 us -> none  [the longest x1 1.04 us: local(): last, first = (t_own[(R - H) * T:], t_own[:TH])]
    ppermute x9, waiting for transfers between devices: 5.04 us -> 6.08 us  [rotated(): moved.append(lax.ppermute(blocks[s], 'col', route))]
    ppermute x1, starting transfers between devices: 5.23 us -> 4.39 us  [local(): lax.ppermute(to_next, 'row', [(r, r + 1) for r in range(nrow - 1)])]
    reshape x1 -> x0, other arithmetic: 0.73 us -> none  [local(): jnp.concatenate([owner, device.reshape(1)]).reshape(1, G + 1)]
  transfers between devices with their start and end apart: 14 -> 14, of which waited for: 5 -> 5; matrix products, arithmetic and copies ran while one was open for 2% -> 0% of each run, Pallas kernels for 39% -> 41%
where the time goes in v4:
time: 69.1 us; the launch traced here: 68.8 us
  Pallas kernels  32.1 us (46%)
  starting transfers between devices  24.4 us (35%)
  waiting for transfers between devices  12.1 us (18%)
    pallas_call x1, Pallas kernels, local(): pl.pallas_call(lambda *refs: early_kernel(*refs, ncol=ncol), out_shape=[p...  19.9 us
    ppermute x9, starting transfers between devices, rotated(): moved.append(lax.ppermute(blocks[s], 'col', route))  9.84 us
    pallas_call x1, Pallas kernels, local(): pl.pallas_call(lambda *refs: late_kernel(*refs, ncol=ncol), out_shape=[ma...  8.54 us
    ppermute x9, waiting for transfers between devices, rotated(): moved.append(lax.ppermute(blocks[s], 'col', route))  6.08 us
    ppermute x1, starting transfers between devices, local(): big = lax.ppermute(pay_big, AXES, up)  5.23 us
    ppermute x1, starting transfers between devices, local(): lax.ppermute(to_next, 'row', [(r, r + 1) for r in range(nrow - 1)])  4.39 us
    ppermute x1, waiting for transfers between devices, local(): lax.ppermute(to_next, 'row', [(r, r + 1) for r in range(nrow - 1)])  3.05 us
    ppermute x1, waiting for transfers between devices, local(): lax.ppermute(to_last, 'row', [(r + 1, r) for r in range(nrow - 1)])  2.95 us
  transfers between devices with their start and end apart: 14, of which 5 were waited for; matrix products, arithmetic and copies ran while one was open for 0% of the time, Pallas kernels for 41%

profile of v4, /device:TPU:0, one launch (start us, length us, event | category | flops | bytes accessed | tf_op | source)
XLA Modules:
  0.0 68.8 jit_solution(5443693956348018565)
XLA Ops:
  0.0 1.5 %shard_map.55 = (f32[8,128]{1,0:T(8,128)S(1)}, f32[264,128]{1,0:T(8,128)S(1)}, f32[264,128]{1,0:T(8,128)S(1)}, f32[2304,128]{1,0:T(8,128)S(1)}) custom-call(f32[6144,128]{1,0:T(8,128)} %bitcast.20, f32[1024,128]{1,0:T(8,128)} %bitcast.22, s32[6,32]{1,0:T(8,128)} %bitcast.24, s32[1,32]{1,0:T(1,128)} %bitcast.25, s32[1,4]{1,0:T(1,128)} %bitcast.26), custom_call_target="tpu_custom_call" | custom-call | tf_op jit(solution)/shard_map/pallas_call | solution.py:587
  1.5 2.4 %collective-permute-start = (f32[264,128]{1,0:T(8,128)S(1)}, f32[264,128]{1,0:T(8,128)S(1)}, u32[]{:S(2)}, u32[]{:S(2)}) collective-permute-start(f32[264,128]{1,0:T(8,128)S(1)} %get-tuple-element.30), channel_id=1, source_target_pairs={{0,1},{1,2},{2,3},{3,4},{4,5},{5,6},{6,7},{7,8},{8,9},{9,10},{10,1... | collective-permute-start | bytes 405512 | tf_op jit(solution)/shard_map/ppermute | solution.py:612
  3.9 1.3 %collective-permute-start.1 = (f32[264,128]{1,0:T(8,128)S(1)}, f32[264,128]{1,0:T(8,128)S(1)}, u32[]{:S(2)}, u32[]{:S(2)}) collective-permute-start(f32[264,128]{1,0:T(8,128)S(1)} %get-tuple-element.31.refs_2_), channel_id=1, source_target_pairs={{1,0},{2,1},{3,2},{4,3},{5,4},{6,5},{7,6},{8,7},{9,8},{10,9},{11,1... | collective-permute-start | bytes 405512 | tf_op jit(solution)/shard_map/ppermute | solution.py:613
  5.2 5.2 %collective-permute-start.5 = (f32[2304,128]{1,0:T(8,128)S(1)}, f32[2304,128]{1,0:T(8,128)S(1)}, u32[]{:S(2)}, u32[]{:S(2)}) collective-permute-start(f32[2304,128]{1,0:T(8,128)S(1)} %get-tuple-element.36), channel_id=1, source_target_pairs={{0,1},{1,2},{2,3},{3,4},{4,5},{5,6},{6,7},{7,8},{8,9},{9,10},{10,1... | collective-permute-start | bytes 3538952 | tf_op jit(solution)/shard_map/ppermute | solution.py:614
  10.4 0.0 collective-permute-done.1.refs_4_
  10.4 19.9 %shard_map.56 = (f32[384,128]{1,0:T(8,128)S(1)}, f32[384,128]{1,0:T(8,128)}, f32[384,128]{1,0:T(8,128)}, f32[384,128]{1,0:T(8,128)}, f32[6,256,128]{2,1,0:T(8,12...) custom-call(f32[8,128]{1,0:T(8,128)S(1)} %get-tuple-element.29.refs_, ...), custom_call_target="tpu_custom_call" | custom-call | flops 22000001024 | bytes 12582912 | tf_op jit(solution)/shard_map/pallas_call | solution.py:627
  30.3 1.9 %collective-permute-start.2 = (f32[384,128]{1,0:T(8,128)}, f32[384,128]{1,0:T(8,128)S(1)}, u32[]{:S(2)}, u32[]{:S(2)}) collective-permute-start(f32[384,128]{1,0:T(8,128)} %get-tuple-element.33), channel_id=1, source_target_pairs={{0,1},{1,2},{2,3},{3,0},{4,5},{5,6},{6,7},{7,4},{8,9},{9,10},{10,1... | collective-permute-start | bytes 589832 | tf_op jit(solution)/shard_map/ppermute | solution.py:669
  32.2 2.9 %collective-permute-start.3 = (f32[384,128]{1,0:T(8,128)}, f32[384,128]{1,0:T(8,128)S(1)}, u32[]{:S(2)}, u32[]{:S(2)}) collective-permute-start(f32[384,128]{1,0:T(8,128)} %get-tuple-element.34), channel_id=1, source_target_pairs={{0,2},{1,3},{2,0},{3,1},{4,6},{5,7},{6,4},{7,5},{8,10},{9,11},{10,... | collective-permute-start | bytes 589832 | tf_op jit(solution)/shard_map/ppermute | solution.py:669
  35.1 0.0 collective-permute-start.4
  35.1 8.5 %shard_map.57 = (f32[392,128]{1,0:T(8,128)S(1)}, f32[392,128]{1,0:T(8,128)S(1)}, f32[392,128]{1,0:T(8,128)S(1)}, f32[392,128]{1,0:T(8,128)S(1)}, f32[384,128]{1,...) custom-call(f32[8,128]{1,0:T(8,128)S(1)} %get-tuple-element.29.refs_0_, ...), custom_call_target="tpu_custom_call" | custom-call | tf_op jit(solution)/shard_map/pallas_call | solution.py:679
  43.7 1.5 %collective-permute-start.9 = (f32[384,128]{1,0:T(8,128)S(1)}, f32[384,128]{1,0:T(8,128)S(1)}, u32[]{:S(2)}, u32[]{:S(2)}) collective-permute-start(f32[384,128]{1,0:T(8,128)S(1)} %get-tuple-element.49), channel_id=1, source_target_pairs={{0,1},{1,2},{2,3},{3,0},{4,5},{5,6},{6,7},{7,4},{8,9},{9,10},{10,1... | collective-permute-start | bytes 589832 | tf_op jit(solution)/shard_map/ppermute | solution.py:669
  45.2 1.0 %collective-permute-start.10 = (f32[384,128]{1,0:T(8,128)S(1)}, f32[384,128]{1,0:T(8,128)S(1)}, u32[]{:S(2)}, u32[]{:S(2)}) collective-permute-start(f32[384,128]{1,0:T(8,128)S(1)} %get-tuple-element.50), channel_id=1, source_target_pairs={{0,2},{1,3},{2,0},{3,1},{4,6},{5,7},{6,4},{7,5},{8,10},{9,11},{10,... | collective-permute-start | bytes 589832 | tf_op jit(solution)/shard_map/ppermute | solution.py:669
  46.2 1.4 %collective-permute-start.11 = (f32[384,128]{1,0:T(8,128)S(1)}, f32[384,128]{1,0:T(8,128)S(1)}, u32[]{:S(2)}, u32[]{:S(2)}) collective-permute-start(f32[384,128]{1,0:T(8,128)S(1)} %get-tuple-element.51), channel_id=1, source_target_pairs={{0,3},{1,0},{2,1},{3,2},{4,7},{5,4},{6,5},{7,6},{8,11},{9,8},{10,9... | collective-permute-start | bytes 589832 | tf_op jit(solution)/shard_map/ppermute | solution.py:669
  47.6 0.1 collective-permute-start.6
  47.7 0.4 collective-permute-start.7
  48.1 0.7 %collective-permute-done.9.refs_10_ = f32[384,128]{1,0:T(8,128)S(1)} collective-permute-done((f32[384,128]{1,0:T(8,128)S(1)}, f32[384,128]{1,0:T(8,128)S(1)}, u32[]{:S(2)}, u32[]{:S(2)}) %collective-permute-start.9) | collective-permute-done | bytes 196640 | tf_op jit(solution)/shard_map/ppermute | solution.py:669
  48.8 0.7 collective-permute-start.8
  49.5 3.5 %collective-permute-done.10.refs_11_ = f32[384,128]{1,0:T(8,128)S(1)} collective-permute-done((f32[384,128]{1,0:T(8,128)S(1)}, f32[384,128]{1,0:T(8,128)S(1)}, u32[]{:S(2)}, u32[]{:S(2)}) %collective-permute-start.10) | collective-permute-done | bytes 196640 | tf_op jit(solution)/shard_map/ppermute | solution.py:669
  53.0 4.4 %collective-permute-start.12 = (f32[384,128]{1,0:T(8,128)S(1)}, f32[384,128]{1,0:T(8,128)S(1)}, u32[]{:S(2)}, u32[]{:S(2)}) collective-permute-start(f32[384,128]{1,0:T(8,128)S(1)} %select_select_fusion.1), channel_id=1, source_target_pairs={{0,4},{4,8},{8,12},{12,16},{16,20},{20,24},{24,28},{1,5},{5,9},{9,... | collective-permute-start | bytes 589832 | tf_op jit(solution)/shard_map/ppermute | solution.py:722
  57.5 1.3 %collective-permute-start.13 = (f32[384,128]{1,0:T(8,128)S(1)}, f32[384,128]{1,0:T(8,128)S(1)}, u32[]{:S(2)}, u32[]{:S(2)}) collective-permute-start(f32[384,128]{1,0:T(8,128)S(1)} %select_select_fusion), channel_id=1, source_target_pairs={{4,0},{8,4},{12,8},{16,12},{20,16},{24,20},{28,24},{5,1},{9,5},{13... | collective-permute-start | bytes 589832 | tf_op jit(solution)/shard_map/ppermute | solution.py:723
  58.8 3.0 %collective-permute-done.12.refs_13_ = f32[384,128]{1,0:T(8,128)S(1)} collective-permute-done((f32[384,128]{1,0:T(8,128)S(1)}, f32[384,128]{1,0:T(8,128)S(1)}, u32[]{:S(2)}, u32[]{:S(2)}) %collective-permute-start.12) | collective-permute-done | bytes 196640 | tf_op jit(solution)/shard_map/ppermute | solution.py:722
  61.8 1.8 %collective-permute-done.8.refs_8_ = f32[392,128]{1,0:T(8,128)S(1)} collective-permute-done((f32[392,128]{1,0:T(8,128)S(1)}, f32[392,128]{1,0:T(8,128)S(1)}, u32[]{:S(2)}, u32[]{:S(2)}) %collective-permute-start.8) | collective-permute-done | bytes 200736 | tf_op jit(solution)/shard_map/ppermute | solution.py:669
  63.6 2.9 %collective-permute-done.13.refs_14_ = f32[384,128]{1,0:T(8,128)S(1)} collective-permute-done((f32[384,128]{1,0:T(8,128)S(1)}, f32[384,128]{1,0:T(8,128)S(1)}, u32[]{:S(2)}, u32[]{:S(2)}) %collective-permute-start.13) | collective-permute-done | bytes 196640 | tf_op jit(solution)/shard_map/ppermute | solution.py:723
  66.6 2.2 %shard_map.58 = f32[2560,128]{1,0:T(8,128)} custom-call(f32[8,128]{1,0:T(8,128)S(1)} %get-tuple-element.29.refs_0_, f32[384,128]{1,0:T(8,128)S(1)} %get-tuple-element.32.refs_1_, f32[384,128]{1,0:T(8,128)S(1)} %collective-permute-done.2.refs_2_, f32[384,128]{1,0:T(8,128)S(1)} %collective-permute-done.3.refs_3_, ...), custom_call_target="tpu_custom_call" | custom-call | tf_op jit(solution)/shard_map/pallas_call | solution.py:725
  (10 shorter events, 0.1 us)
Async XLA Ops:
  1.5 8.9 %collective-permute-start = (f32[264,128]{1,0:T(8,128)S(1)}, f32[264,128]{1,0:T(8,128)S(1)}, u32[]{:S(2)}, u32[]{:S(2)}) collective-permute-start(f32[264,128]{1,0:T(8,128)S(1)} %get-tuple-element.30), channel_id=1, source_target_pairs={{0,1},{1,2},{2,3},{3,4},{4,5},{5,6},{6,7},{7,8},{8,9},{9,10},{10,1... | collective-permute-start | bytes 405512 | tf_op jit(solution)/shard_map/ppermute | solution.py:612
  3.9 6.6 %collective-permute-start.1 = (f32[264,128]{1,0:T(8,128)S(1)}, f32[264,128]{1,0:T(8,128)S(1)}, u32[]{:S(2)}, u32[]{:S(2)}) collective-permute-start(f32[264,128]{1,0:T(8,128)S(1)} %get-tuple-element.31.refs_2_), channel_id=1, source_target_pairs={{1,0},{2,1},{3,2},{4,3},{5,4},{6,5},{7,6},{8,7},{9,8},{10,9},{11,1... | collective-permute-start | bytes 405512 | tf_op jit(solution)/shard_map/ppermute | solution.py:613
  5.2 29.9 %collective-permute-start.5 = (f32[2304,128]{1,0:T(8,128)S(1)}, f32[2304,128]{1,0:T(8,128)S(1)}, u32[]{:S(2)}, u32[]{:S(2)}) collective-permute-start(f32[2304,128]{1,0:T(8,128)S(1)} %get-tuple-element.36), channel_id=1, source_target_pairs={{0,1},{1,2},{2,3},{3,4},{4,5},{5,6},{6,7},{7,8},{8,9},{9,10},{10,1... | collective-permute-start | bytes 3538952 | tf_op jit(solution)/shard_map/ppermute | solution.py:614
  30.3 15.9 %collective-permute-start.2 = (f32[384,128]{1,0:T(8,128)}, f32[384,128]{1,0:T(8,128)S(1)}, u32[]{:S(2)}, u32[]{:S(2)}) collective-permute-start(f32[384,128]{1,0:T(8,128)} %get-tuple-element.33), channel_id=1, source_target_pairs={{0,1},{1,2},{2,3},{3,0},{4,5},{5,6},{6,7},{7,4},{8,9},{9,10},{10,1... | collective-permute-start | bytes 589832 | tf_op jit(solution)/shard_map/ppermute | solution.py:669
  32.2 15.3 %collective-permute-start.3 = (f32[384,128]{1,0:T(8,128)}, f32[384,128]{1,0:T(8,128)S(1)}, u32[]{:S(2)}, u32[]{:S(2)}) collective-permute-start(f32[384,128]{1,0:T(8,128)} %get-tuple-element.34), channel_id=1, source_target_pairs={{0,2},{1,3},{2,0},{3,1},{4,6},{5,7},{6,4},{7,5},{8,10},{9,11},{10,... | collective-permute-start | bytes 589832 | tf_op jit(solution)/shard_map/ppermute | solution.py:669
  35.1 12.5 %collective-permute-start.4 = (f32[384,128]{1,0:T(8,128)}, f32[384,128]{1,0:T(8,128)S(1)}, u32[]{:S(2)}, u32[]{:S(2)}) collective-permute-start(f32[384,128]{1,0:T(8,128)} %get-tuple-element.35), channel_id=1, source_target_pairs={{0,3},{1,0},{2,1},{3,2},{4,7},{5,4},{6,5},{7,6},{8,11},{9,8},{10,9... | collective-permute-start | bytes 589832 | tf_op jit(solution)/shard_map/ppermute | solution.py:669
  43.7 5.1 %collective-permute-start.9 = (f32[384,128]{1,0:T(8,128)S(1)}, f32[384,128]{1,0:T(8,128)S(1)}, u32[]{:S(2)}, u32[]{:S(2)}) collective-permute-start(f32[384,128]{1,0:T(8,128)S(1)} %get-tuple-element.49), channel_id=1, source_target_pairs={{0,1},{1,2},{2,3},{3,0},{4,5},{5,6},{6,7},{7,4},{8,9},{9,10},{10,1... | collective-permute-start | bytes 589832 | tf_op jit(solution)/shard_map/ppermute | solution.py:669
  45.2 7.8 %collective-permute-start.10 = (f32[384,128]{1,0:T(8,128)S(1)}, f32[384,128]{1,0:T(8,128)S(1)}, u32[]{:S(2)}, u32[]{:S(2)}) collective-permute-start(f32[384,128]{1,0:T(8,128)S(1)} %get-tuple-element.50), channel_id=1, source_target_pairs={{0,2},{1,3},{2,0},{3,1},{4,6},{5,7},{6,4},{7,5},{8,10},{9,11},{10,... | collective-permute-start | bytes 589832 | tf_op jit(solution)/shard_map/ppermute | solution.py:669
  46.2 11.2 %collective-permute-start.11 = (f32[384,128]{1,0:T(8,128)S(1)}, f32[384,128]{1,0:T(8,128)S(1)}, u32[]{:S(2)}, u32[]{:S(2)}) collective-permute-start(f32[384,128]{1,0:T(8,128)S(1)} %get-tuple-element.51), channel_id=1, source_target_pairs={{0,3},{1,0},{2,1},{3,2},{4,7},{5,4},{6,5},{7,6},{8,11},{9,8},{10,9... | collective-permute-start | bytes 589832 | tf_op jit(solution)/shard_map/ppermute | solution.py:669
  47.6 14.2 %collective-permute-start.6 = (f32[392,128]{1,0:T(8,128)S(1)}, f32[392,128]{1,0:T(8,128)S(1)}, u32[]{:S(2)}, u32[]{:S(2)}) collective-permute-start(f32[392,128]{1,0:T(8,128)S(1)} %get-tuple-element.44), channel_id=1, source_target_pairs={{0,1},{1,2},{2,3},{3,0},{4,5},{5,6},{6,7},{7,4},{8,9},{9,10},{10,1... | collective-permute-start | bytes 602120 | tf_op jit(solution)/shard_map/ppermute | solution.py:669
  47.7 14.1 %collective-permute-start.7 = (f32[392,128]{1,0:T(8,128)S(1)}, f32[392,128]{1,0:T(8,128)S(1)}, u32[]{:S(2)}, u32[]{:S(2)}) collective-permute-start(f32[392,128]{1,0:T(8,128)S(1)} %get-tuple-element.45), channel_id=1, source_target_pairs={{0,2},{1,3},{2,0},{3,1},{4,6},{5,7},{6,4},{7,5},{8,10},{9,11},{10,... | collective-permute-start | bytes 602120 | tf_op jit(solution)/shard_map/ppermute | solution.py:669
  48.8 14.8 %collective-permute-start.8 = (f32[392,128]{1,0:T(8,128)S(1)}, f32[392,128]{1,0:T(8,128)S(1)}, u32[]{:S(2)}, u32[]{:S(2)}) collective-permute-start(f32[392,128]{1,0:T(8,128)S(1)} %get-tuple-element.46), channel_id=1, source_target_pairs={{0,3},{1,0},{2,1},{3,2},{4,7},{5,4},{6,5},{7,6},{8,11},{9,8},{10,9... | collective-permute-start | bytes 602120 | tf_op jit(solution)/shard_map/ppermute | solution.py:669
  53.0 8.8 %collective-permute-start.12 = (f32[384,128]{1,0:T(8,128)S(1)}, f32[384,128]{1,0:T(8,128)S(1)}, u32[]{:S(2)}, u32[]{:S(2)}) collective-permute-start(f32[384,128]{1,0:T(8,128)S(1)} %select_select_fusion.1), channel_id=1, source_target_pairs={{0,4},{4,8},{8,12},{12,16},{16,20},{20,24},{24,28},{1,5},{5,9},{9,... | collective-permute-start | bytes 589832 | tf_op jit(solution)/shard_map/ppermute | solution.py:722
  57.5 9.1 %collective-permute-start.13 = (f32[384,128]{1,0:T(8,128)S(1)}, f32[384,128]{1,0:T(8,128)S(1)}, u32[]{:S(2)}, u32[]{:S(2)}) collective-permute-start(f32[384,128]{1,0:T(8,128)S(1)} %select_select_fusion), channel_id=1, source_target_pairs={{4,0},{8,4},{12,8},{16,12},{20,16},{24,20},{28,24},{5,1},{9,5},{13... | collective-permute-start | bytes 589832 | tf_op jit(solution)/shard_map/ppermute | solution.py:723

commit v5 on v4

--- a/solution.py
+++ b/solution.py
@@ -533,37 +533,34 @@
 
 def combine_kernel(mine, *refs, ncol):
     ups, owns, downs = refs[:ncol], refs[ncol : 2 * ncol], refs[2 * ncol : 3 * ncol]
-    cross_up, cross_down, out, total = refs[3 * ncol :]
+    cross_up, cross_down, out = refs[3 * ncol :]
     col = lax.rem(mine[1, G].astype(I32), ncol)
     span = G * T
-    for s in range(ncol):
-        home = lax.rem(col - s + ncol, ncol)
-        total[s, 0:span] = jnp.zeros((span, 128), F32)
-        total[s, 4 * span : 5 * span] = jnp.zeros((span, 128), F32)
-        total[s, span : 4 * span] = owns[s][0 : 3 * span]
-
-        @pl.when(home > 0)
-        def _():
-            total[s, 0 : 3 * span] += ups[(s + 1) % ncol][...]
-
-        @pl.when(home == 0)
-        def _():
-            total[s, 0 : 3 * span] += cross_up[...]
-
-        @pl.when(home < ncol - 1)
-        def _():
-            total[s, 2 * span : 5 * span] += downs[(s - 1) % ncol][...]
-
-        @pl.when(home == ncol - 1)
-        def _():
-            total[s, 2 * span : 5 * span] += cross_down[...]
-
-    for j in range(G):
-        for c in range(5):
+    homes = [jnp.full((span, 128), lax.rem(col - s + ncol, ncol)) for s in range(ncol)]
+    for c in range(5):
+        terms = []
+        for s in range(ncol):
+            pieces = []
+            if c < 3:
+                rows = slice(c * span, (c + 1) * span)
+                pieces.append(
+                    jnp.where(homes[s] > 0, ups[(s + 1) % ncol][rows, :], cross_up[rows, :])
+                )
+            if 1 <= c < 4:
+                pieces.append(owns[s][(c - 1) * span : c * span, :])
+            if c >= 2:
+                rows = slice((c - 2) * span, (c - 1) * span)
+                pieces.append(
+                    jnp.where(
+                        homes[s] < ncol - 1, downs[(s - 1) % ncol][rows, :], cross_down[rows, :]
+                    )
+                )
+            terms.append(sum(pieces[1:], pieces[0]))
+        for j in range(G):
             value = jnp.zeros((span, 128), F32)
             for s in range(ncol):
                 mark = owns[s][3 * span : 3 * span + 1, :] == float(j)
-                value = jnp.where(mark, total[s, c * span : (c + 1) * span], value)
+                value = jnp.where(mark, terms[s], value)
             out[pl.ds(c * span * G + j, span, stride=G), :] = value
 
 
@@ -727,7 +724,6 @@
         out_shape=jax.ShapeDtypeStruct((5 * G * T * G, 128), F32),
         in_specs=[smem] + [vmem] * (3 * ncol + 2),
         out_specs=vmem,
-        scratch_shapes=[pltpu.VMEM((ncol, 5 * G * T, 128), F32)],
         compiler_params=pltpu.CompilerParams(vmem_limit_bytes=16 * MB),
     )(meta, *ups, *owns, *downs, cross_up, cross_down)
     return result.reshape(5 * G, T, G, 128).transpose(2, 0, 1, 3).reshape(G, 5 * G, T * 128)

time: 69.1 us -> 68.9 us (level)
  no operation moved by 1% of the time
where the time goes in v5:
time: 68.9 us; the launch traced here: 68.7 us
  Pallas kernels  31.5 us (46%)
  starting transfers between devices  24.9 us (36%)
  waiting for transfers between devices  12.1 us (18%)
    pallas_call x1, Pallas kernels, local(): pl.pallas_call(lambda *refs: early_kernel(*refs, ncol=ncol), out_shape=[p...  19.4 us
    ppermute x9, starting transfers between devices, rotated(): moved.append(lax.ppermute(blocks[s], 'col', route))  10.3 us
    pallas_call x1, Pallas kernels, local(): pl.pallas_call(lambda *refs: late_kernel(*refs, ncol=ncol), out_shape=[ma...  8.54 us
    ppermute x9, waiting for transfers between devices, rotated(): moved.append(lax.ppermute(blocks[s], 'col', route))  6.09 us
    ppermute x1, starting transfers between devices, local(): big = lax.ppermute(pay_big, AXES, up)  5.23 us
    ppermute x1, starting transfers between devices, local(): lax.ppermute(to_next, 'row', [(r, r + 1) for r in range(nrow - 1)])  4.37 us
    ppermute x1, waiting for transfers between devices, local(): lax.ppermute(to_next, 'row', [(r, r + 1) for r in range(nrow - 1)])  3.06 us
    ppermute x1, waiting for transfers between devices, local(): lax.ppermute(to_last, 'row', [(r + 1, r) for r in range(nrow - 1)])  2.95 us
  transfers between devices with their start and end apart: 14, of which 5 were waited for; matrix products, arithmetic and copies ran while one was open for 0% of the time, Pallas kernels for 41%

profile of v5, /device:TPU:0, one launch (start us, length us, event | category | flops | bytes accessed | tf_op | source)
XLA Modules:
  0.0 68.7 jit_solution(7465266103640137643)
XLA Ops:
  0.0 1.5 %shard_map.55 = (f32[8,128]{1,0:T(8,128)S(1)}, f32[264,128]{1,0:T(8,128)S(1)}, f32[264,128]{1,0:T(8,128)S(1)}, f32[2304,128]{1,0:T(8,128)S(1)}) custom-call(f32[6144,128]{1,0:T(8,128)} %bitcast.20, f32[1024,128]{1,0:T(8,128)} %bitcast.22, s32[6,32]{1,0:T(8,128)} %bitcast.24, s32[1,32]{1,0:T(1,128)} %bitcast.25, s32[1,4]{1,0:T(1,128)} %bitcast.26), custom_call_target="tpu_custom_call" | custom-call | tf_op jit(solution)/shard_map/pallas_call | solution.py:584
  1.5 2.4 %collective-permute-start = (f32[264,128]{1,0:T(8,128)S(1)}, f32[264,128]{1,0:T(8,128)S(1)}, u32[]{:S(2)}, u32[]{:S(2)}) collective-permute-start(f32[264,128]{1,0:T(8,128)S(1)} %get-tuple-element.30), channel_id=1, source_target_pairs={{0,1},{1,2},{2,3},{3,4},{4,5},{5,6},{6,7},{7,8},{8,9},{9,10},{10,1... | collective-permute-start | bytes 405512 | tf_op jit(solution)/shard_map/ppermute | solution.py:609
  3.9 1.3 %collective-permute-start.1 = (f32[264,128]{1,0:T(8,128)S(1)}, f32[264,128]{1,0:T(8,128)S(1)}, u32[]{:S(2)}, u32[]{:S(2)}) collective-permute-start(f32[264,128]{1,0:T(8,128)S(1)} %get-tuple-element.31.refs_2_), channel_id=1, source_target_pairs={{1,0},{2,1},{3,2},{4,3},{5,4},{6,5},{7,6},{8,7},{9,8},{10,9},{11,1... | collective-permute-start | bytes 405512 | tf_op jit(solution)/shard_map/ppermute | solution.py:610
  5.2 5.2 %collective-permute-start.5 = (f32[2304,128]{1,0:T(8,128)S(1)}, f32[2304,128]{1,0:T(8,128)S(1)}, u32[]{:S(2)}, u32[]{:S(2)}) collective-permute-start(f32[2304,128]{1,0:T(8,128)S(1)} %get-tuple-element.36), channel_id=1, source_target_pairs={{0,1},{1,2},{2,3},{3,4},{4,5},{5,6},{6,7},{7,8},{8,9},{9,10},{10,1... | collective-permute-start | bytes 3538952 | tf_op jit(solution)/shard_map/ppermute | solution.py:611
  10.4 0.0 collective-permute-done.refs_3_.refs_1_
  10.4 0.0 collective-permute-done.1.refs_4_
  10.4 19.4 %shard_map.56 = (f32[384,128]{1,0:T(8,128)S(1)}, f32[384,128]{1,0:T(8,128)}, f32[384,128]{1,0:T(8,128)}, f32[384,128]{1,0:T(8,128)}, f32[6,256,128]{2,1,0:T(8,12...) custom-call(f32[8,128]{1,0:T(8,128)S(1)} %get-tuple-element.29.refs_, ...), custom_call_target="tpu_custom_call" | custom-call | flops 22000001024 | bytes 12582912 | tf_op jit(solution)/shard_map/pallas_call | solution.py:624
  29.8 2.4 %collective-permute-start.2 = (f32[384,128]{1,0:T(8,128)}, f32[384,128]{1,0:T(8,128)S(1)}, u32[]{:S(2)}, u32[]{:S(2)}) collective-permute-start(f32[384,128]{1,0:T(8,128)} %get-tuple-element.33), channel_id=1, source_target_pairs={{0,1},{1,2},{2,3},{3,0},{4,5},{5,6},{6,7},{7,4},{8,9},{9,10},{10,1... | collective-permute-start | bytes 589832 | tf_op jit(solution)/shard_map/ppermute | solution.py:666
  32.2 2.9 %collective-permute-start.3 = (f32[384,128]{1,0:T(8,128)}, f32[384,128]{1,0:T(8,128)S(1)}, u32[]{:S(2)}, u32[]{:S(2)}) collective-permute-start(f32[384,128]{1,0:T(8,128)} %get-tuple-element.34), channel_id=1, source_target_pairs={{0,2},{1,3},{2,0},{3,1},{4,6},{5,7},{6,4},{7,5},{8,10},{9,11},{10,... | collective-permute-start | bytes 589832 | tf_op jit(solution)/shard_map/ppermute | solution.py:666
  35.1 8.5 %shard_map.57 = (f32[392,128]{1,0:T(8,128)S(1)}, f32[392,128]{1,0:T(8,128)S(1)}, f32[392,128]{1,0:T(8,128)S(1)}, f32[392,128]{1,0:T(8,128)S(1)}, f32[384,128]{1,...) custom-call(f32[8,128]{1,0:T(8,128)S(1)} %get-tuple-element.29.refs_0_, ...), custom_call_target="tpu_custom_call" | custom-call | tf_op jit(solution)/shard_map/pallas_call | solution.py:676
  43.7 1.5 %collective-permute-start.9 = (f32[384,128]{1,0:T(8,128)S(1)}, f32[384,128]{1,0:T(8,128)S(1)}, u32[]{:S(2)}, u32[]{:S(2)}) collective-permute-start(f32[384,128]{1,0:T(8,128)S(1)} %get-tuple-element.49), channel_id=1, source_target_pairs={{0,1},{1,2},{2,3},{3,0},{4,5},{5,6},{6,7},{7,4},{8,9},{9,10},{10,1... | collective-permute-start | bytes 589832 | tf_op jit(solution)/shard_map/ppermute | solution.py:666
  45.2 1.0 %collective-permute-start.10 = (f32[384,128]{1,0:T(8,128)S(1)}, f32[384,128]{1,0:T(8,128)S(1)}, u32[]{:S(2)}, u32[]{:S(2)}) collective-permute-start(f32[384,128]{1,0:T(8,128)S(1)} %get-tuple-element.50), channel_id=1, source_target_pairs={{0,2},{1,3},{2,0},{3,1},{4,6},{5,7},{6,4},{7,5},{8,10},{9,11},{10,... | collective-permute-start | bytes 589832 | tf_op jit(solution)/shard_map/ppermute | solution.py:666
  46.2 1.4 %collective-permute-start.11 = (f32[384,128]{1,0:T(8,128)S(1)}, f32[384,128]{1,0:T(8,128)S(1)}, u32[]{:S(2)}, u32[]{:S(2)}) collective-permute-start(f32[384,128]{1,0:T(8,128)S(1)} %get-tuple-element.51), channel_id=1, source_target_pairs={{0,3},{1,0},{2,1},{3,2},{4,7},{5,4},{6,5},{7,6},{8,11},{9,8},{10,9... | collective-permute-start | bytes 589832 | tf_op jit(solution)/shard_map/ppermute | solution.py:666
  47.6 0.1 collective-permute-start.6
  47.7 0.4 collective-permute-start.7
  48.1 0.7 %collective-permute-done.9.refs_10_ = f32[384,128]{1,0:T(8,128)S(1)} collective-permute-done((f32[384,128]{1,0:T(8,128)S(1)}, f32[384,128]{1,0:T(8,128)S(1)}, u32[]{:S(2)}, u32[]{:S(2)}) %collective-permute-start.9) | collective-permute-done | bytes 196640 | tf_op jit(solution)/shard_map/ppermute | solution.py:666
  48.8 0.7 collective-permute-start.8
  49.5 3.5 %collective-permute-done.10.refs_11_ = f32[384,128]{1,0:T(8,128)S(1)} collective-permute-done((f32[384,128]{1,0:T(8,128)S(1)}, f32[384,128]{1,0:T(8,128)S(1)}, u32[]{:S(2)}, u32[]{:S(2)}) %collective-permute-start.10) | collective-permute-done | bytes 196640 | tf_op jit(solution)/shard_map/ppermute | solution.py:666
  53.0 4.4 %collective-permute-start.12 = (f32[384,128]{1,0:T(8,128)S(1)}, f32[384,128]{1,0:T(8,128)S(1)}, u32[]{:S(2)}, u32[]{:S(2)}) collective-permute-start(f32[384,128]{1,0:T(8,128)S(1)} %select_select_fusion.1), channel_id=1, source_target_pairs={{0,4},{4,8},{8,12},{12,16},{16,20},{20,24},{24,28},{1,5},{5,9},{9,... | collective-permute-start | bytes 589832 | tf_op jit(solution)/shard_map/ppermute | solution.py:719
  57.5 1.3 %collective-permute-start.13 = (f32[384,128]{1,0:T(8,128)S(1)}, f32[384,128]{1,0:T(8,128)S(1)}, u32[]{:S(2)}, u32[]{:S(2)}) collective-permute-start(f32[384,128]{1,0:T(8,128)S(1)} %select_select_fusion), channel_id=1, source_target_pairs={{4,0},{8,4},{12,8},{16,12},{20,16},{24,20},{28,24},{5,1},{9,5},{13... | collective-permute-start | bytes 589832 | tf_op jit(solution)/shard_map/ppermute | solution.py:720
  58.8 3.1 %collective-permute-done.12.refs_13_ = f32[384,128]{1,0:T(8,128)S(1)} collective-permute-done((f32[384,128]{1,0:T(8,128)S(1)}, f32[384,128]{1,0:T(8,128)S(1)}, u32[]{:S(2)}, u32[]{:S(2)}) %collective-permute-start.12) | collective-permute-done | bytes 196640 | tf_op jit(solution)/shard_map/ppermute | solution.py:719
  61.8 1.8 %collective-permute-done.8.refs_8_ = f32[392,128]{1,0:T(8,128)S(1)} collective-permute-done((f32[392,128]{1,0:T(8,128)S(1)}, f32[392,128]{1,0:T(8,128)S(1)}, u32[]{:S(2)}, u32[]{:S(2)}) %collective-permute-start.8) | collective-permute-done | bytes 200736 | tf_op jit(solution)/shard_map/ppermute | solution.py:666
  63.7 3.0 %collective-permute-done.13.refs_14_ = f32[384,128]{1,0:T(8,128)S(1)} collective-permute-done((f32[384,128]{1,0:T(8,128)S(1)}, f32[384,128]{1,0:T(8,128)S(1)}, u32[]{:S(2)}, u32[]{:S(2)}) %collective-permute-start.13) | collective-permute-done | bytes 196640 | tf_op jit(solution)/shard_map/ppermute | solution.py:720
  66.6 2.1 %shard_map.58 = f32[2560,128]{1,0:T(8,128)} custom-call(f32[8,128]{1,0:T(8,128)S(1)} %get-tuple-element.29.refs_0_, f32[384,128]{1,0:T(8,128)S(1)} %get-tuple-element.32.refs_1_, f32[384,128]{1,0:T(8,128)S(1)} %collective-permute-done.2.refs_2_, f32[384,128]{1,0:T(8,128)S(1)} %collective-permute-done.3.refs_3_, ...), custom_call_target="tpu_custom_call" | custom-call | tf_op jit(solution)/shard_map/pallas_call | solution.py:722
  (10 shorter events, 0.1 us)
Async XLA Ops:
  1.5 8.9 %collective-permute-start = (f32[264,128]{1,0:T(8,128)S(1)}, f32[264,128]{1,0:T(8,128)S(1)}, u32[]{:S(2)}, u32[]{:S(2)}) collective-permute-start(f32[264,128]{1,0:T(8,128)S(1)} %get-tuple-element.30), channel_id=1, source_target_pairs={{0,1},{1,2},{2,3},{3,4},{4,5},{5,6},{6,7},{7,8},{8,9},{9,10},{10,1... | collective-permute-start | bytes 405512 | tf_op jit(solution)/shard_map/ppermute | solution.py:609
  3.9 6.6 %collective-permute-start.1 = (f32[264,128]{1,0:T(8,128)S(1)}, f32[264,128]{1,0:T(8,128)S(1)}, u32[]{:S(2)}, u32[]{:S(2)}) collective-permute-start(f32[264,128]{1,0:T(8,128)S(1)} %get-tuple-element.31.refs_2_), channel_id=1, source_target_pairs={{1,0},{2,1},{3,2},{4,3},{5,4},{6,5},{7,6},{8,7},{9,8},{10,9},{11,1... | collective-permute-start | bytes 405512 | tf_op jit(solution)/shard_map/ppermute | solution.py:610
  5.2 29.9 %collective-permute-start.5 = (f32[2304,128]{1,0:T(8,128)S(1)}, f32[2304,128]{1,0:T(8,128)S(1)}, u32[]{:S(2)}, u32[]{:S(2)}) collective-permute-start(f32[2304,128]{1,0:T(8,128)S(1)} %get-tuple-element.36), channel_id=1, source_target_pairs={{0,1},{1,2},{2,3},{3,4},{4,5},{5,6},{6,7},{7,8},{8,9},{9,10},{10,1... | collective-permute-start | bytes 3538952 | tf_op jit(solution)/shard_map/ppermute | solution.py:611
  29.8 16.4 %collective-permute-start.2 = (f32[384,128]{1,0:T(8,128)}, f32[384,128]{1,0:T(8,128)S(1)}, u32[]{:S(2)}, u32[]{:S(2)}) collective-permute-start(f32[384,128]{1,0:T(8,128)} %get-tuple-element.33), channel_id=1, source_target_pairs={{0,1},{1,2},{2,3},{3,0},{4,5},{5,6},{6,7},{7,4},{8,9},{9,10},{10,1... | collective-permute-start | bytes 589832 | tf_op jit(solution)/shard_map/ppermute | solution.py:666
  32.2 15.3 %collective-permute-start.3 = (f32[384,128]{1,0:T(8,128)}, f32[384,128]{1,0:T(8,128)S(1)}, u32[]{:S(2)}, u32[]{:S(2)}) collective-permute-start(f32[384,128]{1,0:T(8,128)} %get-tuple-element.34), channel_id=1, source_target_pairs={{0,2},{1,3},{2,0},{3,1},{4,6},{5,7},{6,4},{7,5},{8,10},{9,11},{10,... | collective-permute-start | bytes 589832 | tf_op jit(solution)/shard_map/ppermute | solution.py:666
  35.1 12.5 %collective-permute-start.4 = (f32[384,128]{1,0:T(8,128)}, f32[384,128]{1,0:T(8,128)S(1)}, u32[]{:S(2)}, u32[]{:S(2)}) collective-permute-start(f32[384,128]{1,0:T(8,128)} %get-tuple-element.35), channel_id=1, source_target_pairs={{0,3},{1,0},{2,1},{3,2},{4,7},{5,4},{6,5},{7,6},{8,11},{9,8},{10,9... | collective-permute-start | bytes 589832 | tf_op jit(solution)/shard_map/ppermute | solution.py:666
  43.7 5.1 %collective-permute-start.9 = (f32[384,128]{1,0:T(8,128)S(1)}, f32[384,128]{1,0:T(8,128)S(1)}, u32[]{:S(2)}, u32[]{:S(2)}) collective-permute-start(f32[384,128]{1,0:T(8,128)S(1)} %get-tuple-element.49), channel_id=1, source_target_pairs={{0,1},{1,2},{2,3},{3,0},{4,5},{5,6},{6,7},{7,4},{8,9},{9,10},{10,1... | collective-permute-start | bytes 589832 | tf_op jit(solution)/shard_map/ppermute | solution.py:666
  45.2 7.8 %collective-permute-start.10 = (f32[384,128]{1,0:T(8,128)S(1)}, f32[384,128]{1,0:T(8,128)S(1)}, u32[]{:S(2)}, u32[]{:S(2)}) collective-permute-start(f32[384,128]{1,0:T(8,128)S(1)} %get-tuple-element.50), channel_id=1, source_target_pairs={{0,2},{1,3},{2,0},{3,1},{4,6},{5,7},{6,4},{7,5},{8,10},{9,11},{10,... | collective-permute-start | bytes 589832 | tf_op jit(solution)/shard_map/ppermute | solution.py:666
  46.2 11.2 %collective-permute-start.11 = (f32[384,128]{1,0:T(8,128)S(1)}, f32[384,128]{1,0:T(8,128)S(1)}, u32[]{:S(2)}, u32[]{:S(2)}) collective-permute-start(f32[384,128]{1,0:T(8,128)S(1)} %get-tuple-element.51), channel_id=1, source_target_pairs={{0,3},{1,0},{2,1},{3,2},{4,7},{5,4},{6,5},{7,6},{8,11},{9,8},{10,9... | collective-permute-start | bytes 589832 | tf_op jit(solution)/shard_map/ppermute | solution.py:666
  47.6 14.2 %collective-permute-start.6 = (f32[392,128]{1,0:T(8,128)S(1)}, f32[392,128]{1,0:T(8,128)S(1)}, u32[]{:S(2)}, u32[]{:S(2)}) collective-permute-start(f32[392,128]{1,0:T(8,128)S(1)} %get-tuple-element.44), channel_id=1, source_target_pairs={{0,1},{1,2},{2,3},{3,0},{4,5},{5,6},{6,7},{7,4},{8,9},{9,10},{10,1... | collective-permute-start | bytes 602120 | tf_op jit(solution)/shard_map/ppermute | solution.py:666
  47.7 14.1 %collective-permute-start.7 = (f32[392,128]{1,0:T(8,128)S(1)}, f32[392,128]{1,0:T(8,128)S(1)}, u32[]{:S(2)}, u32[]{:S(2)}) collective-permute-start(f32[392,128]{1,0:T(8,128)S(1)} %get-tuple-element.45), channel_id=1, source_target_pairs={{0,2},{1,3},{2,0},{3,1},{4,6},{5,7},{6,4},{7,5},{8,10},{9,11},{10,... | collective-permute-start | bytes 602120 | tf_op jit(solution)/shard_map/ppermute | solution.py:666
  48.8 14.8 %collective-permute-start.8 = (f32[392,128]{1,0:T(8,128)S(1)}, f32[392,128]{1,0:T(8,128)S(1)}, u32[]{:S(2)}, u32[]{:S(2)}) collective-permute-start(f32[392,128]{1,0:T(8,128)S(1)} %get-tuple-element.46), channel_id=1, source_target_pairs={{0,3},{1,0},{2,1},{3,2},{4,7},{5,4},{6,5},{7,6},{8,11},{9,8},{10,9... | collective-permute-start | bytes 602120 | tf_op jit(solution)/shard_map/ppermute | solution.py:666
  53.0 8.8 %collective-permute-start.12 = (f32[384,128]{1,0:T(8,128)S(1)}, f32[384,128]{1,0:T(8,128)S(1)}, u32[]{:S(2)}, u32[]{:S(2)}) collective-permute-start(f32[384,128]{1,0:T(8,128)S(1)} %select_select_fusion.1), channel_id=1, source_target_pairs={{0,4},{4,8},{8,12},{12,16},{16,20},{20,24},{24,28},{1,5},{5,9},{9,... | collective-permute-start | bytes 589832 | tf_op jit(solution)/shard_map/ppermute | solution.py:719
  57.5 9.1 %collective-permute-start.13 = (f32[384,128]{1,0:T(8,128)S(1)}, f32[384,128]{1,0:T(8,128)S(1)}, u32[]{:S(2)}, u32[]{:S(2)}) collective-permute-start(f32[384,128]{1,0:T(8,128)S(1)} %select_select_fusion), channel_id=1, source_target_pairs={{4,0},{8,4},{12,8},{16,12},{20,16},{24,20},{28,24},{5,1},{9,5},{13... | collective-permute-start | bytes 589832 | tf_op jit(solution)/shard_map/ppermute | solution.py:720
